TPU v7x, 32 devices: a whole 2x2x4 slice. The times are simulated.
32 devices in a mesh: dp: 8 (over y, x, core), tensor: 4 (over z).
Axes of the slice: x: 2, y: 2, z: 4, core: 2. Of those that a mesh axis runs over, the one named last changes fastest.
Arguments:
- hidden_in: bfloat16 [8192, 1536], P(('dp', 'tensor')), may hold values from -6 to 6
- out_grad: bfloat16 [8192, 1536], P(('dp', 'tensor')), may hold values from -6 to 6
- norm_gain: bfloat16 [2, 1536], P(None, 'dp'), may hold values from 0.5 to 1.5
- proj_z: bfloat16 [2, 1536, 3072], P(None, 'dp', 'tensor'), may hold values from -0.15625 to 0.15625
- proj_x: bfloat16 [2, 1536, 3072], P(None, 'dp', 'tensor'), may hold values from -0.15625 to 0.15625
- proj_bc: bfloat16 [2, 1536, 256], P(None, 'dp'), may hold values from -0.15625 to 0.15625
- proj_dt: bfloat16 [2, 1536, 48], P(None, 'dp', 'tensor'), may hold values from -0.15625 to 0.15625
- conv_value: bfloat16 [2, 4, 3072], P(None, None, 'tensor'), may hold values from -3 to 3
- conv_value_bias: bfloat16 [2, 3072], P(None, 'tensor'), may hold values from -3 to 3
- conv_state: bfloat16 [2, 4, 256], P(None, None, 'dp'), may hold values from -3 to 3
- conv_state_bias: bfloat16 [2, 256], P(None, 'dp'), may hold values from -3 to 3
- step_bias: bfloat16 [2, 48], P(None, 'tensor'), may hold values from -7 to -2
- log_decay: bfloat16 [2, 48], P(None, 'tensor'), may hold values from 0 to 2.6875
- skip_gain: bfloat16 [2, 48], P(None, 'tensor'), may hold values from 0.5 to 1.5
- gate_gain: bfloat16 [2, 3072], P(None, 'tensor'), may hold values from 0.5 to 1.5
- proj_out: bfloat16 [2, 3072, 1536], P(None, 'tensor', 'dp'), may hold values from -0.109375 to 0.109375
Outputs:
- hidden_out: float32 [8192, 1536], P(('dp', 'tensor'))
- hidden_grad: float32 [8192, 1536], P(('dp', 'tensor'))
- grad_norm_gain: float32 [2, 1536], P(None, 'dp')
- grad_proj_z: float32 [2, 1536, 3072], P(None, 'dp', 'tensor')
- grad_proj_x: float32 [2, 1536, 3072], P(None, 'dp', 'tensor')
- grad_proj_bc: float32 [2, 1536, 256], P(None, 'dp')
- grad_proj_dt: float32 [2, 1536, 48], P(None, 'dp', 'tensor')
- grad_conv_value: float32 [2, 4, 3072], P(None, None, 'tensor')
- grad_conv_value_bias: float32 [2, 3072], P(None, 'tensor')
- grad_conv_state: float32 [2, 4, 256], P(None, None, 'dp')
- grad_conv_state_bias: float32 [2, 256], P(None, 'dp')
- grad_step_bias: float32 [2, 48], P(None, 'tensor')
- grad_log_decay: float32 [2, 48], P(None, 'tensor')
- grad_skip_gain: float32 [2, 48], P(None, 'tensor')
- grad_gate_gain: float32 [2, 3072], P(None, 'tensor')
- grad_proj_out: float32 [2, 3072, 1536], P(None, 'tensor', 'dp')
All inputs are finite; a program needn't handle non-finite values.
Results may differ from a plain program's by a relative error of at most 0.018.
Values may be sent and summed in bfloat16 or wider, within the bound.
A program may use at most 256 MiB of HBM per device.

v0:
```python
import jax
import jax.numpy as jnp
from jax import lax
from jax.sharding import PartitionSpec as P

GROUP = 256


EPSILON = 1e-05
HIGHEST = lax.Precision.HIGHEST


def conv_silu(series, weight, offset):
    tap_count = weight.shape[0]
    length = series.shape[0]
    padded = jnp.pad(series, ((tap_count - 1, 0), (0, 0)))
    summed = jnp.zeros_like(series) + offset[None, :]
    for tap_index in range(tap_count):
        summed = summed + weight[tap_index][None, :] * padded[tap_index : tap_index + length]
    return jax.nn.silu(summed)


def ssd_scan(inputs, step_sizes, log_rates, b_values, c_values, skip_gain, block_size):
    length, head_count, head_width = inputs.shape
    state_size = b_values.shape[1]
    blocks = length // block_size
    decay_rates = (step_sizes * (-jnp.exp(log_rates))[None, :]).reshape(
        blocks, block_size, head_count
    )
    cumuls = jnp.cumsum(decay_rates, axis=1)
    weighted = (inputs * step_sizes[:, :, None]).reshape(blocks, block_size, head_count, head_width)
    b_blocks = b_values.reshape(blocks, block_size, state_size)
    c_blocks = c_values.reshape(blocks, block_size, state_size)
    scores = jnp.einsum("cqn,csn->cqs", c_blocks, b_blocks, precision=HIGHEST)
    causal = (jnp.arange(block_size)[:, None] >= jnp.arange(block_size)[None, :])[None, :, :, None]
    gap_sums = jnp.where(causal, cumuls[:, :, None, :] - cumuls[:, None, :, :], 0.0)
    decays = jnp.where(causal, jnp.exp(gap_sums), 0.0)
    inside = jnp.einsum("cqs,cqsh,cshp->cqhp", scores, decays, weighted, precision=HIGHEST)
    tail_decay = jnp.exp(cumuls[:, -1:, :] - cumuls)
    end_states = jnp.einsum("csh,cshp,csn->chpn", tail_decay, weighted, b_blocks, precision=HIGHEST)
    block_drops = jnp.exp(cumuls[:, -1, :])

    def carry_step(carried, paired):
        one_drop, fresh_state = paired
        return (carried * one_drop[:, None, None] + fresh_state, carried)

    _, entering = lax.scan(carry_step, jnp.zeros_like(end_states[0]), (block_drops, end_states))
    outside = (
        jnp.einsum("cqn,chpn->cqhp", c_blocks, entering, precision=HIGHEST)
        * jnp.exp(cumuls)[:, :, :, None]
    )
    return (inside + outside).reshape(length, head_count, head_width) + skip_gain[
        None, :, None
    ] * inputs


def state_inputs(projected, conv_weight, conv_offset):
    conved = conv_silu(projected, conv_weight, conv_offset)
    half_width = conved.shape[1] // 2
    return (conved[:, :half_width], conved[:, half_width:])


def mixer(
    gate_in,
    value_in,
    step_in,
    b_values,
    c_values,
    conv_weight,
    conv_offset,
    step_offset,
    log_rates,
    skip_gain,
):
    length = value_in.shape[0]
    head_count = step_in.shape[1]
    conved = conv_silu(value_in, conv_weight, conv_offset)
    step_sizes = jax.nn.softplus(step_in + step_offset[None, :])
    mixed = ssd_scan(
        conved.reshape(length, head_count, -1),
        step_sizes,
        log_rates,
        b_values,
        c_values,
        skip_gain,
        GROUP,
    )
    return mixed.reshape(length, -1) * jax.nn.silu(gate_in)


def pre_norm(residual, gain_pre):
    scale = lax.rsqrt(jnp.mean(residual * residual, axis=1, keepdims=True) + EPSILON)
    return residual * scale * gain_pre[None, :]


def row_slice(matrix, start, count):
    return lax.dynamic_slice_in_dim(matrix, start, count, 0)


def shards(
    hidden_in,
    out_grad,
    norm_gain,
    proj_z,
    proj_x,
    proj_bc,
    proj_dt,
    conv_value,
    conv_value_bias,
    conv_state,
    conv_state_bias,
    step_bias,
    log_decay,
    skip_gain,
    gate_gain,
    proj_out,
):
    tensor_count = lax.axis_size("tensor")
    tensor_index = lax.axis_index("tensor")
    row_count = hidden_in.shape[0]
    layer_count = proj_z.shape[0]
    residual = hidden_in.astype(jnp.float32)
    kept_list = []
    for layer_index in range(layer_count):
        gathered = (
            lax.all_gather(norm_gain[layer_index], "dp", axis=0, tiled=True),
            lax.all_gather(proj_z[layer_index], "dp", axis=0, tiled=True),
            lax.all_gather(proj_x[layer_index], "dp", axis=0, tiled=True),
            lax.all_gather(proj_bc[layer_index], "dp", axis=0, tiled=True),
            lax.all_gather(proj_dt[layer_index], "dp", axis=0, tiled=True),
            lax.all_gather(conv_state[layer_index], "dp", axis=1, tiled=True),
            lax.all_gather(conv_state_bias[layer_index], "dp", axis=0, tiled=True),
            lax.all_gather(proj_out[layer_index], "dp", axis=1, tiled=True),
        )
        gain_pre, full_z, full_x, full_bc, full_dt, full_conv, full_offset, full_out = gathered
        normed = pre_norm(residual, gain_pre.astype(jnp.float32)).astype(jnp.bfloat16)
        seq_rows = lax.all_gather(normed, "tensor", axis=0, tiled=True)
        gate_in = jnp.dot(seq_rows, full_z, preferred_element_type=jnp.float32)
        value_in = jnp.dot(seq_rows, full_x, preferred_element_type=jnp.float32)
        state_in = jnp.dot(seq_rows, full_bc, preferred_element_type=jnp.float32)
        step_in = jnp.dot(seq_rows, full_dt, preferred_element_type=jnp.float32)
        b_values, c_values = state_inputs(
            state_in, full_conv.astype(jnp.float32), full_offset.astype(jnp.float32)
        )
        gated = mixer(
            gate_in,
            value_in,
            step_in,
            b_values,
            c_values,
            conv_value[layer_index].astype(jnp.float32),
            conv_value_bias[layer_index].astype(jnp.float32),
            step_bias[layer_index].astype(jnp.float32),
            log_decay[layer_index].astype(jnp.float32),
            skip_gain[layer_index].astype(jnp.float32),
        )
        inner_total = lax.psum(jnp.sum(gated * gated, axis=1), "tensor")
        inner_count = gated.shape[1] * tensor_count
        inner_scale = lax.rsqrt(inner_total / inner_count + EPSILON)[:, None]
        gain_gate = gate_gain[layer_index].astype(jnp.float32)
        mixed = (gated * inner_scale * gain_gate[None, :]).astype(jnp.bfloat16)
        branch = lax.psum_scatter(
            jnp.dot(
                row_slice(mixed, jnp.int32(0), row_count * lax.axis_size("tensor")),
                full_out,
                preferred_element_type=jnp.float32,
            ),
            "tensor",
            scatter_dimension=0,
            tiled=True,
        )
        kept_weights = None
        kept_list.append(
            (residual, seq_rows, gate_in, value_in, state_in, step_in, inner_scale, kept_weights)
        )
        residual = residual + branch
    gradient = out_grad.astype(jnp.float32)
    scatter_list = [None] * layer_count
    head_list = [None] * layer_count
    for layer_index in reversed(range(layer_count)):
        residual_in, seq_rows, gate_in, value_in, state_in, step_in, inner_scale, kept_weights = (
            kept_list[layer_index]
        )
        weights_now = (
            lax.all_gather(norm_gain[layer_index], "dp", axis=0, tiled=True),
            lax.all_gather(proj_z[layer_index], "dp", axis=0, tiled=True),
            lax.all_gather(proj_x[layer_index], "dp", axis=0, tiled=True),
            lax.all_gather(proj_bc[layer_index], "dp", axis=0, tiled=True),
            lax.all_gather(proj_dt[layer_index], "dp", axis=0, tiled=True),
            lax.all_gather(conv_state[layer_index], "dp", axis=1, tiled=True),
            lax.all_gather(conv_state_bias[layer_index], "dp", axis=0, tiled=True),
            lax.all_gather(proj_out[layer_index], "dp", axis=1, tiled=True),
        )
        gain_pre, full_z, full_x, full_bc, full_dt, full_conv, full_offset, full_out = weights_now
        grad_rows = lax.all_gather(gradient.astype(jnp.bfloat16), "tensor", axis=0, tiled=True)
        (b_values, c_values), state_back = jax.vjp(
            state_inputs, state_in, full_conv.astype(jnp.float32), full_offset.astype(jnp.float32)
        )
        gated, mixer_back = jax.vjp(
            mixer,
            gate_in,
            value_in,
            step_in,
            b_values,
            c_values,
            conv_value[layer_index].astype(jnp.float32),
            conv_value_bias[layer_index].astype(jnp.float32),
            step_bias[layer_index].astype(jnp.float32),
            log_decay[layer_index].astype(jnp.float32),
            skip_gain[layer_index].astype(jnp.float32),
        )
        gain_gate = gate_gain[layer_index].astype(jnp.float32)
        normal = gated * inner_scale
        mixed = (normal * gain_gate[None, :]).astype(jnp.bfloat16)
        grad_out = jnp.einsum("ti,td->id", mixed, grad_rows, preferred_element_type=jnp.float32)
        grad_mixed = jnp.einsum(
            "td,id->ti", grad_rows, full_out, preferred_element_type=jnp.float32
        )
        grad_gate_gain = jnp.sum(normal * grad_mixed, axis=0)
        grad_normal = grad_mixed * gain_gate[None, :]
        cross_total = lax.psum(jnp.sum(grad_normal * gated, axis=1), "tensor")
        inner_count = gated.shape[1] * tensor_count
        grad_gated = (
            inner_scale * grad_normal
            - gated * inner_scale**3 * (cross_total / inner_count)[:, None]
        )
        (
            grad_gate_in,
            grad_value_in,
            grad_step_in,
            grad_bvals,
            grad_cvals,
            grad_conv_weight,
            grad_conv_offset,
            grad_step_offset,
            grad_log_rates,
            grad_skip,
        ) = mixer_back(grad_gated)
        grad_bvals, grad_cvals = lax.psum((grad_bvals, grad_cvals), "tensor")
        grad_state_in, grad_shared_conv, grad_shared_offset = state_back((grad_bvals, grad_cvals))
        low_gate = grad_gate_in.astype(jnp.bfloat16)
        low_value = grad_value_in.astype(jnp.bfloat16)
        low_step = grad_step_in.astype(jnp.bfloat16)
        low_state = grad_state_in.astype(jnp.bfloat16)
        first_row = tensor_index * row_count
        own_rows = row_slice(seq_rows, first_row, row_count)
        own_state = row_slice(low_state, first_row, row_count)
        grad_weight_z = jnp.einsum(
            "td,tj->dj", seq_rows, low_gate, preferred_element_type=jnp.float32
        )
        grad_weight_x = jnp.einsum(
            "td,tj->dj", seq_rows, low_value, preferred_element_type=jnp.float32
        )
        grad_weight_dt = jnp.einsum(
            "td,tj->dj", seq_rows, low_step, preferred_element_type=jnp.float32
        )
        grad_weight_bc = jnp.einsum(
            "td,tj->dj", own_rows, own_state, preferred_element_type=jnp.float32
        )
        back_start = jnp.int32(0)
        back_summed = jnp.einsum(
            "tj,dj->td",
            row_slice(low_gate, back_start, row_count * lax.axis_size("tensor")),
            full_z,
            preferred_element_type=jnp.float32,
        )
        back_summed = back_summed + jnp.einsum(
            "tj,dj->td",
            row_slice(low_value, back_start, row_count * lax.axis_size("tensor")),
            full_x,
            preferred_element_type=jnp.float32,
        )
        grad_normed = lax.psum_scatter(
            back_summed
            + jnp.einsum(
                "tj,dj->td",
                row_slice(low_step, back_start, row_count * lax.axis_size("tensor")),
                full_dt,
                preferred_element_type=jnp.float32,
            ),
            "tensor",
            scatter_dimension=0,
            tiled=True,
        )
        grad_normed = grad_normed + jnp.einsum(
            "tj,dj->td", own_state, full_bc, preferred_element_type=jnp.float32
        )
        _, norm_back = jax.vjp(pre_norm, residual_in, gain_pre.astype(jnp.float32))
        grad_residual, grad_gain_pre = norm_back(grad_normed)
        gradient = gradient + grad_residual
        scatter_list[layer_index] = (
            lax.psum_scatter(
                grad_gain_pre.astype(jnp.bfloat16), "dp", scatter_dimension=0, tiled=True
            ).astype(jnp.float32),
            lax.psum_scatter(
                grad_weight_z.astype(jnp.bfloat16), "dp", scatter_dimension=0, tiled=True
            ).astype(jnp.float32),
            lax.psum_scatter(
                grad_weight_x.astype(jnp.bfloat16), "dp", scatter_dimension=0, tiled=True
            ).astype(jnp.float32),
            lax.psum_scatter(
                grad_weight_bc.astype(jnp.bfloat16), "dp", scatter_dimension=0, tiled=True
            ).astype(jnp.float32),
            lax.psum_scatter(
                grad_weight_dt.astype(jnp.bfloat16), "dp", scatter_dimension=0, tiled=True
            ).astype(jnp.float32),
            lax.psum_scatter(
                grad_shared_conv.astype(jnp.bfloat16), "dp", scatter_dimension=1, tiled=True
            ).astype(jnp.float32),
            lax.psum_scatter(
                grad_shared_offset.astype(jnp.bfloat16), "dp", scatter_dimension=0, tiled=True
            ).astype(jnp.float32),
            lax.psum_scatter(
                grad_out.astype(jnp.bfloat16), "dp", scatter_dimension=1, tiled=True
            ).astype(jnp.float32),
        )
        head_list[layer_index] = (
            grad_conv_weight,
            grad_conv_offset,
            grad_step_offset,
            grad_log_rates,
            grad_skip,
            grad_gate_gain,
        )
    stacked = [
        jnp.stack([scatter_list[layer_index][member] for layer_index in range(layer_count)])
        for member in range(8)
    ]
    shared = (
        lax.psum(stacked[0].astype(jnp.bfloat16), "tensor").astype(jnp.float32),
        lax.psum(stacked[3].astype(jnp.bfloat16), "tensor").astype(jnp.float32),
    )
    per_head = [
        jnp.stack([head_list[layer_index][member] for layer_index in range(layer_count)])
        for member in range(6)
    ]
    head_sums = lax.psum(
        (per_head[0], per_head[1], per_head[2], per_head[3], per_head[4], per_head[5]), "dp"
    )
    return (
        residual,
        gradient,
        shared[0],
        stacked[1],
        stacked[2],
        shared[1],
        stacked[4],
        head_sums[0],
        head_sums[1],
        stacked[5],
        stacked[6],
        head_sums[2],
        head_sums[3],
        head_sums[4],
        head_sums[5],
        stacked[7],
    )


def solution(mesh):
    placed = (
        P(("dp", "tensor"), None),
        P(("dp", "tensor"), None),
        P(None, "dp"),
        P(None, "dp", "tensor"),
        P(None, "dp", "tensor"),
        P(None, "dp", None),
        P(None, "dp", "tensor"),
        P(None, None, "tensor"),
        P(None, "tensor"),
        P(None, None, "dp"),
        P(None, "dp"),
        P(None, "tensor"),
        P(None, "tensor"),
        P(None, "tensor"),
        P(None, "tensor"),
        P(None, "tensor", "dp"),
    )
    return jax.shard_map(
        shards,
        mesh=mesh,
        in_specs=placed,
        out_specs=(
            P(("dp", "tensor"), None),
            P(("dp", "tensor"), None),
            P(None, "dp"),
            P(None, "dp", "tensor"),
            P(None, "dp", "tensor"),
            P(None, "dp", None),
            P(None, "dp", "tensor"),
            P(None, None, "tensor"),
            P(None, "tensor"),
            P(None, None, "dp"),
            P(None, "dp"),
            P(None, "tensor"),
            P(None, "tensor"),
            P(None, "tensor"),
            P(None, "tensor"),
            P(None, "tensor", "dp"),
        ),
        check_vma=False,
    )
```

profile of v0, /device:TPU:0, one launch (start us, length us, event | category | flops | bytes accessed | tf_op | source)
XLA Modules:
  0.0 1870.4 jit_solution(15592791892708864510)
XLA Ops:
  12.4 16.2 all-reduce.54
  78.0 17.9 all-gather.27.cloned.1.call-done
  152.5 17.1 fusion.34
  220.2 107.5 %reduce-scatter.25.cloned.1.call-done = f32[256,1536]{1,0:T(8,128)} async-done(((f32[1024,1536]{1,0:T(8,128)}), f32[256,1536]{1,0:T(8,128)}) %reduce-scatter.25.cloned.1.call-update) | async-done | bytes 1572880 | tf_op jit(solution)/shard_map/reduce_scatter | solution.py:162
  371.8 24.0 %all-gather.29.cloned.1.call-done = bf16[1024,1536]{1,0:T(8,128)(2,1)} async-done(((bf16[256,1536]{1,0:T(8,128)(2,1)}), bf16[1024,1536]{1,0:T(8,128)(2,1)}) %all-gather.29.cloned.1.call-update) | async-done | bytes 3145744 | tf_op jit(solution)/shard_map/all_gather | solution.py:137
  455.9 22.0 %while.96 = (s32[]{:T(128)}, f32[12,64,128]{2,1,0:T(8,128)}, f32[4,12,64,128]{3,2,1,0:T(8,128)}, f32[4,12,1,1]{1,3,2,0:T(1,128)}, f32[4,12]{1,0:T(4,128)}, /*index=5*/f32[4,12,64,128]{3,2,1,0:T(8,128)}, s32[]{:T(128)}, s32[]{:T(128)}) while((s32[]{:T(128)}, f32[12,64,128]{2,1,0:T(8,128)}, f32[4,12,64,128]{3,2,1,0:T(8,128)}, ...), condition=%wide.region_19.21_spmd.clone, body=%wide.region_18.20_spmd.clone.sunk | while | flops 393219 | bytes 1968376 | solution.py:47
  484.3 15.5 bitcast_add_fusion.9
  517.5 16.6 fusion.28
  637.0 16.2 while.97
  665.2 20.0 %fusion.41 = (f32[4,256,12]{1,2,0:T(8,128)}, f32[4,256,12]{1,2,0:T(8,128)}, f32[4,256,256]{2,1,0:T(8,128)S(1)}) fusion(f32[4,256,12]{1,2,0:T(8,128)S(1)} %bitcast.555, f32[4,256,256]{2,1,0:T(8,128)S(1)} %copy-done.74, pred[256,256]{1,0:T(8,128)(4,1)S(1)} %copy-done.116, f32[4,256,12,64]{1,0,3,2:T(4,128)S(1)} %reshape.525, f32[4,256,12]{1,2,0:T(8,128)S(1)} %copy-done.68, ...), kind=kOutput, calls=%fused_computation.65 | convolution fusion | flops 2451021824 | bytes 8650752 | tf_op jit(solution)/shard_map/transpose(jvp(cqs,cqsh,cshp->cqhp))/dot_general | solution.py:38
  700.9 12.5 bitcast_add_fusion.8
  767.7 103.8 %reduce-scatter.29.cloned.1.call-done = f32[256,1536]{1,0:T(8,128)} async-done(((f32[1024,1536]{1,0:T(8,128)}), f32[256,1536]{1,0:T(8,128)}) %reduce-scatter.29.cloned.1.call-update) | async-done | bytes 1572880 | tf_op jit(solution)/shard_map/reduce_scatter | solution.py:273
  900.1 15.8 bitcast_add_fusion.7
  923.9 17.1 all-gather.33.cloned.1.call-done
  941.1 12.5 multiply_reduce_fusion.3
  993.3 20.0 %fusion.43 = (f32[4,256,12]{1,2,0:T(8,128)}, f32[4,256,12]{1,2,0:T(8,128)}, f32[4,256,256]{2,1,0:T(8,128)}) fusion(f32[4,256,12]{1,2,0:T(8,128)S(1)} %bitcast.551, f32[4,256,256]{2,1,0:T(8,128)S(1)} %copy-done.71, pred[256,256]{1,0:T(8,128)(4,1)S(1)} %copy-done.118, f32[4,256,12,64]{1,0,3,2:T(4,128)S(1)} %copy-done.1, f32[4,256,12]{1,2,0:T(8,128)S(1)} %copy-done.64, ...), kind=kOutput, calls=%fused_computation.67 | convolution fusion | flops 2451021824 | bytes 8650752 | tf_op jit(solution)/shard_map/transpose(jvp(cqs,cqsh,cshp->cqhp))/dot_general | solution.py:38
  1015.3 16.2 while.99
  1045.0 48.2 %all-reduce.63.cloned.1.call-done = f32[1024,256]{1,0:T(8,128)} async-done(((f32[1024,256]{1,0:T(8,128)}), f32[1024,256]{1,0:T(8,128)}) %all-reduce.63.cloned.1.call-update) | async-done | bytes 1048592 | tf_op jit(solution)/shard_map/psum | solution.py:239
  1127.8 13.0 bitcast_add_fusion.6
  1148.4 21.5 %reduce-scatter.41.cloned.1.call-done = bf16[192,256]{1,0:T(8,128)(2,1)} async-done(((bf16[1536,256]{1,0:T(8,128)(2,1)}), bf16[192,256]{1,0:T(8,128)(2,1)}) %reduce-scatter.41.cloned.1.call-update) | async-done | bytes 98320 | tf_op jit(solution)/shard_map/reduce_scatter | solution.py:301
  1261.7 24.0 %all-reduce.52 = (f32[2,4,768]{2,1,0:T(4,128)}, f32[2,768]{1,0:T(2,128)}, f32[2,12]{1,0:T(2,128)}, f32[2,12]{1,0:T(2,128)}, f32[2,12]{1,0:T(2,128)}, /*index=5*/f32[2,768]{1,0:T(2,128)}) all-reduce(f32[2,4,768]{2,1,0:T(4,128)S(1)} %pad_maximum_fusion.1, ...), channel_id=1, replica_groups=mesh['dp'=8,'tensor'=4] {'dp'}, use_global_device_ids=true, to_apply=%region_78.80 | all-reduce | flops 9288 | bytes 74304 | tf_op jit(solution)/shard_map/psum | solution.py:337
  1287.2 31.0 %reduce-scatter.53.cloned.1.call-done = bf16[32,4]{1,0:T(8,128)(2,1)} async-done(((bf16[256,4]{1,0:T(8,128)(2,1)}), bf16[32,4]{1,0:T(8,128)(2,1)}) %reduce-scatter.53.cloned.1.call-update) | async-done | bytes 272
  1319.6 36.4 %all-reduce.59.cloned.1.call-done = bf16[2,192,256]{2,1,0:T(8,128)(2,1)} async-done(((bf16[2,192,256]{2,1,0:T(8,128)(2,1)}), bf16[2,192,256]{2,1,0:T(8,128)(2,1)}) %all-reduce.59.cloned.1.call-update) | async-done | bytes 196624 | tf_op jit(solution)/shard_map/psum | solution.py:331
  1357.7 44.2 %reduce-scatter.47.cloned.1.call-done = bf16[768,192]{0,1:T(8,128)(2,1)} async-done(((bf16[768,1536]{0,1:T(8,128)(2,1)}), bf16[768,192]{0,1:T(8,128)(2,1)}) %reduce-scatter.47.cloned.1.call-update) | async-done | bytes 294928 | tf_op jit(solution)/shard_map/reduce_scatter | solution.py:313
  1401.9 45.9 %reduce-scatter.45.cloned.1.call-done = bf16[768,192]{0,1:T(8,128)(2,1)} async-done(((bf16[768,1536]{0,1:T(8,128)(2,1)}), bf16[768,192]{0,1:T(8,128)(2,1)}) %reduce-scatter.45.cloned.1.call-update) | async-done | bytes 294928 | tf_op jit(solution)/shard_map/reduce_scatter | solution.py:313
  1449.9 43.9 %reduce-scatter.39.cloned.1.call-done = bf16[192,768]{1,0:T(8,128)(2,1)} async-done(((bf16[1536,768]{1,0:T(8,128)(2,1)}), bf16[192,768]{1,0:T(8,128)(2,1)}) %reduce-scatter.39.cloned.1.call-update) | async-done | bytes 294928 | tf_op jit(solution)/shard_map/reduce_scatter | solution.py:298
  1493.9 45.8 %reduce-scatter.37.cloned.1.call-done = bf16[192,768]{1,0:T(8,128)(2,1)} async-done(((bf16[1536,768]{1,0:T(8,128)(2,1)}), bf16[192,768]{1,0:T(8,128)(2,1)}) %reduce-scatter.37.cloned.1.call-update) | async-done | bytes 294928 | tf_op jit(solution)/shard_map/reduce_scatter | solution.py:298
  1541.9 43.9 %reduce-scatter.35.cloned.1.call-done = bf16[192,768]{1,0:T(8,128)(2,1)} async-done(((bf16[1536,768]{1,0:T(8,128)(2,1)}), bf16[192,768]{1,0:T(8,128)(2,1)}) %reduce-scatter.35.cloned.1.call-update) | async-done | bytes 294928 | tf_op jit(solution)/shard_map/reduce_scatter | solution.py:295
  1585.8 45.7 %reduce-scatter.33.cloned.1.call-done = bf16[192,768]{1,0:T(8,128)(2,1)} async-done(((bf16[1536,768]{1,0:T(8,128)(2,1)}), bf16[192,768]{1,0:T(8,128)(2,1)}) %reduce-scatter.33.cloned.1.call-update) | async-done | bytes 294928 | tf_op jit(solution)/shard_map/reduce_scatter | solution.py:295
  1633.8 110.8 %reduce-scatter.31.cloned.1.call-done = f32[256,1536]{1,0:T(8,128)} async-done(((f32[1024,1536]{1,0:T(8,128)}), f32[256,1536]{1,0:T(8,128)}) %reduce-scatter.31.cloned.1.call-update) | async-done | bytes 1572880 | tf_op jit(solution)/shard_map/reduce_scatter | solution.py:273
  1748.1 14.7 all-reduce.53
  1775.4 83.3 %reduce-scatter.27.cloned.1.call-done = f32[256,1536]{1,0:T(8,128)} async-done(((f32[1024,1536]{1,0:T(8,128)}), f32[256,1536]{1,0:T(8,128)}) %reduce-scatter.27.cloned.1.call-update) | async-done | bytes 1572880 | tf_op jit(solution)/shard_map/reduce_scatter | solution.py:162
  (933 shorter events, 807.1 us)
Async XLA Ops:
  7.2 88.7 %all-gather.27.cloned.1.call-start = ((), (), s32[]{:S(2)}) async-start(), calls=%async_computation.16 | async-start | bytes 3932160 | tf_op jit(solution)/shard_map/all_gather | solution.py:137
  32.9 93.2 %all-gather.35.cloned.1.call-start = ((), (), s32[]{:S(2)}) async-start(), calls=%async_computation.33 | async-start | bytes 2654208 | tf_op jit(solution)/shard_map/all_gather | solution.py:128
  33.8 157.2 %all-gather.37.cloned.1.call-start = ((), (), s32[]{:S(2)}) async-start(), calls=%async_computation.34 | async-start | bytes 2654208 | tf_op jit(solution)/shard_map/all_gather | solution.py:127
  34.8 176.8 %all-gather.39.cloned.1.call-start = ((), (), s32[]{:S(2)}) async-start(), calls=%async_computation.35 | async-start | bytes 2654208 | tf_op jit(solution)/shard_map/all_gather | solution.py:133
  35.7 292.0 %reduce-scatter.25.cloned.1.call-start = ((), (), s32[]{:S(2)}) async-start(), calls=%async_computation.17 | async-start | bytes 7864320 | tf_op jit(solution)/shard_map/reduce_scatter | solution.py:162
  219.6 176.3 %all-gather.29.cloned.1.call-start = ((), (), s32[]{:S(2)}) async-start(), calls=%async_computation.18 | async-start | bytes 3932160 | tf_op jit(solution)/shard_map/all_gather | solution.py:137
  331.7 94.3 %all-gather.41.cloned.1.call-start = ((), (), s32[]{:S(2)}) async-start(), calls=%async_computation.36 | async-start | bytes 2654208 | tf_op jit(solution)/shard_map/all_gather | solution.py:128
  332.5 227.3 %all-gather.43.cloned.1.call-start = ((), (), s32[]{:S(2)}) async-start(), calls=%async_computation.37 | async-start | bytes 2654208 | tf_op jit(solution)/shard_map/all_gather | solution.py:127
  333.2 248.7 %all-gather.45.cloned.1.call-start = ((), (), s32[]{:S(2)}) async-start(), calls=%async_computation.38 | async-start | bytes 2654208 | tf_op jit(solution)/shard_map/all_gather | solution.py:133
  333.9 248.0 %all-gather.31.cloned.1.call-start = ((), (), s32[]{:S(2)}) async-start(), calls=%async_computation.20 | async-start | bytes 3932160 | tf_op jit(solution)/shard_map/all_gather | solution.py:195
  334.5 429.3 %all-reduce.61.cloned.1.call-start = ((), (), s32[]{:S(2)}) async-start(), calls=%async_computation.39 | async-start | bytes 2097152 | tf_op jit(solution)/shard_map/psum | solution.py:239
  689.2 182.3 %reduce-scatter.29.cloned.1.call-start = ((), (), s32[]{:S(2)}) async-start(), calls=%async_computation.21 | async-start | bytes 7864320 | tf_op jit(solution)/shard_map/reduce_scatter | solution.py:273
  761.5 179.5 %all-gather.33.cloned.1.call-start = ((), (), s32[]{:S(2)}) async-start(), calls=%async_computation.22 | async-start | bytes 3932160 | tf_op jit(solution)/shard_map/all_gather | solution.py:195
  876.9 216.4 %all-reduce.63.cloned.1.call-start = ((), (), s32[]{:S(2)}) async-start(), calls=%async_computation.40 | async-start | bytes 2097152 | tf_op jit(solution)/shard_map/psum | solution.py:239
  1042.5 105.9 %reduce-scatter.43.cloned.1.call-start = ((), (), s32[]{:S(2)}) async-start(), calls=%async_computation.29 | async-start | bytes 884736 | tf_op jit(solution)/shard_map/reduce_scatter | solution.py:301
  1045.0 124.9 %reduce-scatter.41.cloned.1.call-start = ((), (), s32[]{:S(2)}) async-start(), calls=%async_computation.28 | async-start | bytes 884736 | tf_op jit(solution)/shard_map/reduce_scatter | solution.py:301
  1100.8 158.7 %reduce-scatter.51.cloned.1.call-start = ((), (), s32[]{:S(2)}) async-start(), calls=%async_computation.42 | async-start | bytes 442368
  1104.3 156.1 %reduce-scatter.55.cloned.1.call-start = ((), (), s32[]{:S(2)}) async-start(), calls=%async_computation.44 | async-start | bytes 73728
  1105.2 180.4 %reduce-scatter.49.cloned.1.call-start = ((), (), s32[]{:S(2)}) async-start(), calls=%async_computation.41 | async-start | bytes 442368
  1147.4 170.8 %reduce-scatter.53.cloned.1.call-start = ((), (), s32[]{:S(2)}) async-start(), calls=%async_computation.43 | async-start | bytes 73728
  1148.3 207.7 %all-reduce.59.cloned.1.call-start = ((), (), s32[]{:S(2)}) async-start(), calls=%async_computation.30 | async-start | bytes 393216 | tf_op jit(solution)/shard_map/psum | solution.py:331
  1171.6 230.3 %reduce-scatter.47.cloned.1.call-start = ((), (), s32[]{:S(2)}) async-start(), calls=%async_computation.32 | async-start | bytes 2654208 | tf_op jit(solution)/shard_map/reduce_scatter | solution.py:313
  1178.9 268.9 %reduce-scatter.45.cloned.1.call-start = ((), (), s32[]{:S(2)}) async-start(), calls=%async_computation.31 | async-start | bytes 2654208 | tf_op jit(solution)/shard_map/reduce_scatter | solution.py:313
  1186.1 307.7 %reduce-scatter.39.cloned.1.call-start = ((), (), s32[]{:S(2)}) async-start(), calls=%async_computation.27 | async-start | bytes 2654208 | tf_op jit(solution)/shard_map/reduce_scatter | solution.py:298
  1192.8 347.0 %reduce-scatter.37.cloned.1.call-start = ((), (), s32[]{:S(2)}) async-start(), calls=%async_computation.26 | async-start | bytes 2654208 | tf_op jit(solution)/shard_map/reduce_scatter | solution.py:298
  1226.1 359.7 %reduce-scatter.35.cloned.1.call-start = ((), (), s32[]{:S(2)}) async-start(), calls=%async_computation.25 | async-start | bytes 2654208 | tf_op jit(solution)/shard_map/reduce_scatter | solution.py:295
  1232.6 398.9 %reduce-scatter.33.cloned.1.call-start = ((), (), s32[]{:S(2)}) async-start(), calls=%async_computation.24 | async-start | bytes 2654208 | tf_op jit(solution)/shard_map/reduce_scatter | solution.py:295
  1238.3 506.3 %reduce-scatter.31.cloned.1.call-start = ((), (), s32[]{:S(2)}) async-start(), calls=%async_computation.23 | async-start | bytes 7864320 | tf_op jit(solution)/shard_map/reduce_scatter | solution.py:273
  1249.7 609.0 %reduce-scatter.27.cloned.1.call-start = ((), (), s32[]{:S(2)}) async-start(), calls=%async_computation.19 | async-start | bytes 7864320 | tf_op jit(solution)/shard_map/reduce_scatter | solution.py:162
  1261.5 483.2 %copy-start.20 = (bf16[256,1536]{1,0:T(8,128)(2,1)S(1)}, bf16[256,1536]{1,0:T(8,128)(2,1)}, u32[]{:S(2)}) copy-start(bf16[256,1536]{1,0:T(8,128)(2,1)} %param.29) | copy-start | bytes 2359300
  1261.5 483.2 %copy-start.110 = (f32[1536]{0:T(1024)S(1)}, f32[1536]{0:T(1024)}, u32[]{:S(2)}) copy-start(f32[1536]{0:T(1024)} %copy-done.109) | copy-start | bytes 18436
  1261.5 483.1 %copy-start.148 = (f32[256]{0:T(256)S(1)}, f32[256]{0:T(256)}, u32[]{:S(2)}) copy-start(f32[256]{0:T(256)} %copy-done.147) | copy-start | bytes 3076
  (216 other events, 4178.3 us)
Sparse Core Ops, SparseCore 0:
  33.0 62.8 all-gather.26
  98.4 27.6 all-gather.34
  128.5 29.0 all-gather.36
  159.3 29.0 all-gather.38
  219.7 107.9 reduce-scatter.24
  331.8 63.9 all-gather.28
  398.3 27.6 all-gather.40
  427.9 29.0 all-gather.42
  458.8 29.0 all-gather.44
  489.3 63.4 all-gather.30
  689.3 50.8 all-reduce.60
  761.6 109.8 reduce-scatter.28
  877.0 63.9 all-gather.32
  1042.5 50.6 all-reduce.62
  1096.9 34.4 reduce-scatter.42
  1134.9 34.9 reduce-scatter.40
  1173.4 33.8 reduce-scatter.50
  1210.1 33.2 reduce-scatter.54
  1247.3 33.8 reduce-scatter.48
  1285.0 33.2 reduce-scatter.52
  1321.1 34.8 all-reduce.58
  1359.7 42.1 reduce-scatter.46
  1405.3 42.4 reduce-scatter.44
  1451.4 42.4 reduce-scatter.38
  1497.2 42.4 reduce-scatter.36
  1543.3 42.4 reduce-scatter.34
  1589.0 42.4 reduce-scatter.32
  1633.9 110.7 reduce-scatter.30
  1747.1 111.5 reduce-scatter.26
where the time goes:
time: 1880 us; the launch traced here: 1870 us
  waiting for transfers between devices  876 us (47%)
  matrix products  384 us (20%)
  local copies, waits for them, and re-layouts  222 us (12%)
  other arithmetic  198 us (11%)
  blocking collectives  167 us (9%)
  between operations  19.8 us (1%)
    reduce_scatter x2, waiting for transfers between devices, shards(): lax.psum_scatter(back_summed + jnp.einsum('tj,dj->td', row_slice(low_step...  215 us
    reduce_scatter x2, waiting for transfers between devices, shards(): lax.psum_scatter(jnp.dot(row_slice(mixed, jnp.int32(0), row_count * lax.a...  191 us
    dot_general x8, matrix products, ssd_scan(): jnp.einsum('cqs,cqsh,cshp->cqhp', scores, decays, weighted, precision=HIG...  131 us
    reduce_scatter x2, waiting for transfers between devices, shards(): lax.psum_scatter(grad_out.astype(jnp.bfloat16), 'dp', scatter_dimension=1...  90.1 us
    reduce_scatter x2, waiting for transfers between devices, shards(): lax.psum_scatter(grad_weight_x.astype(jnp.bfloat16), 'dp', scatter_dimens...  89.8 us
    reduce_scatter x2, waiting for transfers between devices, shards(): lax.psum_scatter(grad_weight_z.astype(jnp.bfloat16), 'dp', scatter_dimens...  89.6 us
    psum x2, waiting for transfers between devices, shards(): grad_bvals, grad_cvals = lax.psum((grad_bvals, grad_cvals), 'tensor')  48.2 us
    dot_general x8, matrix products, ssd_scan(): jnp.einsum('cqn,chpn->cqhp', c_blocks, entering, precision=HIGHEST)  44.8 us
  transfers between devices with their start and end apart: 29, of which 19 were waited for; matrix products, arithmetic and copies ran while one was open for 30% of the time, Pallas kernels for 0%

commit v1 on v0

v1 whole, which is shorter than its diff:
```python
import functools

import jax
import jax.numpy as jnp
from jax import lax
from jax.sharding import PartitionSpec as P
import jax.experimental.pallas as pl
import jax.experimental.pallas.tpu as pltpu

GROUP = 256
EPSILON = 1e-05
BF = jnp.bfloat16
F32 = jnp.float32
WIDTH = 64
MIB = 1024 * 1024


def nn(a, b):
    return lax.dot_general(a, b, (((1,), (0,)), ((), ())), preferred_element_type=F32)


def nt(a, b):
    return lax.dot_general(a, b, (((1,), (1,)), ((), ())), preferred_element_type=F32)


def parts3(v):
    one = v.astype(BF)
    rest = v - one.astype(F32)
    two = rest.astype(BF)
    three = (rest - two.astype(F32)).astype(BF)
    return one, two, three


def sum_rows(select, v):
    one, two, three = parts3(v)
    return nn(select, one) + nn(select, two) + nn(select, three)


def sum_lanes(v, select):
    one = v.astype(BF)
    two = (v - one.astype(F32)).astype(BF)
    return nn(one, select) + nn(two, select)


def silu_parts(v):
    sig = 1.0 / (1.0 + jnp.exp(-v))
    return sig, v * sig


def softplus(v):
    return jnp.maximum(v, 0.0) + jnp.log1p(jnp.exp(-jnp.abs(v)))


def pair_spread(column_values, pair, lane_low):
    low = column_values[:, 2 * pair : 2 * pair + 1]
    high = column_values[:, 2 * pair + 1 : 2 * pair + 2]
    return jnp.where(lane_low, low, high)


def spread(column_values, pairs, lane_low):
    return jnp.concatenate([pair_spread(column_values, p, lane_low) for p in range(pairs)], axis=1)


def conv_pre(padded, taps, bias, length):
    count = 4
    total = bias
    for k in range(count):
        total = total + taps[k : k + 1, :] * padded[pl.ds(8 - (count - 1) + k, length), :]
    return total


def fwd_kernel(
    rows_ref, wz_ref, wx_ref, wbc_ref, wdt_ref, wot_ref,
    cv_ref, cvb_ref, cs_ref, csb_ref, sb_ref, rate_ref, skip_ref, gg_ref,
    gate_ref, val_ref, st_ref, dt_ref, y_ref, ent_ref, mixed_ref, part_ref, ssq_ref,
    state, vpad, spad,
):
    step = pl.program_id(0)
    length = rows_ref.shape[0]
    inner = wz_ref.shape[1]
    pairs = inner // 128

    @pl.when(step == 0)
    def _():
        state[...] = jnp.zeros_like(state)
        vpad[0:8, :] = jnp.zeros((8, inner), F32)
        spad[0:8, :] = jnp.zeros((8, spad.shape[1]), F32)

    @pl.when(step > 0)
    def _():
        vpad[0:8, :] = vpad[length : length + 8, :]
        spad[0:8, :] = spad[length : length + 8, :]

    rows = rows_ref[...]
    gate_ref[...] = nn(rows, wz_ref[...])
    val = nn(rows, wx_ref[...])
    val_ref[...] = val
    vpad[8 : length + 8, :] = val
    st = nn(rows, wbc_ref[...])
    st_ref[...] = st
    spad[8 : length + 8, :] = st
    dt_in = nn(rows, wdt_ref[...])
    dt_ref[...] = dt_in

    _, v = silu_parts(conv_pre(vpad, cv_ref, cvb_ref[...], length))
    _, bc = silu_parts(conv_pre(spad, cs_ref, csb_ref[...], length))
    half = bc.shape[1] // 2
    bb = bc[:, :half].astype(BF)
    cb = bc[:, half:].astype(BF)
    dt = softplus(dt_in + sb_ref[...])
    q_index = lax.broadcasted_iota(jnp.int32, (length, length), 0)
    s_index = lax.broadcasted_iota(jnp.int32, (length, length), 1)
    causal = q_index >= s_index
    tril = jnp.where(causal, 1.0, 0.0).astype(BF)
    a = sum_rows(tril, dt * rate_ref[...])
    a_rows = a.T
    lane_low = lax.broadcasted_iota(jnp.int32, (length, 128), 1) < WIDTH
    dt_x = spread(dt, pairs, lane_low)
    a_x = spread(a, pairs, lane_low)
    x = v * dt_x
    xb = x.astype(BF)
    scores = jnp.where(causal, nt(cb, bb), 0.0)
    inside = []
    zero = jnp.zeros((length, 128), BF)
    for p in range(pairs):
        xp = xb[:, 128 * p : 128 * (p + 1)]
        total = None
        for j in range(2):
            h = 2 * p + j
            decay = jnp.exp(jnp.minimum(a[:, h : h + 1] - a_rows[h : h + 1, :], 0.0))
            m = (scores * decay).astype(BF)
            term = nn(m, jnp.where(lane_low, xp, zero) if j == 0 else jnp.where(lane_low, zero, xp))
            total = term if total is None else total + term
        inside.append(total)
    entering = state[...]
    ent_ref[0] = entering
    outside = jnp.exp(a_x) * nn(cb, entering.astype(BF))
    a_last = a_x[length - 1 : length, :]
    xw = (x * jnp.exp(a_last - a_x)).astype(BF)
    state[...] = jnp.exp(a_last) * entering + nn(bc[:, :half].T.astype(BF), xw)
    y = jnp.concatenate(inside, axis=1) + outside + skip_ref[...] * v
    y_ref[...] = y
    _, sgate = silu_parts(gate_ref[...])
    gated = y * sgate
    square = (gated * gated).astype(BF)
    ssq_ref[...] = nt(jnp.ones((8, inner), BF), square)
    mixed = (gated * gg_ref[...]).astype(BF)
    mixed_ref[...] = mixed
    part_ref[...] = nt(mixed, wot_ref[...]).astype(BF)


def whole(shape):
    return pl.BlockSpec(shape, lambda i: (0,) * len(shape), pipeline_mode=pl.Buffered(1))


def forward_mix(rows, weights, params):
    tokens, width = rows.shape
    inner = weights[0].shape[1]
    bc_width = weights[2].shape[1]
    dt_width = weights[3].shape[1]
    half = bc_width // 2
    q = GROUP
    blocks = tokens // q
    tok = lambda n: pl.BlockSpec((q, n), lambda i: (i, 0))
    outs = [
        ((tokens, inner), F32, tok(inner)),
        ((tokens, inner), F32, tok(inner)),
        ((tokens, bc_width), F32, tok(bc_width)),
        ((tokens, dt_width), F32, tok(dt_width)),
        ((tokens, inner), F32, tok(inner)),
        ((blocks, half, inner), F32, pl.BlockSpec((1, half, inner), lambda i: (i, 0, 0))),
        ((tokens, inner), BF, tok(inner)),
        ((tokens, width), BF, tok(width)),
        ((8, tokens), F32, pl.BlockSpec((8, q), lambda i: (0, i))),
    ]
    return pl.pallas_call(
        fwd_kernel,
        grid=(blocks,),
        in_specs=[tok(width)] + [whole(w.shape) for w in (*weights, *params)],
        out_specs=[o[2] for o in outs],
        out_shape=[jax.ShapeDtypeStruct(o[0], o[1]) for o in outs],
        scratch_shapes=[
            pltpu.VMEM((half, inner), F32),
            pltpu.VMEM((q + 8, inner), F32),
            pltpu.VMEM((q + 8, bc_width), F32),
        ],
        compiler_params=pltpu.CompilerParams(
            dimension_semantics=("arbitrary",), vmem_limit_bytes=56 * MIB
        ),
        name="mix_forward",
    )(rows, *weights, *params)


def bwd_kernel(
    gb_ref, e_ref, gate_ref, val_ref, valp_ref, st_ref, stp_ref, dt_ref, y_ref, ent_ref,
    wz_ref, wx_ref, wbc_ref, wdt_ref, wot_ref,
    cv_ref, cvb_ref, cs_ref, csb_ref, sb_ref, rate_ref, skip_ref, gg_ref, pick_ref,
    dgate_ref, dval_ref, dst_ref, ddt_ref, dpart_ref, gvec_ref, gst_ref, gdt_ref,
    dstate, vpad, spad, dvpad, dspad,
):
    step = pl.program_id(0)
    blocks = pl.num_programs(0)
    length = gb_ref.shape[0]
    inner = wz_ref.shape[1]
    bc_width = wbc_ref.shape[1]
    half = bc_width // 2
    pairs = inner // 128

    @pl.when(step == 0)
    def _():
        dstate[...] = jnp.zeros_like(dstate)
        dvpad[length : length + 8, :] = jnp.zeros((8, inner), F32)
        dspad[length : length + 8, :] = jnp.zeros((8, bc_width), F32)
        gvec_ref[...] = jnp.zeros_like(gvec_ref)
        gst_ref[...] = jnp.zeros_like(gst_ref)
        gdt_ref[...] = jnp.zeros_like(gdt_ref)

    @pl.when(step > 0)
    def _():
        dvpad[length : length + 8, :] = dvpad[0:8, :]
        dspad[length : length + 8, :] = dspad[0:8, :]

    first = step == blocks - 1
    vpad[0:8, :] = jnp.where(first, 0.0, valp_ref[...])
    spad[0:8, :] = jnp.where(first, 0.0, stp_ref[...])
    vpad[8 : length + 8, :] = val_ref[...]
    spad[8 : length + 8, :] = st_ref[...]

    pre_v = conv_pre(vpad, cv_ref, cvb_ref[...], length)
    sig_v, v = silu_parts(pre_v)
    pre_s = conv_pre(spad, cs_ref, csb_ref[...], length)
    sig_s, bc = silu_parts(pre_s)
    bb = bc[:, :half].astype(BF)
    cb = bc[:, half:].astype(BF)
    z = dt_ref[...] + sb_ref[...]
    dt = softplus(z)
    rate = rate_ref[...]
    s_index = lax.broadcasted_iota(jnp.int32, (length, length), 0)
    q_index = lax.broadcasted_iota(jnp.int32, (length, length), 1)
    upper = q_index >= s_index
    a = sum_rows(jnp.where(s_index >= q_index, 1.0, 0.0).astype(BF), dt * rate)
    a_rows = a.T
    lane_low = lax.broadcasted_iota(jnp.int32, (length, 128), 1) < WIDTH
    dt_x = spread(dt, pairs, lane_low)
    a_x = spread(a, pairs, lane_low)
    x = v * dt_x
    xb = x.astype(BF)
    skip = skip_ref[...]

    y = y_ref[...]
    gate = gate_ref[...]
    sig_g, sgate = silu_parts(gate)
    gated = y * sgate
    dm = nn(gb_ref[...], wot_ref[...])
    e = e_ref[...].T[:, 0:1]
    dgated = dm * gg_ref[...] - e * gated
    dgate = (dgated * y * (sig_g * (1.0 + gate * (1.0 - sig_g)))).astype(BF)
    dgate_ref[...] = dgate
    dy = dgated * sgate
    dyb = dy.astype(BF)
    dyf = dyb.astype(F32)

    scores = jnp.where(upper, nt(bb, cb), 0.0)
    zero = jnp.zeros((length, 128), BF)
    dscores = jnp.zeros((length, length), F32)
    dx_list = []
    for p in range(pairs):
        xp = xb[:, 128 * p : 128 * (p + 1)]
        dp = dyb[:, 128 * p : 128 * (p + 1)]
        total = None
        for j in range(2):
            h = 2 * p + j
            decay = jnp.exp(jnp.minimum(a_rows[h : h + 1, :] - a[:, h : h + 1], 0.0))
            m = (scores * decay).astype(BF)
            dh = jnp.where(lane_low, dp, zero) if j == 0 else jnp.where(lane_low, zero, dp)
            term = nn(m, dh)
            total = term if total is None else total + term
            dscores = dscores + nt(xp, dh) * decay
        dx_list.append(total)
    dx_in = jnp.concatenate(dx_list, axis=1)
    dscores = jnp.where(upper, dscores, 0.0)
    db = nn(dscores.astype(BF), cb)
    dc = nn(dscores.T.astype(BF), bb)

    entering = ent_ref[0]
    dleaving = dstate[...]
    dleaving_b = dleaving.astype(BF)
    ea = jnp.exp(a_x)
    a_last = a_x[length - 1 : length, :]
    ea_last = jnp.exp(a_last)
    w = jnp.exp(a_last - a_x)
    dxw = nn(bb, dleaving_b) * w
    db = db + nt((x * w).astype(BF), dleaving_b)
    eady = (ea * dyf).astype(BF)
    dc = dc + nt(eady, entering.astype(BF))
    dstate[...] = ea_last * dleaving + nn(bc[:, half:].T.astype(BF), eady)
    dx = dx_in + dxw
    u = x * dxw
    last_add = jnp.sum(u, axis=0, keepdims=True) + ea_last * jnp.sum(
        entering * dleaving, axis=0, keepdims=True
    )
    da_x = dyf * (y - skip * v) - xb.astype(F32) * dx_in - u
    row_index = lax.broadcasted_iota(jnp.int32, (length, inner), 0)
    da_x = da_x + jnp.where(row_index == length - 1, last_add, 0.0)
    pick = pick_ref[...]
    da = sum_lanes(da_x, pick)
    dr = sum_rows(jnp.where(upper, 1.0, 0.0).astype(BF), da)
    ddt = sum_lanes(dx * v, pick) + dr * rate
    dz = ddt * (1.0 / (1.0 + jnp.exp(-z)))
    ddtb = dz.astype(BF)
    ddt_ref[...] = ddtb
    gdt_ref[0:1, :] += jnp.sum(dz, axis=0, keepdims=True)
    gdt_ref[1:2, :] += jnp.sum(dr * dt * rate, axis=0, keepdims=True)

    dpre_v = (skip * dy + dt_x * dx) * (sig_v * (1.0 + pre_v * (1.0 - sig_v)))
    dvpad[0:length, :] = dpre_v
    dval = jnp.zeros((length, inner), F32)
    for k in range(4):
        dval = dval + cv_ref[k : k + 1, :] * dvpad[pl.ds(3 - k, length), :]
        gvec_ref[k : k + 1, :] += jnp.sum(
            dpre_v * vpad[pl.ds(5 + k, length), :], axis=0, keepdims=True
        )
    gvec_ref[4:5, :] += jnp.sum(dpre_v, axis=0, keepdims=True)
    gvec_ref[5:6, :] += jnp.sum(gated * dm, axis=0, keepdims=True)
    gvec_ref[6:7, :] += jnp.sum(dy * v, axis=0, keepdims=True)
    dvalb = dval.astype(BF)
    dval_ref[...] = dvalb

    dbc = jnp.concatenate([db, dc], axis=1)
    dpre_s = dbc * (sig_s * (1.0 + pre_s * (1.0 - sig_s)))
    dspad[0:length, :] = dpre_s
    dst = jnp.zeros((length, bc_width), F32)
    for k in range(4):
        dst = dst + cs_ref[k : k + 1, :] * dspad[pl.ds(3 - k, length), :]
        gst_ref[k : k + 1, :] += jnp.sum(
            dpre_s * spad[pl.ds(5 + k, length), :], axis=0, keepdims=True
        )
    gst_ref[4:5, :] += jnp.sum(dpre_s, axis=0, keepdims=True)
    dstb = dst.astype(BF)
    dst_ref[...] = dstb
    dpart = nt(dgate, wz_ref[...]) + nt(dvalb, wx_ref[...])
    dpart = dpart + nt(dstb, wbc_ref[...]) + nt(ddtb, wdt_ref[...])
    dpart_ref[...] = dpart.astype(BF)


def backward_mix(gb, e_rows, kept, weights, params, pick):
    gate, val, st, dt, y, ent = kept
    tokens, width = gb.shape
    inner = weights[0].shape[1]
    bc_width = weights[2].shape[1]
    dt_width = weights[3].shape[1]
    half = bc_width // 2
    q = GROUP
    blocks = tokens // q
    back = lambda i: blocks - 1 - i
    tok = lambda n: pl.BlockSpec((q, n), lambda i: (back(i), 0))
    halo = lambda n: pl.BlockSpec(
        (8, n), lambda i: (jnp.maximum(back(i) * (q // 8) - 1, 0), 0)
    )
    fixed = lambda r, c: pl.BlockSpec((r, c), lambda i: (0, 0))
    outs = [
        ((tokens, inner), BF, tok(inner)),
        ((tokens, inner), BF, tok(inner)),
        ((tokens, bc_width), BF, tok(bc_width)),
        ((tokens, dt_width), BF, tok(dt_width)),
        ((tokens, width), BF, tok(width)),
        ((8, inner), F32, fixed(8, inner)),
        ((8, bc_width), F32, fixed(8, bc_width)),
        ((8, dt_width), F32, fixed(8, dt_width)),
    ]
    return pl.pallas_call(
        bwd_kernel,
        grid=(blocks,),
        in_specs=[
            tok(width),
            pl.BlockSpec((8, q), lambda i: (0, back(i))),
            tok(inner), tok(inner), halo(inner), tok(bc_width), halo(bc_width), tok(dt_width),
            tok(inner),
            pl.BlockSpec((1, half, inner), lambda i: (back(i), 0, 0)),
        ]
        + [whole(w.shape) for w in (*weights, *params, pick)],
        out_specs=[o[2] for o in outs],
        out_shape=[jax.ShapeDtypeStruct(o[0], o[1]) for o in outs],
        scratch_shapes=[
            pltpu.VMEM((half, inner), F32),
            pltpu.VMEM((q + 8, inner), F32),
            pltpu.VMEM((q + 8, bc_width), F32),
            pltpu.VMEM((q + 8, inner), F32),
            pltpu.VMEM((q + 8, bc_width), F32),
        ],
        compiler_params=pltpu.CompilerParams(
            dimension_semantics=("arbitrary",), vmem_limit_bytes=60 * MIB
        ),
        name="mix_backward",
    )(gb, e_rows, gate, val, val, st, st, dt, y, ent, *weights, *params, pick)


def pad_to(v, rows, columns):
    return jnp.pad(v, ((0, rows - v.shape[0]), (0, columns - v.shape[1])))


def shards(
    hidden_in,
    out_grad,
    norm_gain,
    proj_z,
    proj_x,
    proj_bc,
    proj_dt,
    conv_value,
    conv_value_bias,
    conv_state,
    conv_state_bias,
    step_bias,
    log_decay,
    skip_gain,
    gate_gain,
    proj_out,
):
    tensor_count = lax.axis_size("tensor")
    dp_count = lax.axis_size("dp")
    layers, shard_rows, inner = proj_z.shape
    rows_own, width = hidden_in.shape
    heads = step_bias.shape[1]
    bc_width = proj_bc.shape[2]
    inner_all = inner * tensor_count

    def gather_dp(v, axis=0):
        return lax.all_gather(v, "dp", axis=axis, tiled=True)

    def rows_of(v):
        return v.astype(F32).reshape(-1, v.shape[-1])

    small = jnp.concatenate(
        [
            conv_state.reshape(layers, -1),
            conv_state_bias,
        ],
        axis=1,
    )
    small = jnp.pad(small, ((0, 0), (0, shard_rows - small.shape[1])))
    step_block = jnp.concatenate(
        [
            proj_dt,
            norm_gain[:, :, None],
            small[:, :, None],
            jnp.zeros((layers, shard_rows, 128 - heads - 2), BF),
        ],
        axis=2,
    )
    weights, params, gains = [], [], []
    lane = jnp.arange(128)[None, :]
    for l in range(layers):
        wide = gather_dp(step_block[l])
        gains.append(wide[:, heads].astype(F32)[None, :])
        per = bc_width // dp_count
        smalls = wide[:, heads + 1].reshape(dp_count, shard_rows)[:, : 5 * per]
        smalls = smalls.astype(F32).reshape(dp_count, 5, per)
        smalls = jnp.transpose(smalls, (1, 0, 2)).reshape(5, bc_width)
        wdt = jnp.where(lane < heads, wide, jnp.zeros_like(wide))
        weights.append(
            (
                gather_dp(proj_z[l]),
                gather_dp(proj_x[l]),
                gather_dp(proj_bc[l]),
                wdt,
                gather_dp(proj_out[l].T),
            )
        )
        params.append(
            (
                pad_to(rows_of(conv_value[l]), 8, inner),
                rows_of(conv_value_bias[l]),
                pad_to(smalls[:4], 8, bc_width),
                smalls[4:5],
                pad_to(rows_of(step_bias[l]), 1, 128),
                pad_to(-jnp.exp(rows_of(log_decay[l])), 1, 128),
                jnp.repeat(rows_of(skip_gain[l]), WIDTH, axis=1),
                rows_of(gate_gain[l]),
            )
        )
    pick = (jnp.arange(inner)[:, None] // WIDTH == jnp.arange(128)[None, :]).astype(BF)

    residual = hidden_in.astype(F32)
    kept = []
    for l in range(layers):
        r1 = lax.rsqrt(jnp.mean(residual * residual, axis=1, keepdims=True) + EPSILON)
        normed = (residual * r1 * gains[l]).astype(BF)
        rows = lax.all_gather(normed, "tensor", axis=0, tiled=True)
        gate, val, st, dt, y, ent, mixed, part, ssq = forward_mix(rows, weights[l], params[l])
        total = lax.psum_scatter(part, "tensor", scatter_dimension=0, tiled=True).astype(F32)
        ssq_own = lax.psum_scatter(ssq[0], "tensor", scatter_dimension=0, tiled=True)
        r2 = lax.rsqrt(ssq_own / inner_all + EPSILON)[:, None]
        branch = total * r2
        kept.append((residual, r1, rows, (gate, val, st, dt, y, ent), mixed, r2, branch))
        residual = residual + branch
    gradient = out_grad.astype(F32)
    scattered = [None] * layers
    summed = [None] * layers
    for l in reversed(range(layers)):
        residual_in, r1, rows, saved, mixed, r2, branch = kept[l]
        gb = gradient.astype(BF)
        e = r2[:, 0] ** 2 * jnp.sum(gb.astype(F32) * branch, axis=1) / inner_all
        scaled = (r2 * gradient).astype(BF)
        grad_rows = lax.all_gather(scaled, "tensor", axis=0, tiled=True)
        e_rows = jnp.broadcast_to(
            lax.all_gather(e, "tensor", axis=0, tiled=True)[None, :], (8, rows.shape[0])
        )
        dgate, dval, dst, ddt, dpart, gvec, gst, gdt = backward_mix(
            grad_rows, e_rows, saved, weights[l], params[l], pick
        )
        dnormed = lax.psum_scatter(dpart, "tensor", scatter_dimension=0, tiled=True).astype(F32)
        back = lambda left, right: jnp.einsum(
            "td,tj->dj", left, right, preferred_element_type=F32
        )
        gain = gains[l]
        dn = dnormed * gain
        grad_gain = jnp.sum(residual_in * r1 * dnormed, axis=0)
        cross = jnp.sum(dn * residual_in, axis=1, keepdims=True)
        gradient = gradient + r1 * dn - r1**3 * residual_in * cross / width
        scatter = lambda v: lax.psum_scatter(
            v.astype(BF), "dp", scatter_dimension=0, tiled=True
        ).astype(F32)
        scattered[l] = (
            scatter(back(rows, dgate)),
            scatter(back(rows, dval)),
            scatter(back(rows, dst)),
            scatter(back(rows, ddt)),
            scatter(back(grad_rows, mixed)),
        )
        summed[l] = (gvec, gdt, gst, grad_gain)
    stack = lambda i: jnp.stack([scattered[l][i] for l in range(layers)])
    gvec = jnp.stack([s[0] for s in summed])
    gdt = jnp.stack([s[1] for s in summed])
    gst = jnp.stack([s[2] for s in summed])
    ggain = jnp.stack([s[3] for s in summed])
    gvec, gdt = lax.psum((gvec, gdt), "dp")
    gst, ggain, gbc = lax.psum((gst, ggain, stack(2).astype(BF)), "tensor")
    gst, ggain = lax.psum((gst, ggain), "dp")
    own = lambda v, axis: lax.dynamic_slice_in_dim(
        v, lax.axis_index("dp") * (v.shape[axis] // dp_count), v.shape[axis] // dp_count, axis
    )
    gst = own(gst, 2)
    return (
        residual,
        gradient,
        own(ggain, 1),
        stack(0),
        stack(1),
        gbc.astype(F32),
        stack(3)[:, :, :heads],
        gvec[:, 0:4],
        gvec[:, 4],
        gst[:, 0:4],
        gst[:, 4],
        gdt[:, 0, :heads],
        gdt[:, 1, :heads],
        jnp.sum(gvec[:, 6].reshape(layers, heads, WIDTH), axis=2),
        gvec[:, 5],
        jnp.transpose(stack(4), (0, 2, 1)),
    )


def solution(mesh):
    placed = (
        P(("dp", "tensor"), None),
        P(("dp", "tensor"), None),
        P(None, "dp"),
        P(None, "dp", "tensor"),
        P(None, "dp", "tensor"),
        P(None, "dp", None),
        P(None, "dp", "tensor"),
        P(None, None, "tensor"),
        P(None, "tensor"),
        P(None, None, "dp"),
        P(None, "dp"),
        P(None, "tensor"),
        P(None, "tensor"),
        P(None, "tensor"),
        P(None, "tensor"),
        P(None, "tensor", "dp"),
    )
    return jax.shard_map(
        shards,
        mesh=mesh,
        in_specs=placed,
        out_specs=(
            P(("dp", "tensor"), None),
            P(("dp", "tensor"), None),
            P(None, "dp"),
            P(None, "dp", "tensor"),
            P(None, "dp", "tensor"),
            P(None, "dp", None),
            P(None, "dp", "tensor"),
            P(None, None, "tensor"),
            P(None, "tensor"),
            P(None, None, "dp"),
            P(None, "dp"),
            P(None, "tensor"),
            P(None, "tensor"),
            P(None, "tensor"),
            P(None, "tensor"),
            P(None, "tensor", "dp"),
        ),
        check_vma=False,
    )
```

time: 1880 us -> 1360 us (0.72)
  matrix products: 384 us -> 50.4 us
  local copies, waits for them, and re-layouts: 222 us -> 31.5 us
  other arithmetic: 198 us -> 33.9 us
  Pallas kernels: 0 us -> 132 us
  waiting for transfers between devices: 876 us -> 986 us
  blocking collectives: 167 us -> 103 us
    dot_general x60 -> x10, matrix products: 384 us -> 50.4 us  [shards(): jnp.einsum('td,tj->dj', left, right, preferred_element_type=F32)]
    all_gather x10, waiting for transfers between devices: 60.4 us -> 362 us  [the longest x2 131 us: shards(): rows = lax.all_gather(normed, 'tensor', axis=0, tiled=True)]
    reduce_scatter x12 -> x14, waiting for transfers between devices: 696 us -> 537 us  [the longest x10 323 us: shards(): lax.psum_scatter(v.astype(BF), 'dp', scatter_dimension=0, tiled=True)]
    pallas_call x0 -> x4, Pallas kernels: none -> 132 us  [the longest x2 79.3 us: backward_mix(): pl.pallas_call(bwd_kernel, grid=(blocks,), in_specs=[tok(width), pl.Block...]
    psum x6 -> x1, blocking collectives: 76.4 us -> 18.3 us  [shards(): gst, ggain, gbc = lax.psum((gst, ggain, stack(2).astype(BF)), 'tensor')]
    reduce_sum x26 -> x7, other arithmetic: 69 us -> 11.1 us  [the longest x2 4.68 us: shards(): e = r2[:, 0] ** 2 * jnp.sum(gb.astype(F32) * branch, axis=1) / inner_all]
    reshape x28 -> x1, local copies, waits for them, and re-layouts: 46.8 us -> 0.08 us  [shards(): conv_state.reshape(layers, -1)]
    mul x40 -> x0, local copies, waits for them, and re-layouts: 42.7 us -> none  [the longest x8 15.9 us: ssd_scan(): inputs * step_sizes[:, :, None]]
  transfers between devices with their start and end apart: 29 -> 26, of which waited for: 19 -> 23; matrix products, arithmetic and copies ran while one was open for 30% -> 6% of each run, Pallas kernels for 0% -> 3%
where the time goes in v1:
time: 1360 us; the launch traced here: 1350 us
  waiting for transfers between devices  986 us (72%)
  Pallas kernels  132 us (10%)
  blocking collectives  103 us (8%)
  matrix products  50.4 us (4%)
  other arithmetic  33.9 us (2%)
  local copies, waits for them, and re-layouts  31.5 us (2%)
  between operations  15.7 us (1%)
    reduce_scatter x10, waiting for transfers between devices, shards(): lax.psum_scatter(v.astype(BF), 'dp', scatter_dimension=0, tiled=True)  323 us
    all_gather x2, waiting for transfers between devices, shards(): rows = lax.all_gather(normed, 'tensor', axis=0, tiled=True)  131 us
    all_gather x6, waiting for transfers between devices, gather_dp(): return lax.all_gather(v, 'dp', axis=axis, tiled=True)  128 us
    reduce_scatter x2, waiting for transfers between devices, shards(): lax.psum_scatter(dpart, 'tensor', scatter_dimension=0, tiled=True)  119 us
    all_gather x2, waiting for transfers between devices, shards(): grad_rows = lax.all_gather(scaled, 'tensor', axis=0, tiled=True)  103 us
    reduce_scatter x2, waiting for transfers between devices, shards(): lax.psum_scatter(part, 'tensor', scatter_dimension=0, tiled=True)  94.3 us
    pallas_call x2, Pallas kernels, backward_mix(): pl.pallas_call(bwd_kernel, grid=(blocks,), in_specs=[tok(width), pl.Block...  79.3 us
    pallas_call x2, Pallas kernels, forward_mix(): pl.pallas_call(fwd_kernel, grid=(blocks,), in_specs=[tok(width)] + [whole...  52.5 us
  transfers between devices with their start and end apart: 26, of which 23 were waited for; matrix products, arithmetic and copies ran while one was open for 6% of the time, Pallas kernels for 3%

profile of v1, /device:TPU:0, one launch (start us, length us, event | category | flops | bytes accessed | tf_op | source)
XLA Modules:
  0.0 1354.2 jit_solution(7941442642942550620)
XLA Ops:
  12.1 11.0 all-gather
  28.1 12.1 all-gather.4
  41.3 10.8 all-gather.3
  53.7 20.9 %all-gather.33.cloned.1.call-done = bf16[1,1536,768]{2,1,0:T(8,128)(2,1)} async-done(((bf16[1,192,768]{2,1,0:T(8,128)(2,1)}), bf16[1,1536,768]{2,1,0:T(8,128)(2,1)}) %all-gather.33.cloned.1.call-update) | async-done | bytes 2359312 | tf_op jit(solution)/shard_map/all_gather | solution.py:429
  74.6 31.5 %all-gather.35.cloned.1.call-done = bf16[1,1536,768]{2,1,0:T(8,128)(2,1)} async-done(((bf16[1,192,768]{2,1,0:T(8,128)(2,1)}), bf16[1,1536,768]{2,1,0:T(8,128)(2,1)}) %all-gather.35.cloned.1.call-update) | async-done | bytes 2359312 | tf_op jit(solution)/shard_map/all_gather | solution.py:429
  106.2 65.5 %all-gather.21.cloned.1.call-done.rows_ref = bf16[1024,1536]{1,0:T(8,128)(2,1)} async-done(((bf16[256,1536]{1,0:T(8,128)(2,1)}), bf16[1024,1536]{1,0:T(8,128)(2,1)}) %all-gather.21.cloned.1.call-update) | async-done | bytes 3145744 | tf_op jit(solution)/shard_map/all_gather | solution.py:489
  171.7 26.2 %mix_forward.2 = (f32[1024,768]{1,0:T(8,128)}, f32[1024,768]{1,0:T(8,128)}, f32[1024,256]{1,0:T(8,128)}, f32[1024,128]{1,0:T(8,128)}, f32[1024,768]{1,0:T(8,128)...) custom-call(bf16[1024,1536]{1,0:T(8,128)(2,1)} %all-gather.21.cloned.1.ca, ...), custom_call_target="tpu_custom_call" | custom-call | tf_op jit(solution)/shard_map/mix_forward/pallas_call | solution.py:176
  212.0 45.3 %reduce-scatter.15.cloned.1.call-done = bf16[256,1536]{1,0:T(8,128)(2,1)} async-done(((bf16[1024,1536]{1,0:T(8,128)(2,1)}), bf16[256,1536]{1,0:T(8,128)(2,1)}) %reduce-scatter.15.cloned.1.call-update) | async-done | bytes 786448 | tf_op jit(solution)/shard_map/reduce_scatter | solution.py:491
  264.6 12.8 all-gather.7
  277.3 12.7 all-gather.27.cloned.1.call-done.wot_ref
  290.0 31.5 %all-gather.37.cloned.1.call-done = bf16[1,1536,768]{2,1,0:T(8,128)(2,1)} async-done(((bf16[1,192,768]{2,1,0:T(8,128)(2,1)}), bf16[1,1536,768]{2,1,0:T(8,128)(2,1)}) %all-gather.37.cloned.1.call-update) | async-done | bytes 2359312 | tf_op jit(solution)/shard_map/all_gather | solution.py:429
  321.5 31.5 %all-gather.39.cloned.1.call-done = bf16[1,1536,768]{2,1,0:T(8,128)(2,1)} async-done(((bf16[1,192,768]{2,1,0:T(8,128)(2,1)}), bf16[1,1536,768]{2,1,0:T(8,128)(2,1)}) %all-gather.39.cloned.1.call-update) | async-done | bytes 2359312 | tf_op jit(solution)/shard_map/all_gather | solution.py:429
  353.0 65.7 %all-gather.25.cloned.1.call-done.rows_ref = bf16[1024,1536]{1,0:T(8,128)(2,1)} async-done(((bf16[256,1536]{1,0:T(8,128)(2,1)}), bf16[1024,1536]{1,0:T(8,128)(2,1)}) %all-gather.25.cloned.1.call-update) | async-done | bytes 3145744 | tf_op jit(solution)/shard_map/all_gather | solution.py:489
  418.7 26.2 %mix_forward.3 = (f32[1024,768]{1,0:T(8,128)}, f32[1024,768]{1,0:T(8,128)}, f32[1024,256]{1,0:T(8,128)}, f32[1024,128]{1,0:T(8,128)}, f32[1024,768]{1,0:T(8,128)...) custom-call(bf16[1024,1536]{1,0:T(8,128)(2,1)} %all-gather.25.cloned.1.ca, ...), custom_call_target="tpu_custom_call" | custom-call | tf_op jit(solution)/shard_map/mix_forward/pallas_call | solution.py:176
  455.1 49.0 %reduce-scatter.17.cloned.1.call-done = bf16[256,1536]{1,0:T(8,128)(2,1)} async-done(((bf16[1024,1536]{1,0:T(8,128)(2,1)}), bf16[256,1536]{1,0:T(8,128)(2,1)}) %reduce-scatter.17.cloned.1.call-update) | async-done | bytes 786448 | tf_op jit(solution)/shard_map/reduce_scatter | solution.py:491
  517.2 53.0 %all-gather.29.cloned.1.call-done.gb_ref = bf16[1024,1536]{1,0:T(8,128)(2,1)} async-done(((bf16[256,1536]{1,0:T(8,128)(2,1)}), bf16[1024,1536]{1,0:T(8,128)(2,1)}) %all-gather.29.cloned.1.call-update) | async-done | bytes 3145744 | tf_op jit(solution)/shard_map/all_gather | solution.py:505
  570.8 39.6 %mix_backward.2 = (bf16[1024,768]{1,0:T(8,128)(2,1)}, bf16[1024,768]{1,0:T(8,128)(2,1)}, bf16[1024,256]{1,0:T(8,128)(2,1)}, bf16[1024,128]{1,0:T(8,128)(2,1)}, b...) custom-call(bf16[1024,1536]{1,0:T(8,128)(2,1)} %all-gather.29.cloned.1.call-done.gb_ref, ...), custom_call_target="tpu_custom_call" | custom-call | tf_op jit(solution)/shard_map/mix_backward/pallas_call | solution.py:371
  610.5 59.0 %reduce-scatter.19.cloned.1.call-done = bf16[256,1536]{1,0:T(8,128)(2,1)} async-done(((bf16[1024,1536]{1,0:T(8,128)(2,1)}), bf16[256,1536]{1,0:T(8,128)(2,1)}) %reduce-scatter.19.cloned.1.call-update) | async-done | bytes 786448 | tf_op jit(solution)/shard_map/reduce_scatter | solution.py:512
  689.8 49.8 %all-gather.31.cloned.1.call-done.gb_ref = bf16[1024,1536]{1,0:T(8,128)(2,1)} async-done(((bf16[256,1536]{1,0:T(8,128)(2,1)}), bf16[1024,1536]{1,0:T(8,128)(2,1)}) %all-gather.31.cloned.1.call-update) | async-done | bytes 3145744 | tf_op jit(solution)/shard_map/all_gather | solution.py:505
  740.2 39.7 %mix_backward.3 = (bf16[1024,768]{1,0:T(8,128)(2,1)}, bf16[1024,768]{1,0:T(8,128)(2,1)}, bf16[1024,256]{1,0:T(8,128)(2,1)}, bf16[1024,128]{1,0:T(8,128)(2,1)}, b...) custom-call(bf16[1024,1536]{1,0:T(8,128)(2,1)} %all-gather.31.cloned.1.call-done.gb_ref, ...), custom_call_target="tpu_custom_call" | custom-call | tf_op jit(solution)/shard_map/mix_backward/pallas_call | solution.py:371
  790.7 26.0 %reduce-scatter.31.cloned.1.call-done = bf16[192,256]{1,0:T(8,128)(2,1)} async-done(((bf16[1536,256]{1,0:T(8,128)(2,1)}), bf16[192,256]{1,0:T(8,128)(2,1)}) %reduce-scatter.31.cloned.1.call-update) | async-done | bytes 98320 | tf_op jit(solution)/shard_map/reduce_scatter | solution.py:521
  864.0 27.4 %reduce-scatter.35.cloned.1.call-done = bf16[192,128]{1,0:T(8,128)(2,1)} async-done(((bf16[1536,128]{1,0:T(8,128)(2,1)}), bf16[192,128]{1,0:T(8,128)(2,1)}) %reduce-scatter.35.cloned.1.call-update) | async-done | bytes 49168 | tf_op jit(solution)/shard_map/reduce_scatter | solution.py:521
  893.0 36.0 %all-reduce.16.cloned.1.call-done = bf16[2,192,256]{2,1,0:T(8,128)(2,1)} async-done(((bf16[2,192,256]{2,1,0:T(8,128)(2,1)}), bf16[2,192,256]{2,1,0:T(8,128)(2,1)}) %all-reduce.16.cloned.1.call-update) | async-done | bytes 196624 | tf_op jit(solution)/shard_map/psum | solution.py:538
  930.7 44.2 %reduce-scatter.41.cloned.1.call-done = bf16[192,768]{1,0:T(8,128)(2,1)} async-done(((bf16[1536,768]{1,0:T(8,128)(2,1)}), bf16[192,768]{1,0:T(8,128)(2,1)}) %reduce-scatter.41.cloned.1.call-update) | async-done | bytes 294928 | tf_op jit(solution)/shard_map/reduce_scatter | solution.py:521
  974.9 45.7 %reduce-scatter.39.cloned.1.call-done = bf16[192,768]{1,0:T(8,128)(2,1)} async-done(((bf16[1536,768]{1,0:T(8,128)(2,1)}), bf16[192,768]{1,0:T(8,128)(2,1)}) %reduce-scatter.39.cloned.1.call-update) | async-done | bytes 294928 | tf_op jit(solution)/shard_map/reduce_scatter | solution.py:521
  1022.8 44.1 %reduce-scatter.29.cloned.1.call-done = bf16[192,768]{1,0:T(8,128)(2,1)} async-done(((bf16[1536,768]{1,0:T(8,128)(2,1)}), bf16[192,768]{1,0:T(8,128)(2,1)}) %reduce-scatter.29.cloned.1.call-update) | async-done | bytes 294928 | tf_op jit(solution)/shard_map/reduce_scatter | solution.py:521
  1066.9 45.8 %reduce-scatter.27.cloned.1.call-done = bf16[192,768]{1,0:T(8,128)(2,1)} async-done(((bf16[1536,768]{1,0:T(8,128)(2,1)}), bf16[192,768]{1,0:T(8,128)(2,1)}) %reduce-scatter.27.cloned.1.call-update) | async-done | bytes 294928 | tf_op jit(solution)/shard_map/reduce_scatter | solution.py:521
  1114.9 44.1 %reduce-scatter.25.cloned.1.call-done = bf16[192,768]{1,0:T(8,128)(2,1)} async-done(((bf16[1536,768]{1,0:T(8,128)(2,1)}), bf16[192,768]{1,0:T(8,128)(2,1)}) %reduce-scatter.25.cloned.1.call-update) | async-done | bytes 294928 | tf_op jit(solution)/shard_map/reduce_scatter | solution.py:521
  1158.9 45.7 %reduce-scatter.23.cloned.1.call-done = bf16[192,768]{1,0:T(8,128)(2,1)} async-done(((bf16[1536,768]{1,0:T(8,128)(2,1)}), bf16[192,768]{1,0:T(8,128)(2,1)}) %reduce-scatter.23.cloned.1.call-update) | async-done | bytes 294928 | tf_op jit(solution)/shard_map/reduce_scatter | solution.py:521
  1206.9 60.4 %reduce-scatter.21.cloned.1.call-done = bf16[256,1536]{1,0:T(8,128)(2,1)} async-done(((bf16[1024,1536]{1,0:T(8,128)(2,1)}), bf16[256,1536]{1,0:T(8,128)(2,1)}) %reduce-scatter.21.cloned.1.call-update) | async-done | bytes 786448 | tf_op jit(solution)/shard_map/reduce_scatter | solution.py:512
  1269.3 18.3 %all-reduce.12 = (f32[2,1536]{1,0:T(2,128)}, f32[2,8,256]{2,1,0:T(8,128)}) all-reduce(f32[2,1536]{1,0:T(2,128)S(1)} %pad_maximum_fusion.4, f32[2,8,256]{2,1,0:T(8,128)S(1)} %pad_maximum_fusion.3), channel_id=1, replica_groups=mesh['dp'=8,'tensor'=4] {'tensor'}, use_global_device_ids=true, to_apply=%region_14.15 | all-reduce | flops 7168 | bytes 57344 | tf_op jit(solution)/shard_map/psum | solution.py:538
  1289.3 48.3 %all-reduce.18.cloned.1.call-done = (f32[2,1536]{1,0:T(2,128)}, f32[2,8,768]{2,1,0:T(8,128)}, f32[2,8,256]{2,1,0:T(8,128)}, f32[2,8,128]{2,1,0:T(8,128)}) async-done(((f32[2,1536]{1,0:T(2,128)}, f32[2,8,768]{2,1,0:T(8,128)}, f32[2,8,256]{2,1,0:T(8,128)}, f32[2,8,128]{2,1,0:T(8,128)}), (f32[2,1536]{1,0:T(2,128)}, f32[2,8,768]{2,1,0:T(8,128)}, f32[2,8,256]{2,1,0:T(8,128)}, ...) | async-done | bytes 86032 | tf_op jit(solution)/shard_map/psum | solution.py:539
  (241 shorter events, 158.4 us)
Async XLA Ops:
  7.2 46.5 %all-gather.23.cloned.1.call-start = ((), (), s32[]{:S(2)}) async-start(), calls=%async_computation.15 | async-start | bytes 2654208 | tf_op jit(solution)/shard_map/all_gather | solution.py:429
  9.3 65.3 %all-gather.33.cloned.1.call-start = ((), (), s32[]{:S(2)}) async-start(), calls=%async_computation.35 | async-start | bytes 2654208 | tf_op jit(solution)/shard_map/all_gather | solution.py:429
  10.3 95.9 %all-gather.35.cloned.1.call-start = ((), (), s32[]{:S(2)}) async-start(), calls=%async_computation.36 | async-start | bytes 2654208 | tf_op jit(solution)/shard_map/all_gather | solution.py:429
  11.2 160.5 %all-gather.21.cloned.1.call-start = ((), (), s32[]{:S(2)}) async-start(), calls=%async_computation.14 | async-start | bytes 3932160 | tf_op jit(solution)/shard_map/all_gather | solution.py:489
  24.9 27.3 %copy-start.18 = (bf16[2,768]{1,0:T(2,128)(2,1)S(1)}, bf16[2,768]{1,0:T(2,128)(2,1)}, u32[]{:S(2)}) copy-start(bf16[2,768]{1,0:T(2,128)(2,1)} %param.24) | copy-start | bytes 9220
  24.9 232.4 %reduce-scatter.15.cloned.1.call-start = ((), (), s32[]{:S(2)}) async-start(), calls=%async_computation.16 | async-start | bytes 3932160 | tf_op jit(solution)/shard_map/reduce_scatter | solution.py:491
  198.0 92.0 %all-gather.27.cloned.1.call-start = ((), (), s32[]{:S(2)}) async-start(), calls=%async_computation.18 | async-start | bytes 2654208 | tf_op jit(solution)/shard_map/all_gather | solution.py:429
  198.6 122.9 %all-gather.37.cloned.1.call-start = ((), (), s32[]{:S(2)}) async-start(), calls=%async_computation.37 | async-start | bytes 2654208 | tf_op jit(solution)/shard_map/all_gather | solution.py:429
  199.3 153.7 %all-gather.39.cloned.1.call-start = ((), (), s32[]{:S(2)}) async-start(), calls=%async_computation.38 | async-start | bytes 2654208 | tf_op jit(solution)/shard_map/all_gather | solution.py:429
  200.1 218.6 %all-gather.25.cloned.1.call-start = ((), (), s32[]{:S(2)}) async-start(), calls=%async_computation.17 | async-start | bytes 3932160 | tf_op jit(solution)/shard_map/all_gather | solution.py:489
  260.3 243.7 %reduce-scatter.17.cloned.1.call-start = ((), (), s32[]{:S(2)}) async-start(), calls=%async_computation.19 | async-start | bytes 3932160 | tf_op jit(solution)/shard_map/reduce_scatter | solution.py:491
  444.9 59.1 %copy-start.7 = (bf16[256,1536]{1,0:T(8,128)(2,1)S(1)}, bf16[256,1536]{1,0:T(8,128)(2,1)}, u32[]{:S(2)}) copy-start(bf16[256,1536]{1,0:T(8,128)(2,1)} %param.17) | copy-start | bytes 2359300
  445.0 125.2 %all-gather.29.cloned.1.call-start = ((), (), s32[]{:S(2)}) async-start(), calls=%async_computation.20 | async-start | bytes 3932160 | tf_op jit(solution)/shard_map/all_gather | solution.py:505
  506.5 163.0 %reduce-scatter.19.cloned.1.call-start = ((), (), s32[]{:S(2)}) async-start(), calls=%async_computation.21 | async-start | bytes 3932160 | tf_op jit(solution)/shard_map/reduce_scatter | solution.py:512
  610.4 61.0 %copy-start.8 = (bf16[256,1536]{1,0:T(8,128)(2,1)S(1)}, bf16[256,1536]{1,0:T(8,128)(2,1)}, u32[]{:S(2)}) copy-start(bf16[256,1536]{1,0:T(8,128)(2,1)} %reduce-scatter.17.cloned.1.call-done) | copy-start | bytes 2359300
  610.4 129.2 %all-gather.31.cloned.1.call-start = ((), (), s32[]{:S(2)}) async-start(), calls=%async_computation.22 | async-start | bytes 3932160 | tf_op jit(solution)/shard_map/all_gather | solution.py:505
  675.9 114.8 %reduce-scatter.33.cloned.1.call-start = ((), (), s32[]{:S(2)}) async-start(), calls=%async_computation.29 | async-start | bytes 884736 | tf_op jit(solution)/shard_map/reduce_scatter | solution.py:521
  679.8 136.9 %reduce-scatter.31.cloned.1.call-start = ((), (), s32[]{:S(2)}) async-start(), calls=%async_computation.28 | async-start | bytes 884736 | tf_op jit(solution)/shard_map/reduce_scatter | solution.py:521
  740.2 39.7 %copy-start.1 = (bf16[1024,1536]{1,0:T(8,128)(2,1)S(1)}, bf16[1024,1536]{1,0:T(8,128)(2,1)}, u32[]{:S(2)}) copy-start(bf16[1024,1536]{1,0:T(8,128)(2,1)} %all-gather.21.cloned.1.call-done.rows_ref) | copy-start | bytes 9437188
  782.9 81.1 %reduce-scatter.37.cloned.1.call-start = ((), (), s32[]{:S(2)}) async-start(), calls=%async_computation.32 | async-start | bytes 442368 | tf_op jit(solution)/shard_map/reduce_scatter | solution.py:521
  786.7 104.7 %reduce-scatter.35.cloned.1.call-start = ((), (), s32[]{:S(2)}) async-start(), calls=%async_computation.31 | async-start | bytes 442368 | tf_op jit(solution)/shard_map/reduce_scatter | solution.py:521
  786.8 31.9 %copy-start.30 = (bf16[1024,768]{1,0:T(8,128)(2,1)S(1)}, bf16[1024,768]{1,0:T(8,128)(2,1)}, u32[]{:S(2)}) copy-start(bf16[1024,768]{1,0:T(8,128)(2,1)} %get-tuple-element.83) | copy-start | bytes 4718596
  790.6 138.4 %all-reduce.16.cloned.1.call-start = ((), (), s32[]{:S(2)}) async-start(), calls=%async_computation.30 | async-start | bytes 393216 | tf_op jit(solution)/shard_map/psum | solution.py:538
  818.4 156.6 %reduce-scatter.41.cloned.1.call-start = ((), (), s32[]{:S(2)}) async-start(), calls=%async_computation.34 | async-start | bytes 2654208 | tf_op jit(solution)/shard_map/reduce_scatter | solution.py:521
  824.7 195.9 %reduce-scatter.39.cloned.1.call-start = ((), (), s32[]{:S(2)}) async-start(), calls=%async_computation.33 | async-start | bytes 2654208 | tf_op jit(solution)/shard_map/reduce_scatter | solution.py:521
  832.2 234.7 %reduce-scatter.29.cloned.1.call-start = ((), (), s32[]{:S(2)}) async-start(), calls=%async_computation.27 | async-start | bytes 2654208 | tf_op jit(solution)/shard_map/reduce_scatter | solution.py:521
  839.6 273.2 %reduce-scatter.27.cloned.1.call-start = ((), (), s32[]{:S(2)}) async-start(), calls=%async_computation.26 | async-start | bytes 2654208 | tf_op jit(solution)/shard_map/reduce_scatter | solution.py:521
  847.0 312.0 %reduce-scatter.25.cloned.1.call-start = ((), (), s32[]{:S(2)}) async-start(), calls=%async_computation.25 | async-start | bytes 2654208 | tf_op jit(solution)/shard_map/reduce_scatter | solution.py:521
  854.5 350.2 %reduce-scatter.23.cloned.1.call-start = ((), (), s32[]{:S(2)}) async-start(), calls=%async_computation.24 | async-start | bytes 2654208 | tf_op jit(solution)/shard_map/reduce_scatter | solution.py:521
  861.9 405.4 %reduce-scatter.21.cloned.1.call-start = ((), (), s32[]{:S(2)}) async-start(), calls=%async_computation.23 | async-start | bytes 3932160 | tf_op jit(solution)/shard_map/reduce_scatter | solution.py:512
  862.6 475.0 %all-reduce.18.cloned.1.call-start = ((), (), s32[]{:S(2)}) async-start(), calls=%async_computation.39 | async-start | bytes 172032 | tf_op jit(solution)/shard_map/psum | solution.py:539
  1204.6 83.0 %copy-start.3 = (f32[256,1536]{1,0:T(8,128)S(1)}, f32[256,1536]{1,0:T(8,128)}, u32[]{:S(2)}) copy-start(f32[256,1536]{1,0:T(8,128)} %copy-done.2) | copy-start | bytes 4718596
  (31 other events, 158.1 us)
Sparse Core Ops, SparseCore 0:
  9.9 33.0 all-gather.22
  45.5 29.1 all-gather.32
  77.1 29.0 all-gather.34
  108.2 63.4 all-gather.20
  198.1 59.1 reduce-scatter.14
  259.0 30.9 all-gather.26
  292.4 29.0 all-gather.36
  324.0 29.0 all-gather.38
  355.1 63.4 all-gather.24
  445.1 58.8 reduce-scatter.16
  506.6 63.5 all-gather.28
  610.5 58.8 reduce-scatter.18
  676.0 63.5 all-gather.30
  743.2 33.6 reduce-scatter.32
  783.0 33.6 reduce-scatter.30
  820.2 33.8 reduce-scatter.36
  857.6 33.7 reduce-scatter.34
  894.1 34.8 all-reduce.15
  932.7 42.1 reduce-scatter.40
  978.1 42.4 reduce-scatter.38
  1024.4 42.4 reduce-scatter.28
  1070.2 42.4 reduce-scatter.26
  1116.4 42.4 reduce-scatter.24
  1162.1 42.4 reduce-scatter.22
  1207.0 60.2 reduce-scatter.20
  1287.7 49.8 all-reduce.17

commit v2 on v1

--- a/solution.py
+++ b/solution.py
@@ -1,4 +1,5 @@
 import functools
+import types
 
 import jax
 import jax.numpy as jnp
@@ -13,6 +14,7 @@
 F32 = jnp.float32
 WIDTH = 64
 MIB = 1024 * 1024
+WCHUNK = 384
 
 
 def nn(a, b):
@@ -69,16 +71,25 @@
     return total
 
 
+def blocks_of(w_ref, inner, bc_width):
+    sizes = (bc_width, 128, inner, inner, inner)
+    starts = [sum(sizes[:i]) for i in range(5)]
+    return [w_ref.at[:, pl.ds(s, z)] for s, z in zip(starts, sizes)]
+
+
 def fwd_kernel(
-    rows_ref, wz_ref, wx_ref, wbc_ref, wdt_ref, wot_ref,
-    cv_ref, cvb_ref, cs_ref, csb_ref, sb_ref, rate_ref, skip_ref, gg_ref,
-    gate_ref, val_ref, st_ref, dt_ref, y_ref, ent_ref, mixed_ref, part_ref, ssq_ref,
-    state, vpad, spad,
+    first, rows_ref, w_ref,
+    cv_ref, cvb_ref, cs_ref, csb_ref, sb_ref, rate_ref, skip_ref, gg_ref, gain_ref,
+    gate_ref, val_ref, st_ref, dt_ref, y_ref, ent_ref, part_ref, ssq_ref,
+    *rest,
 ):
+    normed_ref = rest[0] if first else None
+    state, vpad, spad = rest[-3:]
     step = pl.program_id(0)
     length = rows_ref.shape[0]
-    inner = wz_ref.shape[1]
+    inner = gg_ref.shape[1]
     pairs = inner // 128
+    wbc_ref, wdt_ref, wz_ref, wx_ref, wot_ref = blocks_of(w_ref, inner, cs_ref.shape[1])
 
     @pl.when(step == 0)
     def _():
@@ -92,6 +103,11 @@
         spad[0:8, :] = spad[length : length + 8, :]
 
     rows = rows_ref[...]
+    if first:
+        rows = rows.astype(F32)
+        r1 = lax.rsqrt(jnp.mean(rows * rows, axis=1, keepdims=True) + EPSILON)
+        rows = (rows * r1 * gain_ref[...]).astype(BF)
+        normed_ref[...] = rows
     gate_ref[...] = nn(rows, wz_ref[...])
     val = nn(rows, wx_ref[...])
     val_ref[...] = val
@@ -145,7 +161,6 @@
     square = (gated * gated).astype(BF)
     ssq_ref[...] = nt(jnp.ones((8, inner), BF), square)
     mixed = (gated * gg_ref[...]).astype(BF)
-    mixed_ref[...] = mixed
     part_ref[...] = nt(mixed, wot_ref[...]).astype(BF)
 
 
@@ -153,11 +168,11 @@
     return pl.BlockSpec(shape, lambda i: (0,) * len(shape), pipeline_mode=pl.Buffered(1))
 
 
-def forward_mix(rows, weights, params):
+def forward_mix(rows, packed, params, first):
     tokens, width = rows.shape
-    inner = weights[0].shape[1]
-    bc_width = weights[2].shape[1]
-    dt_width = weights[3].shape[1]
+    inner = params[0].shape[1]
+    bc_width = params[2].shape[1]
+    dt_width = 128
     half = bc_width // 2
     q = GROUP
     blocks = tokens // q
@@ -169,14 +184,15 @@
         ((tokens, dt_width), F32, tok(dt_width)),
         ((tokens, inner), F32, tok(inner)),
         ((blocks, half, inner), F32, pl.BlockSpec((1, half, inner), lambda i: (i, 0, 0))),
-        ((tokens, inner), BF, tok(inner)),
         ((tokens, width), BF, tok(width)),
         ((8, tokens), F32, pl.BlockSpec((8, q), lambda i: (0, i))),
     ]
+    if first:
+        outs.append(((tokens, width), BF, tok(width)))
     return pl.pallas_call(
-        fwd_kernel,
+        functools.partial(fwd_kernel, first),
         grid=(blocks,),
-        in_specs=[tok(width)] + [whole(w.shape) for w in (*weights, *params)],
+        in_specs=[tok(width)] + [whole(w.shape) for w in (packed, *params)],
         out_specs=[o[2] for o in outs],
         out_shape=[jax.ShapeDtypeStruct(o[0], o[1]) for o in outs],
         scratch_shapes=[
@@ -188,21 +204,23 @@
             dimension_semantics=("arbitrary",), vmem_limit_bytes=56 * MIB
         ),
         name="mix_forward",
-    )(rows, *weights, *params)
+    )(rows, packed, *params)
 
 
 def bwd_kernel(
     gb_ref, e_ref, gate_ref, val_ref, valp_ref, st_ref, stp_ref, dt_ref, y_ref, ent_ref,
-    wz_ref, wx_ref, wbc_ref, wdt_ref, wot_ref,
+    w_ref,
     cv_ref, cvb_ref, cs_ref, csb_ref, sb_ref, rate_ref, skip_ref, gg_ref, pick_ref,
-    dgate_ref, dval_ref, dst_ref, ddt_ref, dpart_ref, gvec_ref, gst_ref, gdt_ref,
+    dcat_ref, dpart_ref, gvec_ref, gst_ref, gdt_ref,
     dstate, vpad, spad, dvpad, dspad,
 ):
     step = pl.program_id(0)
     blocks = pl.num_programs(0)
     length = gb_ref.shape[0]
-    inner = wz_ref.shape[1]
-    bc_width = wbc_ref.shape[1]
+    inner = gg_ref.shape[1]
+    bc_width = cs_ref.shape[1]
+    wbc_ref, wdt_ref, wz_ref, wx_ref, wot_ref = blocks_of(w_ref, inner, bc_width)
+    dst_ref, ddt_ref, dgate_ref, dval_ref, mixed_ref = blocks_of(dcat_ref, inner, bc_width)
     half = bc_width // 2
     pairs = inner // 128
 
@@ -254,6 +272,7 @@
     dm = nn(gb_ref[...], wot_ref[...])
     e = e_ref[...].T[:, 0:1]
     dgated = dm * gg_ref[...] - e * gated
+    mixed_ref[...] = (gated * gg_ref[...]).astype(BF)
     dgate = (dgated * y * (sig_g * (1.0 + gate * (1.0 - sig_g)))).astype(BF)
     dgate_ref[...] = dgate
     dy = dgated * sgate
@@ -343,12 +362,13 @@
     dpart_ref[...] = dpart.astype(BF)
 
 
-def backward_mix(gb, e_rows, kept, weights, params, pick):
+def backward_mix(gb, e_rows, kept, packed, params, pick):
     gate, val, st, dt, y, ent = kept
     tokens, width = gb.shape
-    inner = weights[0].shape[1]
-    bc_width = weights[2].shape[1]
-    dt_width = weights[3].shape[1]
+    inner = params[0].shape[1]
+    bc_width = params[2].shape[1]
+    dt_width = 128
+    packed_width = packed.shape[1]
     half = bc_width // 2
     q = GROUP
     blocks = tokens // q
@@ -359,10 +379,7 @@
     )
     fixed = lambda r, c: pl.BlockSpec((r, c), lambda i: (0, 0))
     outs = [
-        ((tokens, inner), BF, tok(inner)),
-        ((tokens, inner), BF, tok(inner)),
-        ((tokens, bc_width), BF, tok(bc_width)),
-        ((tokens, dt_width), BF, tok(dt_width)),
+        ((tokens, packed_width), BF, tok(packed_width)),
         ((tokens, width), BF, tok(width)),
         ((8, inner), F32, fixed(8, inner)),
         ((8, bc_width), F32, fixed(8, bc_width)),
@@ -378,7 +395,7 @@
             tok(inner),
             pl.BlockSpec((1, half, inner), lambda i: (back(i), 0, 0)),
         ]
-        + [whole(w.shape) for w in (*weights, *params, pick)],
+        + [whole(w.shape) for w in (packed, *params, pick)],
         out_specs=[o[2] for o in outs],
         out_shape=[jax.ShapeDtypeStruct(o[0], o[1]) for o in outs],
         scratch_shapes=[
@@ -392,11 +409,478 @@
             dimension_semantics=("arbitrary",), vmem_limit_bytes=60 * MIB
         ),
         name="mix_backward",
-    )(gb, e_rows, gate, val, val, st, st, dt, y, ent, *weights, *params, pick)
+    )(gb, e_rows, gate, val, val, st, st, dt, y, ent, packed, *params, pick)
+
+
+class Step:
+    def __init__(self, **given):
+        self.rows = 0
+        self.width = 0
+        self.line = 4
+        self.chunks = 8
+        self.partial = False
+        self.gather = False
+        self.late = False
+        self.scale = False
+        self.inner = False
+        self.weights = 0
+        self.grads = 0
+        self.bits = 0
+        self.middle = None
+        self.__dict__.update(given)
+
+
+def remote(src, dst, send, recv, device):
+    return pltpu.make_async_remote_copy(
+        src_ref=src, dst_ref=dst, send_sem=send, recv_sem=recv,
+        device_id=device, device_id_type=pl.DeviceIdType.MESH,
+    )
+
+
+def when(condition):
+    return pl.when(condition)
+
+
+def comm_kernel(o, names, *refs):
+    r = types.SimpleNamespace(**dict(zip(names, refs)))
+    r.gbuf = [v for k, v in zip(names, refs) if k.startswith("gbuf")]
+    n, count, rows = o.line, o.chunks, o.rows
+    size = rows // count
+    t = lax.axis_index("tensor")
+    me = lax.axis_index("dp")
+    own_bits = [(me // (1 << b)) % 2 for b in range(o.bits)]
+    partner = [me + (1 - 2 * own_bits[b]) * (1 << b) for b in range(o.bits)]
+
+    barrier = pltpu.get_barrier_semaphore()
+    for k in range(1, n):
+        pl.semaphore_signal(
+            barrier, inc=1, device_id={"tensor": lax.rem(t + k, n)},
+            device_id_type=pl.DeviceIdType.MESH,
+        )
+    over_dp = o.weights or o.grads
+    if over_dp:
+        for b in range(o.bits):
+            pl.semaphore_signal(
+                barrier, inc=1, device_id={"dp": partner[b]}, device_id_type=pl.DeviceIdType.MESH
+            )
+    pl.semaphore_wait(barrier, n - 1 + (o.bits if over_dp else 0))
+
+    def at(s, c):
+        return pl.ds(pl.multiple_of(s * rows + c * size, size), size)
+
+    def piece(c):
+        return pl.ds(pl.multiple_of(c * size, size), size)
+
+    def hop(side, s, c, src):
+        buf = r.rbuf if side == 0 else r.lbuf
+        return remote(
+            src, buf.at[s, piece(c)], r.rs_send.at[side, s], r.rs_recv.at[side, s, c],
+            {"tensor": t + 1 if side == 0 else t - 1},
+        )
+
+    def reduce_items(side, c):
+        buf = r.rbuf if side == 0 else r.lbuf
+        edge = t == 0 if side == 0 else t == n - 1
+        order = range(n - 1, 0, -1) if side == 0 else range(0, n - 1)
+        for s in order:
+            further = s > t if side == 0 else s < t
+
+            @when(further & edge)
+            def _():
+                hop(side, s, c, r.part.at[at(s, c)]).start()
+
+            @when(further & jnp.logical_not(edge))
+            def _():
+                hop(side, s, c, buf.at[s, piece(c)]).wait_recv()
+                total = buf[s, piece(c), :].astype(F32) + r.part[at(s, c), :].astype(F32)
+                buf[s, piece(c), :] = total.astype(BF)
+                hop(side, s, c, buf.at[s, piece(c)]).start()
+
+    def own_total(c):
+        acc = r.acc
+        acc[...] = r.part[at(t, c), :].astype(F32)
+
+        @when(t > 0)
+        def _():
+            hop(0, t, c, r.rbuf.at[t, piece(c)]).wait_recv()
+            acc[...] += r.rbuf[t, piece(c), :].astype(F32)
+
+        @when(t < n - 1)
+        def _():
+            hop(1, t, c, r.lbuf.at[t, piece(c)]).wait_recv()
+            acc[...] += r.lbuf[t, piece(c), :].astype(F32)
+
+    def pass_on(side, s, c):
+        spot = r.full.at[at(s, c)]
+        return remote(
+            spot, spot, r.ag_send.at[side, s], r.ag_recv.at[side, s, c],
+            {"tensor": t + 1 if side == 0 else t - 1},
+        )
+
+    def forward_items(side, tau):
+        order = range(n - 2, -1, -1) if side == 0 else range(1, n)
+        for s in order:
+            away = t - s if side == 0 else s - t
+            late = max(s, n - 1 - s) if o.late else 0
+            c = tau - late - away
+
+            @when((away > 0) & (c >= 0) & (c < count))
+            def _():
+                pass_on(side, s, c).wait_recv()
+
+                @when(t < n - 1 if side == 0 else t > 0)
+                def _():
+                    pass_on(side, s, c).start()
+
+    def spot_of(k, ref):
+        return ref.at[:, pl.ds(pl.multiple_of(k * rows, rows), rows)]
+
+    def square_copy(k):
+        dest = lax.rem(t + k, n)
+        return remote(
+            spot_of(dest, r.ssq), r.sqbuf.at[k - 1], r.sq_send.at[k - 1],
+            r.sq_recv.at[k - 1], {"tensor": dest},
+        )
+
+    def inner_copy(k):
+        return remote(
+            spot_of(t, r.inner), spot_of(t, r.inner), r.in_send.at[k - 1],
+            r.in_recv.at[k - 1], {"tensor": lax.rem(t + k, n)},
+        )
+
+    def inner_arrival(k):
+        source = lax.rem(t + n - k, n)
+        return remote(
+            spot_of(source, r.inner), spot_of(source, r.inner), r.in_send.at[k - 1],
+            r.in_recv.at[k - 1], {"tensor": source},
+        )
+
+    def bit_order(parity):
+        high = list(range(o.bits - 1, 0, -1))
+        if parity == 1:
+            high = high[1:] + high[:1]
+        return high + [0]
+
+    def cols(j):
+        return pl.ds(pl.multiple_of(j * WCHUNK, WCHUNK), WCHUNK)
+
+    def spots(known):
+        return tuple(slice(None) if b in known else own_bits[b] for b in range(o.bits - 1, -1, -1))
+
+    def weight_copy(parity, stage, j):
+        order = bit_order(parity)
+        spot = r.wfull.at[(*spots(order[:stage]), slice(None), cols(j))]
+        src = r.wown.at[:, cols(j)] if stage == 0 else spot
+        return remote(
+            src, spot, r.wg_send.at[stage, j], r.wg_recv.at[stage, j],
+            {"dp": partner[order[stage]]},
+        )
+
+    def own_weights():
+        return pltpu.make_async_copy(r.wown, r.wfull.at[spots([])], r.wl_sem)
+
+    def each_parity(j, fn):
+        for parity in range(2):
+            @when((j >= 0) & (j < max(o.weights, o.grads)) & (lax.rem(j, 2) == parity))
+            def _():
+                fn(parity, j)
+
+    def weight_items(tau):
+        for stage in range(o.bits + 1):
+            def run(parity, j):
+                if stage > 0:
+                    weight_copy(parity, stage - 1, j).wait_recv()
+                if stage < o.bits:
+                    weight_copy(parity, stage, j).start()
+            each_parity(tau - stage, run)
+
+    def grad_order(parity):
+        high = list(range(1, o.bits))
+        if parity == 1:
+            high = high[1:] + high[:1]
+        return [0] + high
+
+    def grad_spot(parity, stage, mine):
+        order = grad_order(parity)
+        done, bit = order[:stage], order[stage]
+        spot = []
+        for b in range(o.bits - 1, -1, -1):
+            if b in done:
+                spot.append(own_bits[b])
+            elif b == bit:
+                spot.append(own_bits[b] if mine else 1 - own_bits[b])
+            else:
+                spot.append(slice(None))
+        return tuple(spot)
+
+    def grad_copy(parity, stage, j):
+        order = grad_order(parity)
+        return remote(
+            r.grad.at[(j, *grad_spot(parity, stage, False))], r.gbuf[stage].at[j],
+            r.gr_send.at[stage, j], r.gr_recv.at[stage, j],
+            {"dp": partner[order[stage]]},
+        )
+
+    def product(j):
+        left = lax.div(j, jnp.int32(5)) if o.bits else 0
+
+        def one(i, _):
+            spot = tuple((i // (1 << b)) % 2 for b in range(o.bits - 1, -1, -1))
+            depth = r.grad.shape[-2]
+            lhs = r.left[left, pl.ds(pl.multiple_of(i * depth, depth), depth), :]
+            r.grad[(j, *spot)] = nn(lhs, r.right[:, cols(j)]).astype(BF)
+            return 0
+
+        lax.fori_loop(0, 1 << o.bits, one, 0)
+
+    def grad_items(tau):
+        def first(parity, j):
+            product(j)
+            grad_copy(parity, 0, j).start()
+
+        each_parity(tau, first)
+        for stage in range(1, o.bits + 1):
+            def run(parity, j):
+                grad_copy(parity, stage - 1, j).wait_recv()
+                spot = grad_spot(parity, stage - 1, True)
+                free = [i for i, v in enumerate(spot) if isinstance(v, slice)]
+                buf = r.gbuf[stage - 1]
+                for combo in range(1 << len(free)):
+                    pick = [(combo >> i) % 2 for i in range(len(free))]
+                    full = list(spot)
+                    for i, v in zip(free, pick):
+                        full[i] = v
+                    total = r.grad[(j, *full)].astype(F32) + buf[(j, *pick)].astype(F32)
+                    if stage < o.bits:
+                        r.grad[(j, *full)] = total.astype(BF)
+                    else:
+                        r.gout[:, cols(j)] = total
+                if stage < o.bits:
+                    grad_copy(parity, stage, j).start()
+            each_parity(tau - stage, run)
+
+    if o.scale:
+        for k in range(1, n):
+            square_copy(k).start()
+    if o.weights:
+        own_weights().start()
+    if o.grads:
+        def turn(i, _):
+            strip = pl.ds(pl.multiple_of(i * 128, 128), 128)
+            r.left[0, strip, :] = r.lrows[:, strip].T
+            r.left[1, strip, :] = r.lgrad[:, strip].T
+            return 0
+        lax.fori_loop(0, o.width // 128, turn, 0)
+    if o.scale:
+        total = spot_of(t, r.ssq)[...]
+        for k in range(1, n):
+            square_copy(k).wait_recv()
+            total = total + r.sqbuf[k - 1]
+        scale = lax.rsqrt(total / (o.scale * 1.0) + EPSILON)
+        r.r2[...] = jnp.broadcast_to(scale.T[:, 0:1], (rows, 128))
+    if o.gather and not o.late:
+        r.full[pl.ds(pl.multiple_of(t * rows, rows), rows), :] = o.payload(r)
+    if o.middle is not None:
+        o.middle(r, None, None)
+
+    ends = [count + (n - 1)]
+    if o.late:
+        ends.append(count + 2 * (n - 1))
+    if over_dp:
+        ends.append(max(o.weights, o.grads) + o.bits)
+
+    def iteration(tau, _):
+        if o.partial:
+            for side in range(2):
+                c = tau - (t if side == 0 else n - 1 - t)
+
+                @when((c >= 0) & (c < count))
+                def _():
+                    reduce_items(side, c)
+
+            c_own = tau - jnp.maximum(t, n - 1 - t)
+
+            @when((c_own >= 0) & (c_own < count))
+            def _():
+                own_total(c_own)
+                out = o.middle(r, piece(c_own), r.acc[...])
+                if o.late:
+                    r.full[at(t, c_own), :] = out
+        if o.gather:
+            c_out = tau - jnp.maximum(t, n - 1 - t) if o.late else tau
+
+            @when((c_out >= 0) & (c_out < count))
+            def _():
+                @when(t < n - 1)
+                def _():
+                    pass_on(0, t, c_out).start()
+
+                @when(t > 0)
+                def _():
+                    pass_on(1, t, c_out).start()
+
+            for side in range(2):
+                forward_items(side, tau)
+        if o.weights:
+            @when(tau == 1)
+            def _():
+                own_weights().wait()
+            weight_items(tau)
+        if o.grads:
+            grad_items(tau)
+        return 0
+
+    lax.fori_loop(0, max(ends), iteration, 0)
+
+    if o.inner:
+        spot_of(t, r.inner)[...] = r.icol[...].T[0:8, :]
+        for k in range(1, n):
+            inner_copy(k).start()
+        for k in range(1, n):
+            inner_arrival(k).wait_recv()
+        for k in range(1, n):
+            inner_copy(k).wait_send()
+    if o.scale:
+        for k in range(1, n):
+            square_copy(k).wait_send()
+    for s in range(n):
+        for side in range(2):
+            inside = t < n - 1 if side == 0 else t > 0
+            if o.partial:
+                @when((s > t if side == 0 else s < t) & inside)
+                def _():
+                    buf = (r.rbuf if side == 0 else r.lbuf).at[s]
+                    remote(
+                        buf, buf, r.rs_send.at[side, s], r.rs_recv.at[side, s, 0],
+                        {"tensor": t + 1 if side == 0 else t - 1},
+                    ).wait_send()
+            if o.gather:
+                @when((s <= t if side == 0 else s >= t) & inside)
+                def _():
+                    spot = r.full.at[pl.ds(s * rows, rows)]
+                    remote(
+                        spot, spot, r.ag_send.at[side, s], r.ag_recv.at[side, s, 0],
+                        {"tensor": t + 1 if side == 0 else t - 1},
+                    ).wait_send()
+    for j in range(o.weights):
+        for stage in range(o.bits):
+            weight_copy(j % 2, stage, jnp.int32(j)).wait_send()
+    for j in range(o.grads):
+        for stage in range(o.bits):
+            grad_copy(j % 2, stage, jnp.int32(j)).wait_send()
+
+
+def comm_call(o, name, collective, inputs, outputs, **scratch):
+    n, count, rows, width = o.line, o.chunks, o.rows, o.width
+    dma = pltpu.SemaphoreType.DMA
+    if o.partial:
+        scratch.update(
+            rbuf=pltpu.VMEM((n, rows, width), BF),
+            lbuf=pltpu.VMEM((n, rows, width), BF),
+            acc=pltpu.VMEM((rows // count, width), F32),
+            rs_send=dma((2, n)),
+            rs_recv=dma((2, n, count)),
+        )
+    if o.gather:
+        scratch.update(ag_send=dma((2, n)), ag_recv=dma((2, n, count)))
+    if o.scale:
+        scratch.update(
+            sqbuf=pltpu.VMEM((n - 1, 8, rows), F32), sq_send=dma((n - 1,)), sq_recv=dma((n - 1,))
+        )
+    if o.inner:
+        scratch.update(
+            icol=pltpu.VMEM((rows, 128), F32), in_send=dma((n - 1,)), in_recv=dma((n - 1,))
+        )
+    if o.weights:
+        scratch.update(
+            wl_sem=dma(()),
+            wg_send=dma((o.bits, o.weights)),
+            wg_recv=dma((o.bits, o.weights)),
+        )
+    if o.grads:
+        depth = o.width >> o.bits
+        scratch.update(
+            grad=pltpu.VMEM((o.grads, *(2,) * o.bits, depth, WCHUNK), BF),
+            left=pltpu.VMEM((2, width, n * rows), BF),
+            gr_send=dma((o.bits, o.grads)),
+            gr_recv=dma((o.bits, o.grads)),
+        )
+        for stage in range(o.bits):
+            scratch["gbuf%d" % stage] = pltpu.VMEM(
+                (o.grads, *(2,) * (o.bits - 1 - stage), depth, WCHUNK), BF
+            )
+    names = [*inputs, *outputs, *scratch]
+    out = pl.pallas_call(
+        functools.partial(comm_kernel, o, names),
+        in_specs=[pl.BlockSpec(memory_space=i[1]) for i in inputs.values()],
+        out_specs=[pl.BlockSpec(memory_space=i[2]) for i in outputs.values()],
+        out_shape=[jax.ShapeDtypeStruct(i[0], i[1]) for i in outputs.values()],
+        scratch_shapes=list(scratch.values()),
+        compiler_params=pltpu.CompilerParams(
+            collective_id=collective, has_side_effects=True, vmem_limit_bytes=62 * MIB
+        ),
+        name=name,
+    )(*[i[0] for i in inputs.values()])
+    return dict(zip(outputs, out))
+
+
+def plain_payload(r):
+    return r.own[...]
+
+
+def scaled_payload(r):
+    return (r.r2[:, 0:1] * r.grad_in[...].astype(F32)).astype(BF)
+
+
+def forward_middle(r, at, total):
+    if at is None:
+        return None
+    branch = total * r.r2[at, 0:1]
+    residual = r.res[at, :].astype(F32) + branch
+    r.branch[at, :] = branch
+    r.res_out[at, :] = residual
+    r1 = lax.rsqrt(jnp.mean(residual * residual, axis=1, keepdims=True) + EPSILON)
+    return (residual * r1 * r.gain[...]).astype(BF)
+
+
+def last_middle(inner_all, r, at, total):
+    if at is None:
+        return None
+    r2 = r.r2[at, 0:1]
+    branch = total * r2
+    r.res_out[at, :] = r.res[at, :].astype(F32) + branch
+    dot = jnp.sum(r.grad_in[at, :].astype(F32) * branch, axis=1, keepdims=True)
+    r.icol[at, :] = jnp.broadcast_to(r2 * r2 * dot / inner_all, (dot.shape[0], 128))
+    return None
+
+
+def backward_middle(inner_all, r, at, total):
+    if at is None:
+        r.ggain[...] = jnp.zeros_like(r.ggain)
+        return None
+    res = r.res[at, :].astype(F32)
+    width = res.shape[1]
+    r1 = lax.rsqrt(jnp.mean(res * res, axis=1, keepdims=True) + EPSILON)
+    hat = res * r1
+    r.ggain[0:1, :] += jnp.sum(hat * total, axis=0, keepdims=True)
+    dn = total * r.gain[...]
+    cross = jnp.sum(dn * hat, axis=1, keepdims=True) / width
+    grad = r.grad_in[at, :].astype(F32) + r1 * (dn - hat * cross)
+    r.grad_out[at, :] = grad
+    if inner_all is None:
+        return None
+    r2 = r.r2[at, 0:1]
+    dot = jnp.sum(grad.astype(BF).astype(F32) * r.branch[at, :], axis=1, keepdims=True)
+    r.icol[at, :] = jnp.broadcast_to(r2 * r2 * dot / inner_all, (dot.shape[0], 128))
+    return (r2 * grad).astype(BF)
 
 
 def pad_to(v, rows, columns):
     return jnp.pad(v, ((0, rows - v.shape[0]), (0, columns - v.shape[1])))
+
+
+def rows_of(v):
+    return v.astype(F32).reshape(-1, v.shape[-1])
 
 
 def shards(
@@ -419,54 +903,60 @@
 ):
     tensor_count = lax.axis_size("tensor")
     dp_count = lax.axis_size("dp")
+    bits = dp_count.bit_length() - 1
     layers, shard_rows, inner = proj_z.shape
     rows_own, width = hidden_in.shape
+    tokens = rows_own * tensor_count
     heads = step_bias.shape[1]
     bc_width = proj_bc.shape[2]
     inner_all = inner * tensor_count
-
-    def gather_dp(v, axis=0):
-        return lax.all_gather(v, "dp", axis=axis, tiled=True)
-
-    def rows_of(v):
-        return v.astype(F32).reshape(-1, v.shape[-1])
-
-    small = jnp.concatenate(
-        [
-            conv_state.reshape(layers, -1),
-            conv_state_bias,
-        ],
-        axis=1,
+    packed_width = bc_width + 128 + 3 * inner
+    column_chunks = packed_width // WCHUNK
+    vmem, far = pltpu.VMEM, pl.ANY
+
+    small = jnp.concatenate([conv_state.reshape(layers, -1), conv_state_bias], axis=1)
+    small = jnp.pad(small, ((0, 0), (0, shard_rows - small.shape[1])))
+    extra = jnp.stack([norm_gain, small], axis=1).reshape(2 * layers, shard_rows).T
+    packs = []
+    for l in range(layers):
+        packs.append(
+            jnp.concatenate(
+                [
+                    proj_bc[l],
+                    proj_dt[l],
+                    extra,
+                    jnp.zeros((shard_rows, 128 - heads - 2 * layers), BF),
+                    proj_z[l],
+                    proj_x[l],
+                    proj_out[l].T,
+                ],
+                axis=1,
+            )
+        )
+    full_shape = ((2,) * bits) + (shard_rows, packed_width)
+    common = dict(rows=rows_own, width=width, line=tensor_count, bits=bits)
+
+    def weight_io(l):
+        return dict(wown=(packs[l], far)), dict(wfull=(full_shape, BF, far))
+
+    whole_rows, own_rows = ((tokens, width), BF, vmem), ((rows_own, width), F32, vmem)
+    win, wout = weight_io(0)
+    got = comm_call(
+        Step(gather=True, payload=plain_payload, weights=column_chunks, **common),
+        "gather_first", 1,
+        dict(own=(hidden_in, vmem), **win),
+        dict(full=whole_rows, **wout),
     )
-    small = jnp.pad(small, ((0, 0), (0, shard_rows - small.shape[1])))
-    step_block = jnp.concatenate(
-        [
-            proj_dt,
-            norm_gain[:, :, None],
-            small[:, :, None],
-            jnp.zeros((layers, shard_rows, 128 - heads - 2), BF),
-        ],
-        axis=2,
-    )
-    weights, params, gains = [], [], []
-    lane = jnp.arange(128)[None, :]
+    x_rows = got["full"]
+    packed = [got["wfull"].reshape(width, packed_width)]
+    start = bc_width + heads
+    extra_all = packed[0][:, start : start + 2 * layers].astype(F32)
+    gains, params = [], []
+    per = bc_width // dp_count
     for l in range(layers):
-        wide = gather_dp(step_block[l])
-        gains.append(wide[:, heads].astype(F32)[None, :])
-        per = bc_width // dp_count
-        smalls = wide[:, heads + 1].reshape(dp_count, shard_rows)[:, : 5 * per]
-        smalls = smalls.astype(F32).reshape(dp_count, 5, per)
-        smalls = jnp.transpose(smalls, (1, 0, 2)).reshape(5, bc_width)
-        wdt = jnp.where(lane < heads, wide, jnp.zeros_like(wide))
-        weights.append(
-            (
-                gather_dp(proj_z[l]),
-                gather_dp(proj_x[l]),
-                gather_dp(proj_bc[l]),
-                wdt,
-                gather_dp(proj_out[l].T),
-            )
-        )
+        gains.append(extra_all[:, 2 * l][None, :])
+        smalls = extra_all[:, 2 * l + 1].reshape(dp_count, shard_rows)[:, : 5 * per]
+        smalls = jnp.transpose(smalls.reshape(dp_count, 5, per), (1, 0, 2)).reshape(5, bc_width)
         params.append(
             (
                 pad_to(rows_of(conv_value[l]), 8, inner),
@@ -481,74 +971,89 @@
         )
     pick = (jnp.arange(inner)[:, None] // WIDTH == jnp.arange(128)[None, :]).astype(BF)
 
-    residual = hidden_in.astype(F32)
-    kept = []
-    for l in range(layers):
-        r1 = lax.rsqrt(jnp.mean(residual * residual, axis=1, keepdims=True) + EPSILON)
-        normed = (residual * r1 * gains[l]).astype(BF)
-        rows = lax.all_gather(normed, "tensor", axis=0, tiled=True)
-        gate, val, st, dt, y, ent, mixed, part, ssq = forward_mix(rows, weights[l], params[l])
-        total = lax.psum_scatter(part, "tensor", scatter_dimension=0, tiled=True).astype(F32)
-        ssq_own = lax.psum_scatter(ssq[0], "tensor", scatter_dimension=0, tiled=True)
-        r2 = lax.rsqrt(ssq_own / inner_all + EPSILON)[:, None]
-        branch = total * r2
-        kept.append((residual, r1, rows, (gate, val, st, dt, y, ent), mixed, r2, branch))
-        residual = residual + branch
-    gradient = out_grad.astype(F32)
-    scattered = [None] * layers
-    summed = [None] * layers
+    out = forward_mix(x_rows, packed[0], params[0] + (gains[0],), True)
+    saved, rows = [out[:6]], [out[8]]
+    residuals, branches, r2s = [hidden_in], [], []
+    for l in range(layers - 1):
+        win, wout = weight_io(l + 1)
+        got = comm_call(
+            Step(
+                partial=True, gather=True, late=True, scale=inner_all, middle=forward_middle,
+                weights=column_chunks, **common,
+            ),
+            "between_forward", 2 + l,
+            dict(part=(out[6], vmem), ssq=(out[7], vmem), res=(residuals[l], vmem),
+                 gain=(gains[l + 1], vmem), **win),
+            dict(full=whole_rows, branch=own_rows, res_out=own_rows,
+                 r2=((rows_own, 128), F32, vmem), **wout),
+        )
+        rows.append(got["full"])
+        branches.append(got["branch"])
+        residuals.append(got["res_out"])
+        r2s.append(got["r2"])
+        packed.append(got["wfull"].reshape(width, packed_width))
+        out = forward_mix(rows[-1], packed[-1], params[l + 1] + (gains[l + 1],), False)
+        saved.append(out[:6])
+    got = comm_call(
+        Step(
+            partial=True, gather=True, scale=inner_all, inner=True, payload=scaled_payload,
+            middle=functools.partial(last_middle, inner_all), **common,
+        ),
+        "turn_around", 16,
+        dict(part=(out[6], vmem), ssq=(out[7], vmem), res=(residuals[-1], vmem),
+             grad_in=(out_grad, vmem)),
+        dict(full=whole_rows, res_out=own_rows, inner=((8, tokens), F32, vmem)),
+        r2=pltpu.VMEM((rows_own, 128), F32),
+    )
+    hidden_out = got["res_out"]
+    gradient = out_grad
+    scattered, summed = [None] * layers, [None] * layers
     for l in reversed(range(layers)):
-        residual_in, r1, rows, saved, mixed, r2, branch = kept[l]
-        gb = gradient.astype(BF)
-        e = r2[:, 0] ** 2 * jnp.sum(gb.astype(F32) * branch, axis=1) / inner_all
-        scaled = (r2 * gradient).astype(BF)
-        grad_rows = lax.all_gather(scaled, "tensor", axis=0, tiled=True)
-        e_rows = jnp.broadcast_to(
-            lax.all_gather(e, "tensor", axis=0, tiled=True)[None, :], (8, rows.shape[0])
-        )
-        dgate, dval, dst, ddt, dpart, gvec, gst, gdt = backward_mix(
-            grad_rows, e_rows, saved, weights[l], params[l], pick
-        )
-        dnormed = lax.psum_scatter(dpart, "tensor", scatter_dimension=0, tiled=True).astype(F32)
-        back = lambda left, right: jnp.einsum(
-            "td,tj->dj", left, right, preferred_element_type=F32
-        )
-        gain = gains[l]
-        dn = dnormed * gain
-        grad_gain = jnp.sum(residual_in * r1 * dnormed, axis=0)
-        cross = jnp.sum(dn * residual_in, axis=1, keepdims=True)
-        gradient = gradient + r1 * dn - r1**3 * residual_in * cross / width
-        scatter = lambda v: lax.psum_scatter(
-            v.astype(BF), "dp", scatter_dimension=0, tiled=True
-        ).astype(F32)
-        scattered[l] = (
-            scatter(back(rows, dgate)),
-            scatter(back(rows, dval)),
-            scatter(back(rows, dst)),
-            scatter(back(rows, ddt)),
-            scatter(back(grad_rows, mixed)),
-        )
-        summed[l] = (gvec, gdt, gst, grad_gain)
-    stack = lambda i: jnp.stack([scattered[l][i] for l in range(layers)])
-    gvec = jnp.stack([s[0] for s in summed])
-    gdt = jnp.stack([s[1] for s in summed])
-    gst = jnp.stack([s[2] for s in summed])
-    ggain = jnp.stack([s[3] for s in summed])
+        grad_rows = got["full"]
+        dcat, dpart, gvec, gst, gdt = backward_mix(
+            grad_rows, got["inner"], saved[l], packed[l], params[l], pick
+        )
+        more = l > 0
+        inputs = dict(
+            part=(dpart, vmem), res=(residuals[l], vmem), gain=(gains[l], vmem),
+            grad_in=(gradient, vmem), lrows=(rows[l], vmem), lgrad=(grad_rows, vmem),
+            right=(dcat, vmem),
+        )
+        outputs = dict(
+            grad_out=own_rows, ggain=((8, width), F32, vmem),
+            gout=((shard_rows, packed_width), F32, vmem),
+        )
+        if more:
+            inputs.update(r2=(r2s[l - 1], vmem), branch=(branches[l - 1], vmem))
+            outputs.update(full=whole_rows, inner=((8, tokens), F32, vmem))
+        got = comm_call(
+            Step(
+                partial=True, gather=more, late=more, inner=more, grads=column_chunks,
+                middle=functools.partial(backward_middle, inner_all if more else None), **common,
+            ),
+            "between_backward" if more else "last_backward", 17 + l, inputs, outputs,
+        )
+        gradient = got["grad_out"]
+        scattered[l] = got["gout"]
+        summed[l] = (gvec, gdt, gst, got["ggain"][0])
+    gout = jnp.stack(scattered)
+    gvec, gdt, gst, ggain = (jnp.stack([s[i] for s in summed]) for i in range(4))
     gvec, gdt = lax.psum((gvec, gdt), "dp")
-    gst, ggain, gbc = lax.psum((gst, ggain, stack(2).astype(BF)), "tensor")
-    gst, ggain = lax.psum((gst, ggain), "dp")
+    gst, ggain = lax.psum((gst, ggain), ("dp", "tensor"))
+    gbc = lax.psum(gout[:, :, :bc_width].astype(BF), "tensor").astype(F32)
     own = lambda v, axis: lax.dynamic_slice_in_dim(
         v, lax.axis_index("dp") * (v.shape[axis] // dp_count), v.shape[axis] // dp_count, axis
     )
     gst = own(gst, 2)
+    first = bc_width + 128
     return (
-        residual,
+        hidden_out,
         gradient,
         own(ggain, 1),
-        stack(0),
-        stack(1),
-        gbc.astype(F32),
-        stack(3)[:, :, :heads],
+        gout[:, :, first : first + inner],
+        gout[:, :, first + inner : first + 2 * inner],
+        gbc,
+        gout[:, :, bc_width : bc_width + heads],
         gvec[:, 0:4],
         gvec[:, 4],
         gst[:, 0:4],
@@ -557,7 +1062,7 @@
         gdt[:, 1, :heads],
         jnp.sum(gvec[:, 6].reshape(layers, heads, WIDTH), axis=2),
         gvec[:, 5],
-        jnp.transpose(stack(4), (0, 2, 1)),
+        jnp.transpose(gout[:, :, first + 2 * inner :], (0, 2, 1)),
     )
 
 

time: 1360 us -> 730 us (0.54)
  waiting for transfers between devices: 986 us -> 0.02 us
  Pallas kernels: 132 us -> 606 us
  matrix products: 50.4 us -> 0 us
  blocking collectives: 103 us -> 61.1 us
  other arithmetic: 33.9 us -> 13.7 us
    reduce_scatter x14 -> x0, waiting for transfers between devices: 537 us -> none  [the longest x10 323 us: shards(): lax.psum_scatter(v.astype(BF), 'dp', scatter_dimension=0, tiled=True)]
    pallas_call x2 -> x7, Pallas kernels: 52.5 us -> 527 us  [the longest x5 473 us: comm_call(): pl.pallas_call(functools.partial(comm_kernel, o, names), in_specs=[pl.Blo...]
    all_gather x10 -> x0, waiting for transfers between devices: 362 us -> none  [the longest x2 131 us: shards(): rows = lax.all_gather(normed, 'tensor', axis=0, tiled=True)]
    psum x2 -> x1, waiting for transfers between devices: 84.4 us -> 0.01 us  [shards(): gbc = lax.psum(gout[:, :, :bc_width].astype(BF), 'tensor').astype(F32)]
    all_gather x6 -> x0, blocking collectives: 66.3 us -> none  [the longest x4 46.7 us: gather_dp(): return lax.all_gather(v, 'dp', axis=axis, tiled=True)]
    dot_general x10 -> x0, matrix products: 50.4 us -> none  [shards(): jnp.einsum('td,tj->dj', left, right, preferred_element_type=F32)]
    psum x1 -> x2, blocking collectives: 18.3 us -> 61.1 us  [the longest x1 38.1 us: shards(): gst, ggain = lax.psum((gst, ggain), ('dp', 'tensor'))]
    unnamed x2 -> x0, blocking collectives: 18.6 us -> none
  transfers between devices with their start and end apart: 26 -> 1, of which waited for: 23 -> 0; matrix products, arithmetic and copies ran while one was open for 6% -> 2% of each run, Pallas kernels for 3% -> 0%
where the time goes in v2:
time: 730 us; the launch traced here: 723 us
  Pallas kernels  606 us (83%)
  blocking collectives  61.1 us (8%)
  local copies, waits for them, and re-layouts  26.5 us (4%)
  between operations  14.9 us (2%)
  other arithmetic  13.7 us (2%)
    pallas_call x5, Pallas kernels, comm_call(): pl.pallas_call(functools.partial(comm_kernel, o, names), in_specs=[pl.Blo...  473 us
    pallas_call x2, Pallas kernels, backward_mix(): pl.pallas_call(bwd_kernel, grid=(blocks,), in_specs=[tok(width), pl.Block...  79.8 us
    pallas_call x2, Pallas kernels, forward_mix(): pl.pallas_call(functools.partial(fwd_kernel, first), grid=(blocks,), in_s...  53.3 us
    psum x1, blocking collectives, shards(): gst, ggain = lax.psum((gst, ggain), ('dp', 'tensor'))  38.1 us
    psum x1, blocking collectives, shards(): gvec, gdt = lax.psum((gvec, gdt), 'dp')  22.9 us
  transfers between devices with their start and end apart: 1, of which 0 were waited for; matrix products, arithmetic and copies ran while one was open for 2% of the time, Pallas kernels for 0%

profile of v2, /device:TPU:0, one launch (start us, length us, event | category | flops | bytes accessed | tf_op | source)
XLA Modules:
  0.0 722.6 jit_solution(12866582132718373852)
XLA Ops:
  7.2 1.0 slice_bitcast_fusion.6
  8.3 0.8 fusion.15
  9.2 0.8 reshape.123
  10.0 0.7 fusion.13
  10.7 0.7 pad_maximum_fusion.5
  11.5 1.1 slice_bitcast_fusion
  12.8 1.7 concatenate.10.refs_1_
  14.5 91.3 %gather_first.1 = (bf16[1024,1536]{1,0:T(8,128)(2,1)}, bf16[2,2,2,192,2688]{4,3,2,1,0:T(8,128)(2,1)}) custom-call(bf16[256,1536]{1,0:T(8,128)(2,1)} %refs_1_.1, bf16[192,2688]{1,0:T(8,128)(2,1)} %concatenate.10.refs_1_), custom_call_target="tpu_custom_call" | custom-call | tf_op jit(solution)/shard_map/gather_first/pallas_call | solution.py:813
  105.9 1.2 slice_convert_fusion
  107.1 1.5 slice_reduce_fusion
  115.5 0.8 fusion.5.pick_ref
  118.1 1.7 concatenate.11.refs_4_
  119.8 27.0 %mix_forward.2 = (f32[1024,768]{1,0:T(8,128)}, f32[1024,768]{1,0:T(8,128)}, f32[1024,256]{1,0:T(8,128)}, f32[1024,128]{1,0:T(8,128)}, f32[1024,768]{1,0:T(8,128)...) custom-call(bf16[1024,1536]{1,0:T(8,128)(2,1)} %get-tuple-element.61.row, ...), custom_call_target="tpu_custom_call" | custom-call | tf_op jit(solution)/shard_map/mix_forward/pallas_call | solution.py:192
  146.7 115.8 %between_forward.1 = (bf16[1024,1536]{1,0:T(8,128)(2,1)}, f32[256,1536]{1,0:T(8,128)}, f32[256,1536]{1,0:T(8,128)}, f32[256,128]{1,0:T(8,128)}, bf16[2,2,2,192,2688]{4,3,2,1,0:T(8,128)(2,1)}) custom-call(bf16[1024,1536]{1,0:T(8,128)(2,1)} %get-tuple-element.63.refs_0_, f32[8,1024]{1,0:T(8,128)} %get-tuple-element.64.refs_1_, bf16[256,1536]{1,0:T(8,128)(2,1)} %refs_1_.1, ...), custom_call_target="tpu_custom_call" | custom-call | tf_op jit(solution)/shard_map/between_forward/pallas_call | solution.py:813
  262.6 26.3 %mix_forward.3 = (f32[1024,768]{1,0:T(8,128)}, f32[1024,768]{1,0:T(8,128)}, f32[1024,256]{1,0:T(8,128)}, f32[1024,128]{1,0:T(8,128)}, f32[1024,768]{1,0:T(8,128)...) custom-call(bf16[1024,1536]{1,0:T(8,128)(2,1)} %get-tuple-element.65.rows_ref.refs_4_, ...), custom_call_target="tpu_custom_call" | custom-call | tf_op jit(solution)/shard_map/mix_forward/pallas_call | solution.py:192
  288.9 88.2 %turn_around.1 = (bf16[1024,1536]{1,0:T(8,128)(2,1)}, f32[256,1536]{1,0:T(8,128)}, f32[8,1024]{1,0:T(8,128)}) custom-call(bf16[1024,1536]{1,0:T(8,128)(2,1)} %get-tuple-element.67.refs_0_, f32[8,1024]{1,0:T(8,128)} %get-tuple-element.68.refs_1_, f32[256,1536]{1,0:T(8,128)} %get-tuple-element.69.refs_2_.refs_1_, bf16[256,1536]{1,0:T(8,128)(2,1)} %refs_3_.3), custom_call_target="tpu_custom_call" | custom-call | tf_op jit(solution)/shard_map/turn_around/pallas_call | solution.py:813
  377.1 39.9 %mix_backward.2 = (bf16[1024,2688]{1,0:T(8,128)(2,1)}, bf16[1024,1536]{1,0:T(8,128)(2,1)}, f32[8,768]{1,0:T(8,128)}, f32[8,256]{1,0:T(8,128)}, f32[8,128]{1,0:T(8,128)}) custom-call(bf16[1024,1536]{1,0:T(8,128)(2,1)} %get-tuple-element.71.gb_ref.refs_5_, f32[8,1024]{1,0:T(8,128)} %get-tuple-element.72.e_ref, f32[1024,768]{1,0:T(8,128)} %get-tuple-element.73.gate_ref, ...), custom_call_target="tpu_custom_call" | custom-call | tf_op jit(solution)/shard_map/mix_backward/pallas_call | solution.py:388
  417.0 103.8 %between_backward.1 = (f32[256,1536]{1,0:T(8,128)}, f32[8,1536]{1,0:T(8,128)}, f32[192,2688]{1,0:T(8,128)}, bf16[1024,1536]{1,0:T(8,128)(2,1)}, f32[8,1024]{1,0:T(8,128)}) custom-call(bf16[1024,1536]{1,0:T(8,128)(2,1)} %get-tuple-element.79.refs_0_, f32[256,1536]{1,0:T(8,128)} %get-tuple-element.69.refs_2_.refs_1_, ...), custom_call_target="tpu_custom_call" | custom-call | tf_op jit(solution)/shard_map/between_backward/pallas_call | solution.py:813
  520.8 40.0 %mix_backward.3 = (bf16[1024,2688]{1,0:T(8,128)(2,1)}, bf16[1024,1536]{1,0:T(8,128)(2,1)}, f32[8,768]{1,0:T(8,128)}, f32[8,256]{1,0:T(8,128)}, f32[8,128]{1,0:T(8,128)}) custom-call(bf16[1024,1536]{1,0:T(8,128)(2,1)} %get-tuple-element.83.gb_ref.refs_5_, f32[8,1024]{1,0:T(8,128)} %get-tuple-element.84.e_ref, f32[1024,768]{1,0:T(8,128)} %get-tuple-element.85.gate_ref, ...), custom_call_target="tpu_custom_call" | custom-call | tf_op jit(solution)/shard_map/mix_backward/pallas_call | solution.py:388
  560.8 74.1 %last_backward.1 = (f32[256,1536]{1,0:T(8,128)}, f32[8,1536]{1,0:T(8,128)}, f32[192,2688]{1,0:T(8,128)}) custom-call(bf16[1024,1536]{1,0:T(8,128)(2,1)} %get-tuple-element.91.refs_0_, bf16[256,1536]{1,0:T(8,128)(2,1)} %refs_1_.1, f32[1,1536]{1,0:T(1,128)} %broadcast_in_dim_squeeze.6.gain_ref.refs_2_, f32[256,1536]{1,0:T(8,128)} %get-tuple-element.92.refs_3_, ...), custom_call_target="tpu_custom_call" | custom-call | tf_op jit(solution)/shard_map/last_backward/pallas_call | solution.py:813
  634.9 1.9 fusion.4
  636.9 0.9 fusion.6
  637.9 22.9 %all-reduce.10 = (f32[2,8,768]{2,1,0:T(8,128)S(1)}, f32[2,8,128]{2,1,0:T(8,128)S(1)}) all-reduce(f32[2,8,768]{2,1,0:T(8,128)S(1)} %pad_maximum_fusion.1, f32[2,8,128]{2,1,0:T(8,128)S(1)} %pad_maximum_fusion.4), channel_id=1, replica_groups=mesh['dp'=8,'tensor'=4] {'dp'}, use_global_device_ids=true, to_apply=%region_2.3 | all-reduce | flops 14336 | bytes 114688 | tf_op jit(solution)/shard_map/psum | solution.py:1041
  661.5 0.8 slice.195
  662.3 0.8 slice.194
  663.1 0.7 copy.43
  664.4 38.1 %all-reduce.9 = (f32[2,1536]{1,0:T(2,128)S(1)}, f32[2,8,256]{2,1,0:T(8,128)S(1)}) all-reduce(f32[2,1536]{1,0:T(2,128)S(1)} %pad_maximum_fusion.3, f32[2,8,256]{2,1,0:T(8,128)S(1)} %pad_maximum_fusion.2), channel_id=1, replica_groups=mesh['dp'=8,'tensor'=4] {'dp','tensor'}, use_global_device_ids=true, to_apply=%region_0.1 | all-reduce | flops 7168 | bytes 57344 | tf_op jit(solution)/shard_map/psum | solution.py:1042
  702.6 0.7 constant_dynamic-slice_fusion
  706.4 3.3 fusion.2
  709.7 1.8 convert_element_type.87
  711.5 2.7 copy.55
  714.2 1.1 copy.56
  (87 shorter events, 13.6 us)
Async XLA Ops:
  7.2 5.5 copy-start.2
  7.2 5.5 copy-start.3
  7.2 702.5 %all-reduce.13.cloned.1.call-start = ((), (), s32[]{:S(2)}) async-start(), calls=%async_computation | async-start | bytes 393216 | tf_op jit(solution)/shard_map/psum | solution.py:1043
  105.8 3.1 copy-start.6
  105.8 3.9 copy-start.13
  105.8 3.9 copy-start.14
  105.8 5.0 copy-start.15
  107.0 9.9 %copy-start.7 = (bf16[2,768]{1,0:T(2,128)(2,1)S(1)}, bf16[2,768]{1,0:T(2,128)(2,1)}, u32[]{:S(2)}) copy-start(bf16[2,768]{1,0:T(2,128)(2,1)} %param.30) | copy-start | bytes 9220
  107.1 9.9 %copy-start.8 = (bf16[2,768]{1,0:T(2,128)(2,1)S(1)}, bf16[2,768]{1,0:T(2,128)(2,1)}, u32[]{:S(2)}) copy-start(bf16[2,768]{1,0:T(2,128)(2,1)} %param.24) | copy-start | bytes 9220
  634.9 1.9 copy-start
  636.8 1.0 copy-start.4
  636.8 1.0 copy-start.5
  636.8 1.0 copy-start.11
  636.8 1.0 copy-start.12
  636.8 27.6 %copy-start.9 = (f32[8,256]{1,0:T(8,128)S(1)}, f32[8,256]{1,0:T(8,128)}, u32[]{:S(2)}) copy-start(f32[8,256]{1,0:T(8,128)} %get-tuple-element.103) | copy-start | bytes 24580
  636.8 27.6 %copy-start.10 = (f32[8,256]{1,0:T(8,128)S(1)}, f32[8,256]{1,0:T(8,128)}, u32[]{:S(2)}) copy-start(f32[8,256]{1,0:T(8,128)} %get-tuple-element.102) | copy-start | bytes 24580
  709.7 4.5 copy-start.1
Sparse Core Ops, SparseCore 0:
  636.9 33.9 all-reduce.12

commit v3 on v2

--- a/solution.py
+++ b/solution.py
@@ -77,9 +77,16 @@
     return [w_ref.at[:, pl.ds(s, z)] for s, z in zip(starts, sizes)]
 
 
+def small_refs(vec_ref, cst_ref, tiny_ref):
+    vec, cst, tiny = vec_ref.at[0], cst_ref.at[0], tiny_ref.at[0]
+    return (
+        vec.at[0:4], vec.at[4:5], vec.at[5:6], vec.at[6:7],
+        cst.at[0:4], cst.at[4:5], tiny.at[0:1], tiny.at[1:2],
+    )
+
+
 def fwd_kernel(
-    first, rows_ref, w_ref,
-    cv_ref, cvb_ref, cs_ref, csb_ref, sb_ref, rate_ref, skip_ref, gg_ref, gain_ref,
+    first, rows_ref, w_ref, vec_ref, cst_ref, tiny_ref, gain_ref,
     gate_ref, val_ref, st_ref, dt_ref, y_ref, ent_ref, part_ref, ssq_ref,
     *rest,
 ):
@@ -87,6 +94,9 @@
     state, vpad, spad = rest[-3:]
     step = pl.program_id(0)
     length = rows_ref.shape[0]
+    cv_ref, cvb_ref, skip_ref, gg_ref, cs_ref, csb_ref, sb_ref, rate_ref = small_refs(
+        vec_ref, cst_ref, tiny_ref
+    )
     inner = gg_ref.shape[1]
     pairs = inner // 128
     wbc_ref, wdt_ref, wz_ref, wx_ref, wot_ref = blocks_of(w_ref, inner, cs_ref.shape[1])
@@ -106,7 +116,7 @@
     if first:
         rows = rows.astype(F32)
         r1 = lax.rsqrt(jnp.mean(rows * rows, axis=1, keepdims=True) + EPSILON)
-        rows = (rows * r1 * gain_ref[...]).astype(BF)
+        rows = (rows * r1 * gain_ref[0]).astype(BF)
         normed_ref[...] = rows
     gate_ref[...] = nn(rows, wz_ref[...])
     val = nn(rows, wx_ref[...])
@@ -168,10 +178,18 @@
     return pl.BlockSpec(shape, lambda i: (0,) * len(shape), pipeline_mode=pl.Buffered(1))
 
 
-def forward_mix(rows, packed, params, first):
+def layer_specs(params, l):
+    return [
+        pl.BlockSpec((1,) + p.shape[1:], lambda i: (l, 0, 0), pipeline_mode=pl.Buffered(1))
+        for p in params
+    ]
+
+
+def forward_mix(rows, packed, params, l):
+    first = l == 0
     tokens, width = rows.shape
-    inner = params[0].shape[1]
-    bc_width = params[2].shape[1]
+    inner = params[0].shape[2]
+    bc_width = params[1].shape[2]
     dt_width = 128
     half = bc_width // 2
     q = GROUP
@@ -192,7 +210,7 @@
     return pl.pallas_call(
         functools.partial(fwd_kernel, first),
         grid=(blocks,),
-        in_specs=[tok(width)] + [whole(w.shape) for w in (packed, *params)],
+        in_specs=[tok(width), whole(packed.shape)] + layer_specs(params, l),
         out_specs=[o[2] for o in outs],
         out_shape=[jax.ShapeDtypeStruct(o[0], o[1]) for o in outs],
         scratch_shapes=[
@@ -209,14 +227,16 @@
 
 def bwd_kernel(
     gb_ref, e_ref, gate_ref, val_ref, valp_ref, st_ref, stp_ref, dt_ref, y_ref, ent_ref,
-    w_ref,
-    cv_ref, cvb_ref, cs_ref, csb_ref, sb_ref, rate_ref, skip_ref, gg_ref, pick_ref,
+    w_ref, vec_ref, cst_ref, tiny_ref, pick_ref,
     dcat_ref, dpart_ref, gvec_ref, gst_ref, gdt_ref,
     dstate, vpad, spad, dvpad, dspad,
 ):
     step = pl.program_id(0)
     blocks = pl.num_programs(0)
     length = gb_ref.shape[0]
+    cv_ref, cvb_ref, skip_ref, gg_ref, cs_ref, csb_ref, sb_ref, rate_ref = small_refs(
+        vec_ref, cst_ref, tiny_ref
+    )
     inner = gg_ref.shape[1]
     bc_width = cs_ref.shape[1]
     wbc_ref, wdt_ref, wz_ref, wx_ref, wot_ref = blocks_of(w_ref, inner, bc_width)
@@ -269,10 +289,11 @@
     gate = gate_ref[...]
     sig_g, sgate = silu_parts(gate)
     gated = y * sgate
-    dm = nn(gb_ref[...], wot_ref[...])
-    e = e_ref[...].T[:, 0:1]
+    per_token = e_ref[...].T
+    e, r2 = per_token[:, 0:1], per_token[:, 1:2]
+    dm = nn(gb_ref[...], wot_ref[...]) * r2
     dgated = dm * gg_ref[...] - e * gated
-    mixed_ref[...] = (gated * gg_ref[...]).astype(BF)
+    mixed_ref[...] = (gated * r2 * gg_ref[...]).astype(BF)
     dgate = (dgated * y * (sig_g * (1.0 + gate * (1.0 - sig_g)))).astype(BF)
     dgate_ref[...] = dgate
     dy = dgated * sgate
@@ -362,11 +383,11 @@
     dpart_ref[...] = dpart.astype(BF)
 
 
-def backward_mix(gb, e_rows, kept, packed, params, pick):
+def backward_mix(gb, e_rows, kept, packed, params, pick, l):
     gate, val, st, dt, y, ent = kept
     tokens, width = gb.shape
-    inner = params[0].shape[1]
-    bc_width = params[2].shape[1]
+    inner = params[0].shape[2]
+    bc_width = params[1].shape[2]
     dt_width = 128
     packed_width = packed.shape[1]
     half = bc_width // 2
@@ -395,7 +416,7 @@
             tok(inner),
             pl.BlockSpec((1, half, inner), lambda i: (back(i), 0, 0)),
         ]
-        + [whole(w.shape) for w in (packed, *params, pick)],
+        + [whole(packed.shape)] + layer_specs(params, l) + [whole(pick.shape)],
         out_specs=[o[2] for o in outs],
         out_shape=[jax.ShapeDtypeStruct(o[0], o[1]) for o in outs],
         scratch_shapes=[
@@ -418,6 +439,8 @@
         self.width = 0
         self.line = 4
         self.chunks = 8
+        self.hop = 1
+        self.slack = 0
         self.partial = False
         self.gather = False
         self.late = False
@@ -425,6 +448,8 @@
         self.inner = False
         self.weights = 0
         self.grads = 0
+        self.states = 0
+        self.sums = False
         self.bits = 0
         self.middle = None
         self.__dict__.update(given)
@@ -458,6 +483,9 @@
             device_id_type=pl.DeviceIdType.MESH,
         )
     over_dp = o.weights or o.grads
+    r.early = [v for k, v in zip(names, refs) if k.startswith("esum")]
+    r.lined = [v for k, v in zip(names, refs) if k.startswith("lsum")]
+    r.gains = [v for k, v in zip(names, refs) if k.startswith("gsum")]
     if over_dp:
         for b in range(o.bits):
             pl.semaphore_signal(
@@ -521,8 +549,8 @@
         order = range(n - 2, -1, -1) if side == 0 else range(1, n)
         for s in order:
             away = t - s if side == 0 else s - t
-            late = max(s, n - 1 - s) if o.late else 0
-            c = tau - late - away
+            late = o.hop * max(s, n - 1 - s) + o.slack if o.late else 0
+            c = tau - late - o.hop * away
 
             @when((away > 0) & (c >= 0) & (c < count))
             def _():
@@ -569,8 +597,10 @@
 
     def weight_copy(parity, stage, j):
         order = bit_order(parity)
-        spot = r.wfull.at[(*spots(order[:stage]), slice(None), cols(j))]
-        src = r.wown.at[:, cols(j)] if stage == 0 else spot
+        depth = r.wown.shape[0] // o.weights
+        strip = pl.ds(pl.multiple_of(j * depth, depth), depth)
+        spot = r.wfull.at[(*spots(order[:stage]), strip)]
+        src = r.wown.at[strip] if stage == 0 else spot
         return remote(
             src, spot, r.wg_send.at[stage, j], r.wg_recv.at[stage, j],
             {"dp": partner[order[stage]]},
@@ -579,9 +609,11 @@
     def own_weights():
         return pltpu.make_async_copy(r.wown, r.wfull.at[spots([])], r.wl_sem)
 
-    def each_parity(j, fn):
+    def each_parity(pair, fn):
         for parity in range(2):
-            @when((j >= 0) & (j < max(o.weights, o.grads)) & (lax.rem(j, 2) == parity))
+            j = 2 * pair + parity
+
+            @when((j >= 0) & (j < max(o.weights, o.grads)))
             def _():
                 fn(parity, j)
 
@@ -659,6 +691,99 @@
                     grad_copy(parity, stage, j).start()
             each_parity(tau - stage, run)
 
+    def share(buf, send, recv, k):
+        return remote(buf.at[t], buf.at[t], send.at[k - 1], recv.at[k - 1],
+                      {"tensor": lax.rem(t + k, n)})
+
+    def shared(buf, send, recv):
+        for k in range(1, n):
+            source = lax.rem(t + n - k, n)
+            remote(buf.at[source], buf.at[source], send.at[k - 1], recv.at[k - 1],
+                   {"tensor": source}).wait_recv()
+
+    def line_total(buf):
+        total = buf[0]
+        for k in range(1, n):
+            total = total + buf[k]
+        return total
+
+    def double(acc, buf, send, recv, b):
+        return remote(acc.at[b], buf.at[b], send.at[b], recv.at[b], {"dp": partner[b]})
+
+    def doubled(acc, buf, send, recv, b):
+        double(acc, buf, send, recv, b).wait_recv()
+        acc[b + 1] = acc[b] + buf[b]
+
+    def lanes(index, ref):
+        return slice(index * ref.shape[1], (index + 1) * ref.shape[1])
+
+    line_groups, dp_groups = [], []
+    if o.sums:
+        line_groups = [(r.lbank, r.lb_send, r.lb_recv)]
+        dp_groups = [(r.dbank, r.dbuf, r.db_send, r.db_recv)]
+        if r.gains:
+            line_groups.append((r.gbank, r.gb_send, r.gb_recv))
+            dp_groups.append((r.hbank, r.hbuf, r.hb_send, r.hb_recv))
+
+    def sum_items(tau):
+        @when(tau == 2)
+        def _():
+            for g in line_groups:
+                shared(*g)
+            off = 0
+            for v in r.early:
+                r.dbank[0, :, off : off + v.shape[1]] = v[...]
+                off += v.shape[1]
+            r.dbank[0, :, off:] = line_total(r.lbank)
+            if r.gains:
+                r.hbank[0] = line_total(r.gbank)
+            for g in dp_groups:
+                double(*g, 0).start()
+
+        for b in range(o.bits):
+            @when(tau == 4 + b)
+            def _():
+                for g in dp_groups:
+                    doubled(*g, b)
+                    if b < o.bits - 1:
+                        double(*g, b + 1).start()
+
+    def state_items(tau):
+        at_first = o.bits + 1
+        quarter = r.gout.shape[0] // n
+
+        @when(tau == at_first)
+        def _():
+            for s in range(n):
+                r.qsend[s] = r.gout[s * quarter : (s + 1) * quarter, 0 : o.states].astype(BF)
+            for k in range(1, n):
+                state_out(k).start()
+
+        @when(tau == at_first + 2)
+        def _():
+            total = r.qsend[t].astype(F32)
+            for k in range(1, n):
+                state_out(k).wait_recv()
+                total = total + r.qbuf[k - 1].astype(F32)
+            r.qall[t] = total.astype(BF)
+            for k in range(1, n):
+                share(r.qall, r.qa_send, r.qa_recv, k).start()
+
+    def state_out(k):
+        dest = lax.rem(t + k, n)
+        return remote(r.qsend.at[dest], r.qbuf.at[k - 1], r.qs_send.at[k - 1],
+                      r.qs_recv.at[k - 1], {"tensor": dest})
+
+    if o.sums:
+        off = 0
+        for v in r.lined:
+            r.lbank[t, :, off : off + v.shape[1]] = v[...]
+            off += v.shape[1]
+        for i, v in enumerate(r.gains):
+            r.gbank[t, :, lanes(i, v)] = v[0:1, :]
+        for g in line_groups:
+            for k in range(1, n):
+                share(*g, k).start()
     if o.scale:
         for k in range(1, n):
             square_copy(k).start()
@@ -683,22 +808,26 @@
     if o.middle is not None:
         o.middle(r, None, None)
 
-    ends = [count + (n - 1)]
+    ends = [count + o.hop * (n - 1) + o.slack]
     if o.late:
-        ends.append(count + 2 * (n - 1))
+        ends.append(ends[0] + o.hop * (n - 1))
     if over_dp:
-        ends.append(max(o.weights, o.grads) + o.bits)
+        ends.append((max(o.weights, o.grads) + 1) // 2 + o.bits)
+    if o.grads:
+        ends.append(o.bits + 4)
+    if o.sums:
+        ends.append(4 + o.bits)
 
     def iteration(tau, _):
         if o.partial:
             for side in range(2):
-                c = tau - (t if side == 0 else n - 1 - t)
+                c = tau - o.hop * (t if side == 0 else n - 1 - t)
 
                 @when((c >= 0) & (c < count))
                 def _():
                     reduce_items(side, c)
 
-            c_own = tau - jnp.maximum(t, n - 1 - t)
+            c_own = tau - o.hop * jnp.maximum(t, n - 1 - t) - o.slack
 
             @when((c_own >= 0) & (c_own < count))
             def _():
@@ -707,7 +836,7 @@
                 if o.late:
                     r.full[at(t, c_own), :] = out
         if o.gather:
-            c_out = tau - jnp.maximum(t, n - 1 - t) if o.late else tau
+            c_out = tau - o.hop * jnp.maximum(t, n - 1 - t) - o.slack if o.late else tau
 
             @when((c_out >= 0) & (c_out < count))
             def _():
@@ -728,10 +857,17 @@
             weight_items(tau)
         if o.grads:
             grad_items(tau)
+            state_items(tau)
+        if o.sums:
+            sum_items(tau)
         return 0
 
     lax.fori_loop(0, max(ends), iteration, 0)
 
+    if o.sums:
+        r.jbank[t] = r.ggain[0:1, :]
+        for k in range(1, n):
+            share(r.jbank, r.jb_send, r.jb_recv, k).start()
     if o.inner:
         spot_of(t, r.inner)[...] = r.icol[...].T[0:8, :]
         for k in range(1, n):
@@ -740,6 +876,31 @@
             inner_arrival(k).wait_recv()
         for k in range(1, n):
             inner_copy(k).wait_send()
+    if o.sums:
+        last = (r.kbank, r.kbuf, r.kb_send, r.kb_recv)
+        shared(r.jbank, r.jb_send, r.jb_recv)
+        r.kbank[0] = line_total(r.jbank)
+        for b in range(o.bits):
+            double(*last, b).start()
+            doubled(*last, b)
+        r.sums[...] = r.dbank[o.bits]
+        r.gain_sums[0:1, :] = r.kbank[o.bits]
+        for i, v in enumerate(r.gains):
+            r.gain_sums[i + 1 : i + 2, :] = r.hbank[o.bits, :, lanes(i, v)]
+        for g in line_groups + [(r.jbank, r.jb_send, r.jb_recv)]:
+            for k in range(1, n):
+                share(*g, k).wait_send()
+        for g in dp_groups + [last]:
+            for b in range(o.bits):
+                double(*g, b).wait_send()
+    if o.grads:
+        shared(r.qall, r.qa_send, r.qa_recv)
+        quarter = r.gout.shape[0] // n
+        for s in range(n):
+            r.gout[s * quarter : (s + 1) * quarter, 0 : o.states] = r.qall[s].astype(F32)
+        for k in range(1, n):
+            state_out(k).wait_send()
+            share(r.qall, r.qa_send, r.qa_recv, k).wait_send()
     if o.scale:
         for k in range(1, n):
             square_copy(k).wait_send()
@@ -809,6 +970,29 @@
             scratch["gbuf%d" % stage] = pltpu.VMEM(
                 (o.grads, *(2,) * (o.bits - 1 - stage), depth, WCHUNK), BF
             )
+        part = (n, (width >> o.bits) // n, o.states)
+        scratch.update(
+            qsend=pltpu.VMEM(part, BF), qall=pltpu.VMEM(part, BF),
+            qbuf=pltpu.VMEM((n - 1,) + part[1:], BF),
+            qs_send=dma((n - 1,)), qs_recv=dma((n - 1,)),
+            qa_send=dma((n - 1,)), qa_recv=dma((n - 1,)),
+        )
+    if o.sums:
+        def lanes_of(start):
+            return sum(v[0].shape[1] for k, v in inputs.items() if k.startswith(start))
+
+        lined, early, gains = lanes_of("lsum"), lanes_of("esum"), lanes_of("gsum")
+        for name_of, tall, line_width, dp_width in (
+            ("lb db", 8, lined, lined + early), ("gb hb", 1, gains, gains), ("jb kb", 1, width, width)
+        ):
+            if line_width:
+                one, two = name_of.split()
+                scratch[one + "ank"] = pltpu.VMEM((n, tall, line_width), F32)
+                scratch[two + "ank"] = pltpu.VMEM((o.bits + 1, tall, dp_width), F32)
+                scratch[two + "uf"] = pltpu.VMEM((o.bits, tall, dp_width), F32)
+                for key, size in ((one, n - 1), (two, o.bits)):
+                    scratch[key + "_send"] = dma((size,))
+                    scratch[key + "_recv"] = dma((size,))
     names = [*inputs, *outputs, *scratch]
     out = pl.pallas_call(
         functools.partial(comm_kernel, o, names),
@@ -828,8 +1012,9 @@
     return r.own[...]
 
 
-def scaled_payload(r):
-    return (r.r2[:, 0:1] * r.grad_in[...].astype(F32)).astype(BF)
+def token_columns(first, second):
+    lane = lax.broadcasted_iota(jnp.int32, (first.shape[0], 128), 1)
+    return jnp.where(lane == 0, first, second)
 
 
 def forward_middle(r, at, total):
@@ -850,7 +1035,7 @@
     branch = total * r2
     r.res_out[at, :] = r.res[at, :].astype(F32) + branch
     dot = jnp.sum(r.grad_in[at, :].astype(F32) * branch, axis=1, keepdims=True)
-    r.icol[at, :] = jnp.broadcast_to(r2 * r2 * dot / inner_all, (dot.shape[0], 128))
+    r.icol[at, :] = token_columns(r2 * r2 * dot / inner_all, r2)
     return None
 
 
@@ -871,8 +1056,8 @@
         return None
     r2 = r.r2[at, 0:1]
     dot = jnp.sum(grad.astype(BF).astype(F32) * r.branch[at, :], axis=1, keepdims=True)
-    r.icol[at, :] = jnp.broadcast_to(r2 * r2 * dot / inner_all, (dot.shape[0], 128))
-    return (r2 * grad).astype(BF)
+    r.icol[at, :] = token_columns(r2 * r2 * dot / inner_all, r2)
+    return grad.astype(BF)
 
 
 def pad_to(v, rows, columns):
@@ -911,7 +1096,7 @@
     bc_width = proj_bc.shape[2]
     inner_all = inner * tensor_count
     packed_width = bc_width + 128 + 3 * inner
-    column_chunks = packed_width // WCHUNK
+    column_chunks, row_chunks = packed_width // WCHUNK, shard_rows // 16
     vmem, far = pltpu.VMEM, pl.ANY
 
     small = jnp.concatenate([conv_state.reshape(layers, -1), conv_state_bias], axis=1)
@@ -937,41 +1122,43 @@
     common = dict(rows=rows_own, width=width, line=tensor_count, bits=bits)
 
     def weight_io(l):
-        return dict(wown=(packs[l], far)), dict(wfull=(full_shape, BF, far))
+        return dict(wown=(packs[l], vmem)), dict(wfull=(full_shape, BF, far))
+
+    vec = jnp.concatenate(
+        [
+            conv_value,
+            conv_value_bias[:, None],
+            jnp.repeat(skip_gain, WIDTH, axis=1)[:, None],
+            gate_gain[:, None],
+        ],
+        axis=1,
+    ).astype(F32)
+    tiny = jnp.stack([step_bias.astype(F32), -jnp.exp(log_decay.astype(F32))], axis=1)
+    tiny = jnp.pad(tiny, ((0, 0), (0, 0), (0, 128 - heads)))
+    pick = (jnp.arange(inner)[:, None] // WIDTH == jnp.arange(128)[None, :]).astype(BF)
 
     whole_rows, own_rows = ((tokens, width), BF, vmem), ((rows_own, width), F32, vmem)
     win, wout = weight_io(0)
     got = comm_call(
-        Step(gather=True, payload=plain_payload, weights=column_chunks, **common),
+        Step(gather=True, payload=plain_payload, weights=row_chunks, **common),
         "gather_first", 1,
         dict(own=(hidden_in, vmem), **win),
         dict(full=whole_rows, **wout),
     )
     x_rows = got["full"]
+    out_grad, x_rows = lax.optimization_barrier((out_grad, x_rows))
+    grad_rows = lax.all_gather(out_grad, "tensor", axis=0, tiled=True)
     packed = [got["wfull"].reshape(width, packed_width)]
     start = bc_width + heads
     extra_all = packed[0][:, start : start + 2 * layers].astype(F32)
-    gains, params = [], []
+    gain_rows = extra_all[:, 0 : 2 * layers : 2].T[:, None, :]
     per = bc_width // dp_count
-    for l in range(layers):
-        gains.append(extra_all[:, 2 * l][None, :])
-        smalls = extra_all[:, 2 * l + 1].reshape(dp_count, shard_rows)[:, : 5 * per]
-        smalls = jnp.transpose(smalls.reshape(dp_count, 5, per), (1, 0, 2)).reshape(5, bc_width)
-        params.append(
-            (
-                pad_to(rows_of(conv_value[l]), 8, inner),
-                rows_of(conv_value_bias[l]),
-                pad_to(smalls[:4], 8, bc_width),
-                smalls[4:5],
-                pad_to(rows_of(step_bias[l]), 1, 128),
-                pad_to(-jnp.exp(rows_of(log_decay[l])), 1, 128),
-                jnp.repeat(rows_of(skip_gain[l]), WIDTH, axis=1),
-                rows_of(gate_gain[l]),
-            )
-        )
-    pick = (jnp.arange(inner)[:, None] // WIDTH == jnp.arange(128)[None, :]).astype(BF)
-
-    out = forward_mix(x_rows, packed[0], params[0] + (gains[0],), True)
+    smalls = extra_all[:, 1 : 2 * layers : 2].reshape(dp_count, shard_rows, layers)
+    smalls = smalls[:, : 5 * per].reshape(dp_count, 5, per, layers)
+    cst = jnp.transpose(smalls, (3, 1, 0, 2)).reshape(layers, 5, bc_width)
+    params = (vec, cst, tiny)
+
+    out = forward_mix(x_rows, packed[0], params + (gain_rows,), 0)
     saved, rows = [out[:6]], [out[8]]
     residuals, branches, r2s = [hidden_in], [], []
     for l in range(layers - 1):
@@ -979,11 +1166,11 @@
         got = comm_call(
             Step(
                 partial=True, gather=True, late=True, scale=inner_all, middle=forward_middle,
-                weights=column_chunks, **common,
+                weights=row_chunks, **common,
             ),
             "between_forward", 2 + l,
             dict(part=(out[6], vmem), ssq=(out[7], vmem), res=(residuals[l], vmem),
-                 gain=(gains[l + 1], vmem), **win),
+                 gain=(gain_rows[l + 1], vmem), **win),
             dict(full=whole_rows, branch=own_rows, res_out=own_rows,
                  r2=((rows_own, 128), F32, vmem), **wout),
         )
@@ -992,30 +1179,30 @@
         residuals.append(got["res_out"])
         r2s.append(got["r2"])
         packed.append(got["wfull"].reshape(width, packed_width))
-        out = forward_mix(rows[-1], packed[-1], params[l + 1] + (gains[l + 1],), False)
+        out = forward_mix(rows[-1], packed[-1], params + (gain_rows,), l + 1)
         saved.append(out[:6])
     got = comm_call(
         Step(
-            partial=True, gather=True, scale=inner_all, inner=True, payload=scaled_payload,
+            partial=True, scale=inner_all, inner=True,
             middle=functools.partial(last_middle, inner_all), **common,
         ),
         "turn_around", 16,
         dict(part=(out[6], vmem), ssq=(out[7], vmem), res=(residuals[-1], vmem),
              grad_in=(out_grad, vmem)),
-        dict(full=whole_rows, res_out=own_rows, inner=((8, tokens), F32, vmem)),
+        dict(res_out=own_rows, inner=((8, tokens), F32, vmem)),
         r2=pltpu.VMEM((rows_own, 128), F32),
     )
     hidden_out = got["res_out"]
     gradient = out_grad
-    scattered, summed = [None] * layers, [None] * layers
+    scattered, summed, gain_grads = [None] * layers, [None] * layers, [None] * layers
     for l in reversed(range(layers)):
-        grad_rows = got["full"]
-        dcat, dpart, gvec, gst, gdt = backward_mix(
-            grad_rows, got["inner"], saved[l], packed[l], params[l], pick
-        )
+        dcat, dpart, *small_grads = backward_mix(
+            grad_rows, got["inner"], saved[l], packed[l], params, pick, l
+        )
+        summed[l] = small_grads
         more = l > 0
         inputs = dict(
-            part=(dpart, vmem), res=(residuals[l], vmem), gain=(gains[l], vmem),
+            part=(dpart, vmem), res=(residuals[l], vmem), gain=(gain_rows[l], vmem),
             grad_in=(gradient, vmem), lrows=(rows[l], vmem), lgrad=(grad_rows, vmem),
             right=(dcat, vmem),
         )
@@ -1026,21 +1213,37 @@
         if more:
             inputs.update(r2=(r2s[l - 1], vmem), branch=(branches[l - 1], vmem))
             outputs.update(full=whole_rows, inner=((8, tokens), F32, vmem))
+        else:
+            for i in range(layers):
+                gvec, gst, gdt = summed[i]
+                inputs["esum%d" % i], inputs["esum_%d" % i] = (gvec, vmem), (gdt, vmem)
+                inputs["lsum%d" % i] = (gst, vmem)
+            for i in range(1, layers):
+                inputs["gsum%d" % i] = (gain_grads[i], vmem)
+            early = sum(v.shape[1] for i in range(layers) for v in summed[i])
+            outputs.update(
+                sums=((8, early), F32, vmem), gain_sums=((8, width), F32, vmem)
+            )
         got = comm_call(
             Step(
                 partial=True, gather=more, late=more, inner=more, grads=column_chunks,
+                states=bc_width, sums=not more,
                 middle=functools.partial(backward_middle, inner_all if more else None), **common,
             ),
             "between_backward" if more else "last_backward", 17 + l, inputs, outputs,
         )
         gradient = got["grad_out"]
-        scattered[l] = got["gout"]
-        summed[l] = (gvec, gdt, gst, got["ggain"][0])
+        scattered[l], gain_grads[l] = got["gout"], got["ggain"]
+        if more:
+            grad_rows = got["full"]
     gout = jnp.stack(scattered)
-    gvec, gdt, gst, ggain = (jnp.stack([s[i] for s in summed]) for i in range(4))
-    gvec, gdt = lax.psum((gvec, gdt), "dp")
-    gst, ggain = lax.psum((gst, ggain), ("dp", "tensor"))
-    gbc = lax.psum(gout[:, :, :bc_width].astype(BF), "tensor").astype(F32)
+    sums, ggain = got["sums"], got["gain_sums"][:layers]
+    each = inner + 128
+    gvec = jnp.stack([sums[:, i * each : i * each + inner] for i in range(layers)])
+    gdt = jnp.stack([sums[:, i * each + inner : (i + 1) * each] for i in range(layers)])
+    gst = jnp.stack(
+        [sums[:, layers * each + i * bc_width :][:, :bc_width] for i in range(layers)]
+    )
     own = lambda v, axis: lax.dynamic_slice_in_dim(
         v, lax.axis_index("dp") * (v.shape[axis] // dp_count), v.shape[axis] // dp_count, axis
     )
@@ -1052,7 +1255,7 @@
         own(ggain, 1),
         gout[:, :, first : first + inner],
         gout[:, :, first + inner : first + 2 * inner],
-        gbc,
+        gout[:, :, :bc_width],
         gout[:, :, bc_width : bc_width + heads],
         gvec[:, 0:4],
         gvec[:, 4],

time: 730 us -> 633 us (0.87)
  blocking collectives: 61.1 us -> 0 us
  Pallas kernels: 606 us -> 579 us
    psum x2 -> x0, blocking collectives: 61.1 us -> none  [the longest x1 38.1 us: shards(): gst, ggain = lax.psum((gst, ggain), ('dp', 'tensor'))]
    pallas_call x5, Pallas kernels: 473 us -> 445 us  [comm_call(): pl.pallas_call(functools.partial(comm_kernel, o, names), in_specs=[pl.Blo...]
  transfers between devices with their start and end apart: 1 -> 1, of which waited for: 0 -> 0; matrix products, arithmetic and copies ran while one was open for 2% -> 2% of each run, Pallas kernels for 0% -> 37%
where the time goes in v3:
time: 633 us; the launch traced here: 627 us
  Pallas kernels  579 us (91%)
  local copies, waits for them, and re-layouts  22.8 us (4%)
  between operations  14.8 us (2%)
  other arithmetic  10.2 us (2%)
    pallas_call x5, Pallas kernels, comm_call(): pl.pallas_call(functools.partial(comm_kernel, o, names), in_specs=[pl.Blo...  445 us
    pallas_call x2, Pallas kernels, backward_mix(): pl.pallas_call(bwd_kernel, grid=(blocks,), in_specs=[tok(width), pl.Block...  80.1 us
    pallas_call x2, Pallas kernels, forward_mix(): pl.pallas_call(functools.partial(fwd_kernel, first), grid=(blocks,), in_s...  53.4 us
  transfers between devices with their start and end apart: 1, of which 0 were waited for; matrix products, arithmetic and copies ran while one was open for 2% of the time, Pallas kernels for 37%

profile of v3, /device:TPU:0, one launch (start us, length us, event | category | flops | bytes accessed | tf_op | source)
XLA Modules:
  0.0 626.5 jit_solution(17773746174085017115)
XLA Ops:
  7.2 1.7 slice_bitcast_fusion.6
  8.9 0.8 fusion.19
  9.9 0.8 reshape.94
  10.6 0.7 fusion.17
  11.3 0.7 pad_maximum_fusion.2
  12.2 1.1 slice_bitcast_fusion
  13.4 1.7 concatenate.13.refs_1_
  15.1 61.2 %gather_first.1 = (bf16[1024,1536]{1,0:T(8,128)(2,1)}, bf16[2,2,2,192,2688]{4,3,2,1,0:T(8,128)(2,1)}) custom-call(bf16[256,1536]{1,0:T(8,128)(2,1)} %refs_1_.1, bf16[192,2688]{1,0:T(8,128)(2,1)} %concatenate.13.refs_1_), custom_call_target="tpu_custom_call" | custom-call | tf_op jit(solution)/shard_map/gather_first/pallas_call | solution.py:997
  76.3 1.2 slice.149
  77.5 1.4 slice.119
  79.0 1.3 slice.121
  81.0 0.7 reshape.102.cst_ref
  83.3 0.6 maximum_convert_fusion.vec_ref
  83.9 27.1 %mix_forward.2 = (f32[1024,768]{1,0:T(8,128)}, f32[1024,768]{1,0:T(8,128)}, f32[1024,256]{1,0:T(8,128)}, f32[1024,128]{1,0:T(8,128)}, f32[1024,768]{1,0:T(8,128)...) custom-call(bf16[1024,1536]{1,0:T(8,128)(2,1)} %get-tuple-element.64.row, ...), custom_call_target="tpu_custom_call" | custom-call | tf_op jit(solution)/shard_map/mix_forward/pallas_call | solution.py:210
  111.1 1.7 concatenate.15.refs_4_
  113.4 112.0 %between_forward.1 = (bf16[1024,1536]{1,0:T(8,128)(2,1)}, f32[256,1536]{1,0:T(8,128)}, f32[256,1536]{1,0:T(8,128)}, f32[256,128]{1,0:T(8,128)}, bf16[2,2,2,192,2688]{4,3,2,1,0:T(8,128)(2,1)}) custom-call(bf16[1024,1536]{1,0:T(8,128)(2,1)} %get-tuple-element.66.refs_0_, f32[8,1024]{1,0:T(8,128)} %get-tuple-element.67.refs_1_, bf16[256,1536]{1,0:T(8,128)(2,1)} %refs_1_.1, ...), custom_call_target="tpu_custom_call" | custom-call | tf_op jit(solution)/shard_map/between_forward/pallas_call | solution.py:997
  225.4 26.3 %mix_forward.3 = (f32[1024,768]{1,0:T(8,128)}, f32[1024,768]{1,0:T(8,128)}, f32[1024,256]{1,0:T(8,128)}, f32[1024,128]{1,0:T(8,128)}, f32[1024,768]{1,0:T(8,128)...) custom-call(bf16[1024,1536]{1,0:T(8,128)(2,1)} %get-tuple-element.68.rows_ref.refs_4_, ...), custom_call_target="tpu_custom_call" | custom-call | tf_op jit(solution)/shard_map/mix_forward/pallas_call | solution.py:210
  251.6 68.7 %turn_around.1 = (f32[256,1536]{1,0:T(8,128)}, f32[8,1024]{1,0:T(8,128)}) custom-call(bf16[1024,1536]{1,0:T(8,128)(2,1)} %get-tuple-element.70.refs_0_, f32[8,1024]{1,0:T(8,128)} %get-tuple-element.71.refs_1_, f32[256,1536]{1,0:T(8,128)} %get-tuple-element.72.refs_2_.refs_1_, bf16[256,1536]{1,0:T(8,128)(2,1)} %refs_3_.1), custom_call_target="tpu_custom_call" | custom-call | tf_op jit(solution)/shard_map/turn_around/pallas_call | solution.py:997
  320.4 0.8 fusion.4.pick_ref
  321.3 40.0 %mix_backward.2 = (bf16[1024,2688]{1,0:T(8,128)(2,1)}, bf16[1024,1536]{1,0:T(8,128)(2,1)}, f32[8,768]{1,0:T(8,128)}, f32[8,256]{1,0:T(8,128)}, f32[8,128]{1,0:T(8,128)}) custom-call(bf16[1024,1536]{1,0:T(8,128)(2,1)} %all-gather.2.cloned.1.call-done.gb_ref.refs_5_, f32[8,1024]{1,0:T(8,128)} %get-tuple-element.75.e_ref, ...), custom_call_target="tpu_custom_call" | custom-call | tf_op jit(solution)/shard_map/mix_backward/pallas_call | solution.py:409
  361.3 111.8 %between_backward.1 = (f32[256,1536]{1,0:T(8,128)}, f32[8,1536]{1,0:T(8,128)}, f32[192,2688]{1,0:T(8,128)}, bf16[1024,1536]{1,0:T(8,128)(2,1)}, f32[8,1024]{1,0:T(8,128)}) custom-call(bf16[1024,1536]{1,0:T(8,128)(2,1)} %get-tuple-element.82.refs_0_, f32[256,1536]{1,0:T(8,128)} %get-tuple-element.72.refs_2_.refs_1_, ...), custom_call_target="tpu_custom_call" | custom-call | tf_op jit(solution)/shard_map/between_backward/pallas_call | solution.py:997
  473.1 40.1 %mix_backward.3 = (bf16[1024,2688]{1,0:T(8,128)(2,1)}, bf16[1024,1536]{1,0:T(8,128)(2,1)}, f32[8,768]{1,0:T(8,128)}, f32[8,256]{1,0:T(8,128)}, f32[8,128]{1,0:T(8,128)}) custom-call(bf16[1024,1536]{1,0:T(8,128)(2,1)} %get-tuple-element.86.gb_ref.refs_5_, f32[8,1024]{1,0:T(8,128)} %get-tuple-element.87.e_ref, f32[1024,768]{1,0:T(8,128)} %get-tuple-element.88.gate_ref, ...), custom_call_target="tpu_custom_call" | custom-call | tf_op jit(solution)/shard_map/mix_backward/pallas_call | solution.py:409
  513.2 91.5 %last_backward.1 = (f32[256,1536]{1,0:T(8,128)}, f32[8,1536]{1,0:T(8,128)}, f32[192,2688]{1,0:T(8,128)}, f32[8,2304]{1,0:T(8,128)}, f32[8,1536]{1,0:T(8,128)}) custom-call(bf16[1024,1536]{1,0:T(8,128)(2,1)} %get-tuple-element.94.refs_0_, bf16[256,1536]{1,0:T(8,128)(2,1)} %refs_1_.1, f32[1,1536]{1,0:T(1,128)} %get-tuple-element.162.refs_2_, ...), custom_call_target="tpu_custom_call" | custom-call | tf_op jit(solution)/shard_map/last_backward/pallas_call | solution.py:997
  604.7 4.0 fusion.2
  608.7 0.8 fusion.3
  609.5 0.9 copy-done.7
  612.3 0.8 slice.129
  613.1 0.7 copy.61
  615.1 0.7 constant_dynamic-slice_fusion
  616.3 0.6 reduce_sum.9
  617.0 1.1 copy.77
  618.1 1.1 copy.78
  (65 shorter events, 7.1 us)
Async XLA Ops:
  7.2 6.1 copy-start.4
  7.2 6.1 copy-start.5
  7.2 314.1 %all-gather.2.cloned.1.call-start = ((), (), s32[]{:S(2)}) async-start(), calls=%async_computation | async-start | bytes 3932160 | tf_op jit(solution)/shard_map/all_gather | solution.py:1150
  76.3 4.0 copy-start.9
  76.3 4.0 copy-start.11
  76.3 4.2 copy-start.10
  78.9 3.7 copy-start.12
  79.0 3.7 copy-start.13
  79.0 4.3 copy-start.8
  83.9 27.1 %copy-start.6 = (bf16[192,256]{1,0:T(8,128)(2,1)S(1)}, bf16[192,256]{1,0:T(8,128)(2,1)}, u32[]{:S(2)}) copy-start(bf16[192,256]{1,0:T(8,128)(2,1)} %get-tuple-element.151) | copy-start | bytes 294916
  604.7 4.0 copy-start
  604.7 4.0 copy-start.1
  609.5 0.9 copy-start.7
  609.5 7.5 %copy-start.2 = (f32[256,1536]{1,0:T(8,128)S(1)}, f32[256,1536]{1,0:T(8,128)}, u32[]{:S(2)}) copy-start(f32[256,1536]{1,0:T(8,128)} %get-tuple-element.186) | copy-start | bytes 4718596
  609.5 8.6 %copy-start.3 = (f32[256,1536]{1,0:T(8,128)S(1)}, f32[256,1536]{1,0:T(8,128)}, u32[]{:S(2)}) copy-start(f32[256,1536]{1,0:T(8,128)} %get-tuple-element.187) | copy-start | bytes 4718596
Sparse Core Ops, SparseCore 0:
  76.4 73.7 all-gather.1

commit v4 on v3

--- a/solution.py
+++ b/solution.py
@@ -21,6 +21,10 @@
     return lax.dot_general(a, b, (((1,), (0,)), ((), ())), preferred_element_type=F32)
 
 
+def tn(a, b):
+    return lax.dot_general(a, b, (((0,), (0,)), ((), ())), preferred_element_type=F32)
+
+
 def nt(a, b):
     return lax.dot_general(a, b, (((1,), (1,)), ((), ())), preferred_element_type=F32)
 
@@ -86,11 +90,15 @@
 
 
 def fwd_kernel(
-    first, rows_ref, w_ref, vec_ref, cst_ref, tiny_ref, gain_ref,
-    gate_ref, val_ref, st_ref, dt_ref, y_ref, ent_ref, part_ref, ssq_ref,
-    *rest,
+    first, last, rows_ref, w_ref, vec_ref, cst_ref, tiny_ref, gain_ref, *rest,
 ):
-    normed_ref = rest[0] if first else None
+    if last:
+        gb_ref, *rest = rest
+    gate_ref, val_ref, st_ref, dt_ref, y_ref, ent_ref, part_ref, ssq_ref, *rest = rest
+    if first:
+        normed_ref, *rest = rest
+    if last:
+        dm_ref, *rest = rest
     state, vpad, spad = rest[-3:]
     step = pl.program_id(0)
     length = rows_ref.shape[0]
@@ -172,6 +180,12 @@
     ssq_ref[...] = nt(jnp.ones((8, inner), BF), square)
     mixed = (gated * gg_ref[...]).astype(BF)
     part_ref[...] = nt(mixed, wot_ref[...]).astype(BF)
+    if last:
+        dm = nn(gb_ref[...], wot_ref[...])
+        dm_ref[...] = dm
+        dots = nt(jnp.ones((8, inner), BF), (dm * gg_ref[...] * gated).astype(BF))
+        row = lax.broadcasted_iota(jnp.int32, dots.shape, 0)
+        ssq_ref[...] = jnp.where(row == 0, ssq_ref[...], dots)
 
 
 def whole(shape):
@@ -185,8 +199,8 @@
     ]
 
 
-def forward_mix(rows, packed, params, l):
-    first = l == 0
+def forward_mix(rows, packed, params, l, gb=None):
+    first, last = l == 0, gb is not None
     tokens, width = rows.shape
     inner = params[0].shape[2]
     bc_width = params[1].shape[2]
@@ -207,10 +221,14 @@
     ]
     if first:
         outs.append(((tokens, width), BF, tok(width)))
+    if last:
+        outs.append(((tokens, inner), F32, tok(inner)))
     return pl.pallas_call(
-        functools.partial(fwd_kernel, first),
+        functools.partial(fwd_kernel, first, last),
         grid=(blocks,),
-        in_specs=[tok(width), whole(packed.shape)] + layer_specs(params, l),
+        in_specs=[tok(width), whole(packed.shape)]
+        + layer_specs(params, l)
+        + ([tok(width)] if last else []),
         out_specs=[o[2] for o in outs],
         out_shape=[jax.ShapeDtypeStruct(o[0], o[1]) for o in outs],
         scratch_shapes=[
@@ -222,11 +240,11 @@
             dimension_semantics=("arbitrary",), vmem_limit_bytes=56 * MIB
         ),
         name="mix_forward",
-    )(rows, packed, *params)
+    )(rows, packed, *params, *([gb] if last else []))
 
 
 def bwd_kernel(
-    gb_ref, e_ref, gate_ref, val_ref, valp_ref, st_ref, stp_ref, dt_ref, y_ref, ent_ref,
+    ready, gb_ref, e_ref, gate_ref, val_ref, valp_ref, st_ref, stp_ref, dt_ref, y_ref, ent_ref,
     w_ref, vec_ref, cst_ref, tiny_ref, pick_ref,
     dcat_ref, dpart_ref, gvec_ref, gst_ref, gdt_ref,
     dstate, vpad, spad, dvpad, dspad,
@@ -291,7 +309,7 @@
     gated = y * sgate
     per_token = e_ref[...].T
     e, r2 = per_token[:, 0:1], per_token[:, 1:2]
-    dm = nn(gb_ref[...], wot_ref[...]) * r2
+    dm = (gb_ref[...] if ready else nn(gb_ref[...], wot_ref[...])) * r2
     dgated = dm * gg_ref[...] - e * gated
     mixed_ref[...] = (gated * r2 * gg_ref[...]).astype(BF)
     dgate = (dgated * y * (sig_g * (1.0 + gate * (1.0 - sig_g)))).astype(BF)
@@ -383,9 +401,9 @@
     dpart_ref[...] = dpart.astype(BF)
 
 
-def backward_mix(gb, e_rows, kept, packed, params, pick, l):
+def backward_mix(gb, ready, e_rows, kept, packed, params, pick, l):
     gate, val, st, dt, y, ent = kept
-    tokens, width = gb.shape
+    tokens, width = gb.shape[0], packed.shape[0]
     inner = params[0].shape[2]
     bc_width = params[1].shape[2]
     dt_width = 128
@@ -407,10 +425,10 @@
         ((8, dt_width), F32, fixed(8, dt_width)),
     ]
     return pl.pallas_call(
-        bwd_kernel,
+        functools.partial(bwd_kernel, ready),
         grid=(blocks,),
         in_specs=[
-            tok(width),
+            tok(gb.shape[1]),
             pl.BlockSpec((8, q), lambda i: (0, back(i))),
             tok(inner), tok(inner), halo(inner), tok(bc_width), halo(bc_width), tok(dt_width),
             tok(inner),
@@ -440,6 +458,7 @@
         self.line = 4
         self.chunks = 8
         self.hop = 1
+        self.pass_hop = 1
         self.slack = 0
         self.partial = False
         self.gather = False
@@ -448,6 +467,8 @@
         self.inner = False
         self.weights = 0
         self.grads = 0
+        self.tail = 2
+        self.lag = 1
         self.states = 0
         self.sums = False
         self.bits = 0
@@ -550,7 +571,7 @@
         for s in order:
             away = t - s if side == 0 else s - t
             late = o.hop * max(s, n - 1 - s) + o.slack if o.late else 0
-            c = tau - late - o.hop * away
+            c = tau - late - o.pass_hop * away
 
             @when((away > 0) & (c >= 0) & (c < count))
             def _():
@@ -613,7 +634,7 @@
         for parity in range(2):
             j = 2 * pair + parity
 
-            @when((j >= 0) & (j < max(o.weights, o.grads)))
+            @when((j >= 0) & (j < o.weights))
             def _():
                 fn(parity, j)
 
@@ -654,23 +675,37 @@
         )
 
     def product(j):
-        left = lax.div(j, jnp.int32(5)) if o.bits else 0
-
-        def one(i, _):
-            spot = tuple((i // (1 << b)) % 2 for b in range(o.bits - 1, -1, -1))
-            depth = r.grad.shape[-2]
-            lhs = r.left[left, pl.ds(pl.multiple_of(i * depth, depth), depth), :]
-            r.grad[(j, *spot)] = nn(lhs, r.right[:, cols(j)]).astype(BF)
-            return 0
-
-        lax.fori_loop(0, 1 << o.bits, one, 0)
+        slab = o.width // 2
+        inner_shape = (2,) * (o.bits - 1) + (slab >> (o.bits - 1), WCHUNK)
+
+        def slabs(left):
+            for i in range(2):
+                out = tn(left[:, pl.ds(i * slab, slab)], r.right[:, cols(j)])
+                r.grad[j, i] = out.astype(BF).reshape(inner_shape)
+
+        @when(j < o.grads - o.tail)
+        def _():
+            slabs(r.lrows)
+
+        @when(j >= o.grads - o.tail)
+        def _():
+            slabs(r.lgrad)
+
+    def each_chunk(j, fn):
+        for parity in range(2):
+            @when((j >= 0) & (j < o.grads) & (lax.rem(j, 2) == parity))
+            def _():
+                fn(parity, j)
 
     def grad_items(tau):
+        @when(tau < o.grads)
+        def _():
+            product(tau)
+
         def first(parity, j):
-            product(j)
             grad_copy(parity, 0, j).start()
 
-        each_parity(tau, first)
+        each_chunk(tau, first)
         for stage in range(1, o.bits + 1):
             def run(parity, j):
                 grad_copy(parity, stage - 1, j).wait_recv()
@@ -689,7 +724,10 @@
                         r.gout[:, cols(j)] = total
                 if stage < o.bits:
                     grad_copy(parity, stage, j).start()
-            each_parity(tau - stage, run)
+            each_chunk(tau - grad_lag(stage), run)
+
+    def grad_lag(stage):
+        return o.lag * (2 * stage - 1) if stage else 0
 
     def share(buf, send, recv, k):
         return remote(buf.at[t], buf.at[t], send.at[k - 1], recv.at[k - 1],
@@ -749,7 +787,7 @@
                         double(*g, b + 1).start()
 
     def state_items(tau):
-        at_first = o.bits + 1
+        at_first = grad_lag(o.bits) + 1
         quarter = r.gout.shape[0] // n
 
         @when(tau == at_first)
@@ -789,13 +827,6 @@
             square_copy(k).start()
     if o.weights:
         own_weights().start()
-    if o.grads:
-        def turn(i, _):
-            strip = pl.ds(pl.multiple_of(i * 128, 128), 128)
-            r.left[0, strip, :] = r.lrows[:, strip].T
-            r.left[1, strip, :] = r.lgrad[:, strip].T
-            return 0
-        lax.fori_loop(0, o.width // 128, turn, 0)
     if o.scale:
         total = spot_of(t, r.ssq)[...]
         for k in range(1, n):
@@ -810,11 +841,14 @@
 
     ends = [count + o.hop * (n - 1) + o.slack]
     if o.late:
-        ends.append(ends[0] + o.hop * (n - 1))
-    if over_dp:
-        ends.append((max(o.weights, o.grads) + 1) // 2 + o.bits)
+        ends.append(ends[0] + o.pass_hop * (n - 1))
+    elif o.gather:
+        ends.append(count + o.pass_hop * (n - 1))
+    if o.weights:
+        ends.append((o.weights + 1) // 2 + o.bits)
     if o.grads:
-        ends.append(o.bits + 4)
+        ends.append(o.grads + grad_lag(o.bits))
+        ends.append(grad_lag(o.bits) + 4)
     if o.sums:
         ends.append(4 + o.bits)
 
@@ -962,7 +996,6 @@
         depth = o.width >> o.bits
         scratch.update(
             grad=pltpu.VMEM((o.grads, *(2,) * o.bits, depth, WCHUNK), BF),
-            left=pltpu.VMEM((2, width, n * rows), BF),
             gr_send=dma((o.bits, o.grads)),
             gr_recv=dma((o.bits, o.grads)),
         )
@@ -1008,6 +1041,52 @@
     return dict(zip(outputs, out))
 
 
+def meet_kernel(n, inner_all, own_ref, out_ref, bank, send, recv):
+    t = lax.axis_index("tensor")
+    barrier = pltpu.get_barrier_semaphore()
+    for k in range(1, n):
+        pl.semaphore_signal(
+            barrier, inc=1, device_id={"tensor": lax.rem(t + k, n)},
+            device_id_type=pl.DeviceIdType.MESH,
+        )
+    pl.semaphore_wait(barrier, n - 1)
+    copies = [
+        remote(own_ref, bank.at[t], send.at[k - 1], recv.at[k - 1], {"tensor": lax.rem(t + k, n)})
+        for k in range(1, n)
+    ]
+    for copy in copies:
+        copy.start()
+    bank[t] = own_ref[...]
+    for k in range(1, n):
+        source = lax.rem(t + n - k, n)
+        remote(
+            own_ref, bank.at[source], send.at[k - 1], recv.at[k - 1], {"tensor": source}
+        ).wait_recv()
+    total = bank[0]
+    for s in range(1, n):
+        total = total + bank[s]
+    scale = lax.rsqrt(total[0:1, :] / inner_all + EPSILON)
+    row = lax.broadcasted_iota(jnp.int32, total.shape, 0)
+    e = scale * scale * scale * (total[1:2, :] / inner_all)
+    out_ref[...] = jnp.where(row == 0, e, scale)
+    for copy in copies:
+        copy.wait_send()
+
+
+def meet(own, n, inner_all, collective):
+    vmem = pl.BlockSpec(memory_space=pltpu.VMEM)
+    dma = pltpu.SemaphoreType.DMA
+    return pl.pallas_call(
+        functools.partial(meet_kernel, n, inner_all),
+        in_specs=[vmem],
+        out_specs=vmem,
+        out_shape=jax.ShapeDtypeStruct(own.shape, F32),
+        scratch_shapes=[pltpu.VMEM((n,) + own.shape, F32), dma((n - 1,)), dma((n - 1,))],
+        compiler_params=pltpu.CompilerParams(collective_id=collective, has_side_effects=True),
+        name="turn_around",
+    )(own)
+
+
 def plain_payload(r):
     return r.own[...]
 
@@ -1026,17 +1105,6 @@
     r.res_out[at, :] = residual
     r1 = lax.rsqrt(jnp.mean(residual * residual, axis=1, keepdims=True) + EPSILON)
     return (residual * r1 * r.gain[...]).astype(BF)
-
-
-def last_middle(inner_all, r, at, total):
-    if at is None:
-        return None
-    r2 = r.r2[at, 0:1]
-    branch = total * r2
-    r.res_out[at, :] = r.res[at, :].astype(F32) + branch
-    dot = jnp.sum(r.grad_in[at, :].astype(F32) * branch, axis=1, keepdims=True)
-    r.icol[at, :] = token_columns(r2 * r2 * dot / inner_all, r2)
-    return None
 
 
 def backward_middle(inner_all, r, at, total):
@@ -1179,25 +1247,22 @@
         residuals.append(got["res_out"])
         r2s.append(got["r2"])
         packed.append(got["wfull"].reshape(width, packed_width))
-        out = forward_mix(rows[-1], packed[-1], params + (gain_rows,), l + 1)
+        gb = grad_rows if l + 1 == layers - 1 else None
+        out = forward_mix(rows[-1], packed[-1], params + (gain_rows,), l + 1, gb)
         saved.append(out[:6])
-    got = comm_call(
-        Step(
-            partial=True, scale=inner_all, inner=True,
-            middle=functools.partial(last_middle, inner_all), **common,
-        ),
-        "turn_around", 16,
-        dict(part=(out[6], vmem), ssq=(out[7], vmem), res=(residuals[-1], vmem),
-             grad_in=(out_grad, vmem)),
-        dict(res_out=own_rows, inner=((8, tokens), F32, vmem)),
-        r2=pltpu.VMEM((rows_own, 128), F32),
+    total = lax.psum_scatter(out[6], "tensor", scatter_dimension=0, tiled=True)
+    token_rows = meet(out[7], tensor_count, inner_all, 16)
+    r2_own = lax.dynamic_slice_in_dim(
+        token_rows[1], lax.axis_index("tensor") * rows_own, rows_own, 0
     )
-    hidden_out = got["res_out"]
+    hidden_out = residuals[-1].astype(F32) + r2_own[:, None] * total.astype(F32)
+    product = out[8]
     gradient = out_grad
     scattered, summed, gain_grads = [None] * layers, [None] * layers, [None] * layers
     for l in reversed(range(layers)):
+        last = l == layers - 1
         dcat, dpart, *small_grads = backward_mix(
-            grad_rows, got["inner"], saved[l], packed[l], params, pick, l
+            product if last else grad_rows, last, token_rows, saved[l], packed[l], params, pick, l
         )
         summed[l] = small_grads
         more = l > 0
@@ -1235,7 +1300,7 @@
         gradient = got["grad_out"]
         scattered[l], gain_grads[l] = got["gout"], got["ggain"]
         if more:
-            grad_rows = got["full"]
+            grad_rows, token_rows = got["full"], got["inner"]
     gout = jnp.stack(scattered)
     sums, ggain = got["sums"], got["gain_sums"][:layers]
     each = inner + 128

time: 633 us -> 562 us (0.89)
  Pallas kernels: 579 us -> 504 us
    pallas_call x5 -> x4, Pallas kernels: 445 us -> 362 us  [comm_call(): pl.pallas_call(functools.partial(comm_kernel, o, names), in_specs=[pl.Blo...]
    pallas_call x4 -> x5, Pallas kernels: 134 us -> 143 us  [the longest x2 78.7 us: backward_mix(): pl.pallas_call(functools.partial(bwd_kernel, ready), grid=(blocks,), in_s...]
  transfers between devices with their start and end apart: 1 -> 2, of which waited for: 0 -> 0; matrix products, arithmetic and copies ran while one was open for 2% -> 4% of each run, Pallas kernels for 37% -> 75%
where the time goes in v4:
time: 562 us; the launch traced here: 555 us
  Pallas kernels  504 us (90%)
  local copies, waits for them, and re-layouts  22.3 us (4%)
  between operations  14.8 us (3%)
  other arithmetic  13.3 us (2%)
    pallas_call x4, Pallas kernels, comm_call(): pl.pallas_call(functools.partial(comm_kernel, o, names), in_specs=[pl.Blo...  362 us
    pallas_call x2, Pallas kernels, backward_mix(): pl.pallas_call(functools.partial(bwd_kernel, ready), grid=(blocks,), in_s...  78.7 us
    pallas_call x2, Pallas kernels, forward_mix(): pl.pallas_call(functools.partial(fwd_kernel, first, last), grid=(blocks,)...  56.7 us
  transfers between devices with their start and end apart: 2, of which 0 were waited for; matrix products, arithmetic and copies ran while one was open for 4% of the time, Pallas kernels for 75%

profile of v4, /device:TPU:0, one launch (start us, length us, event | category | flops | bytes accessed | tf_op | source)
XLA Modules:
  0.0 554.8 jit_solution(4507961241624137638)
XLA Ops:
  7.2 1.7 slice_bitcast_fusion.6
  8.9 0.8 fusion.19
  9.9 0.8 reshape.97
  10.6 0.7 fusion.17
  11.3 0.7 pad_maximum_fusion.2
  12.2 1.1 slice_bitcast_fusion
  13.4 1.7 concatenate.13.refs_1_
  15.1 61.2 %gather_first.1 = (bf16[1024,1536]{1,0:T(8,128)(2,1)}, bf16[2,2,2,192,2688]{4,3,2,1,0:T(8,128)(2,1)}) custom-call(bf16[256,1536]{1,0:T(8,128)(2,1)} %refs_1_.1, bf16[192,2688]{1,0:T(8,128)(2,1)} %concatenate.13.refs_1_), custom_call_target="tpu_custom_call" | custom-call | tf_op jit(solution)/shard_map/gather_first/pallas_call | solution.py:1030
  76.4 1.2 slice.153
  77.6 1.4 slice.122
  79.0 1.3 slice.124
  81.0 0.7 reshape.105.cst_ref
  83.3 0.7 maximum_convert_fusion.vec_ref
  84.0 27.1 %mix_forward.2 = (f32[1024,768]{1,0:T(8,128)}, f32[1024,768]{1,0:T(8,128)}, f32[1024,256]{1,0:T(8,128)}, f32[1024,128]{1,0:T(8,128)}, f32[1024,768]{1,0:T(8,128)...) custom-call(bf16[1024,1536]{1,0:T(8,128)(2,1)} %get-tuple-element.63.row, ...), custom_call_target="tpu_custom_call" | custom-call | tf_op jit(solution)/shard_map/mix_forward/pallas_call | solution.py:226
  111.1 1.7 concatenate.15.refs_4_
  113.4 112.0 %between_forward.1 = (bf16[1024,1536]{1,0:T(8,128)(2,1)}, f32[256,1536]{1,0:T(8,128)}, f32[256,1536]{1,0:T(8,128)}, f32[256,128]{1,0:T(8,128)}, bf16[2,2,2,192,2688]{4,3,2,1,0:T(8,128)(2,1)}) custom-call(bf16[1024,1536]{1,0:T(8,128)(2,1)} %get-tuple-element.65.refs_0_, f32[8,1024]{1,0:T(8,128)} %get-tuple-element.66.refs_1_, bf16[256,1536]{1,0:T(8,128)(2,1)} %refs_1_.1, ...), custom_call_target="tpu_custom_call" | custom-call | tf_op jit(solution)/shard_map/between_forward/pallas_call | solution.py:1030
  225.4 29.6 %mix_forward.3 = (f32[1024,768]{1,0:T(8,128)}, f32[1024,768]{1,0:T(8,128)}, f32[1024,256]{1,0:T(8,128)}, f32[1024,128]{1,0:T(8,128)}, f32[1024,768]{1,0:T(8,128)...) custom-call(bf16[1024,1536]{1,0:T(8,128)(2,1)} %get-tuple-element.68.rows_ref.r, ...), custom_call_target="tpu_custom_call" | custom-call | tf_op jit(solution)/shard_map/mix_forward/pallas_call | solution.py:226
  255.1 0.8 fusion.4.pick_ref
  256.0 7.2 %turn_around.1.e_ref = f32[8,1024]{1,0:T(8,128)} custom-call(f32[8,1024]{1,0:T(8,128)} %get-tuple-element.71.own_ref), custom_call_target="tpu_custom_call" | custom-call | tf_op jit(solution)/shard_map/turn_around/pallas_call | solution.py:1079
  263.1 0.8 slice.131
  263.9 38.9 %mix_backward.2 = (bf16[1024,2688]{1,0:T(8,128)(2,1)}, bf16[1024,1536]{1,0:T(8,128)(2,1)}, f32[8,768]{1,0:T(8,128)}, f32[8,256]{1,0:T(8,128)}, f32[8,128]{1,0:T(8,128)}) custom-call(f32[1024,768]{1,0:T(8,128)} %get-tuple-element.73.gb_ref, f32[8,1024]{1,0:T(8,128)} %turn_around.1.e_ref, f32[1024,768]{1,0:T(8,128)} %get-tuple-element.74.gate_ref, ...), custom_call_target="tpu_custom_call" | custom-call | tf_op jit(solution)/shard_map/mix_backward/pallas_call | solution.py:427
  302.8 105.7 %between_backward.1 = (f32[256,1536]{1,0:T(8,128)}, f32[8,1536]{1,0:T(8,128)}, f32[192,2688]{1,0:T(8,128)}, bf16[1024,1536]{1,0:T(8,128)(2,1)}, f32[8,1024]{1,0:T(8,128)}) custom-call(bf16[1024,1536]{1,0:T(8,128)(2,1)} %get-tuple-element.80.refs_0_, f32[256,1536]{1,0:T(8,128)} %get-tuple-element.67.refs_1_, f32[1,1536]{1,0:T(1,128)} %get-tuple-element.161.refs_3_.refs_2_, ...), custom_call_target="tpu_custom_call" | custom-call | tf_op jit(solution)/shard_map/between_backward/pallas_call | solution.py:1030
  408.5 39.9 %mix_backward.3 = (bf16[1024,2688]{1,0:T(8,128)(2,1)}, bf16[1024,1536]{1,0:T(8,128)(2,1)}, f32[8,768]{1,0:T(8,128)}, f32[8,256]{1,0:T(8,128)}, f32[8,128]{1,0:T(8,128)}) custom-call(bf16[1024,1536]{1,0:T(8,128)(2,1)} %get-tuple-element.84.gb_ref.refs_5_, f32[8,1024]{1,0:T(8,128)} %get-tuple-element.85.e_ref, f32[1024,768]{1,0:T(8,128)} %get-tuple-element.86.gate_ref, ...), custom_call_target="tpu_custom_call" | custom-call | tf_op jit(solution)/shard_map/mix_backward/pallas_call | solution.py:427
  448.3 82.7 %last_backward.1 = (f32[256,1536]{1,0:T(8,128)}, f32[8,1536]{1,0:T(8,128)}, f32[192,2688]{1,0:T(8,128)}, f32[8,2304]{1,0:T(8,128)}, f32[8,1536]{1,0:T(8,128)}) custom-call(bf16[1024,1536]{1,0:T(8,128)(2,1)} %get-tuple-element.92.refs_0_, bf16[256,1536]{1,0:T(8,128)(2,1)} %refs_1_.1, f32[1,1536]{1,0:T(1,128)} %get-tuple-element.160.refs_2_, ...), custom_call_target="tpu_custom_call" | custom-call | tf_op jit(solution)/shard_map/last_backward/pallas_call | solution.py:1030
  531.0 0.7 slice_bitcast_fusion.10
  533.0 0.8 slice.133
  533.8 1.1 fusion.5
  534.9 0.7 copy.61
  539.5 1.9 fusion.3
  541.3 1.9 fusion.2
  543.2 3.1 multiply_add_fusion
  546.3 1.1 copy.76
  (68 shorter events, 8.5 us)
Async XLA Ops:
  7.2 6.1 %copy-start.3 = (bf16[2,192,768]{2,1,0:T(8,128)(2,1)S(1)}, bf16[2,192,768]{2,1,0:T(8,128)(2,1)}, u32[]{:S(2)}) copy-start(bf16[2,192,768]{2,1,0:T(8,128)(2,1)} %param.20) | copy-start | bytes 1769476
  7.2 6.1 %copy-start.4 = (bf16[2,192,768]{2,1,0:T(8,128)(2,1)S(1)}, bf16[2,192,768]{2,1,0:T(8,128)(2,1)}, u32[]{:S(2)}) copy-start(bf16[2,192,768]{2,1,0:T(8,128)(2,1)} %param.19) | copy-start | bytes 1769476
  7.2 218.2 %all-gather.2.cloned.1.call-start = ((), (), s32[]{:S(2)}) async-start(), calls=%async_computation.1 | async-start | bytes 3932160 | tf_op jit(solution)/shard_map/all_gather | solution.py:1218
  76.3 4.0 copy-start.8
  76.3 4.1 copy-start.10
  76.3 4.2 copy-start.9
  76.3 466.9 %reduce-scatter.2.cloned.1.call-start = ((), (), s32[]{:S(2)}) async-start(), calls=%async_computation.2 | async-start | bytes 3932160 | tf_op jit(solution)/shard_map/reduce_scatter | solution.py:1253
  79.0 3.7 copy-start.11
  79.0 3.7 copy-start.12
  79.0 4.3 copy-start.7
  84.0 27.1 %copy-start.5 = (bf16[192,256]{1,0:T(8,128)(2,1)S(1)}, bf16[192,256]{1,0:T(8,128)(2,1)}, u32[]{:S(2)}) copy-start(bf16[192,256]{1,0:T(8,128)(2,1)} %get-tuple-element.149) | copy-start | bytes 294916
  533.8 1.8 copy-start.6
  533.8 5.6 %copy-start = (f32[192,2688]{1,0:T(8,128)S(1)}, f32[192,2688]{1,0:T(8,128)}, u32[]{:S(2)}) copy-start(f32[192,2688]{1,0:T(8,128)} %get-tuple-element.106) | copy-start | bytes 6193156
  539.5 1.9 copy-start.1
  543.2 3.1 copy-start.2
Sparse Core Ops, SparseCore 0:
  76.4 73.7 all-gather.1
  255.2 59.3 reduce-scatter.1

commit v5 on v4

--- a/solution.py
+++ b/solution.py
@@ -244,9 +244,9 @@
 
 
 def bwd_kernel(
-    ready, gb_ref, e_ref, gate_ref, val_ref, valp_ref, st_ref, stp_ref, dt_ref, y_ref, ent_ref,
-    w_ref, vec_ref, cst_ref, tiny_ref, pick_ref,
-    dcat_ref, dpart_ref, gvec_ref, gst_ref, gdt_ref,
+    ready, gb_ref, e_ref, rows_ref, gate_ref, val_ref, valp_ref, st_ref, stp_ref, dt_ref, y_ref,
+    ent_ref, w_ref, vec_ref, cst_ref, tiny_ref, gain_ref, pick_ref,
+    dcat_ref, dpart_ref, gvec_ref, gst_ref, gdt_ref, ggain_ref,
     dstate, vpad, spad, dvpad, dspad,
 ):
     step = pl.program_id(0)
@@ -270,6 +270,7 @@
         gvec_ref[...] = jnp.zeros_like(gvec_ref)
         gst_ref[...] = jnp.zeros_like(gst_ref)
         gdt_ref[...] = jnp.zeros_like(gdt_ref)
+        ggain_ref[...] = jnp.zeros_like(ggain_ref)
 
     @pl.when(step > 0)
     def _():
@@ -399,9 +400,14 @@
     dpart = nt(dgate, wz_ref[...]) + nt(dvalb, wx_ref[...])
     dpart = dpart + nt(dstb, wbc_ref[...]) + nt(ddtb, wdt_ref[...])
     dpart_ref[...] = dpart.astype(BF)
-
-
-def backward_mix(gb, ready, e_rows, kept, packed, params, pick, l):
+    ggain_ref[0:1, :] += jnp.sum(rows_ref[...].astype(F32) * dpart, axis=0, keepdims=True)
+
+    @pl.when(step == blocks - 1)
+    def _():
+        ggain_ref[0:1, :] = ggain_ref[0:1, :] / gain_ref[0]
+
+
+def backward_mix(gb, ready, e_rows, rows, kept, packed, params, pick, l):
     gate, val, st, dt, y, ent = kept
     tokens, width = gb.shape[0], packed.shape[0]
     inner = params[0].shape[2]
@@ -423,6 +429,7 @@
         ((8, inner), F32, fixed(8, inner)),
         ((8, bc_width), F32, fixed(8, bc_width)),
         ((8, dt_width), F32, fixed(8, dt_width)),
+        ((8, width), F32, fixed(8, width)),
     ]
     return pl.pallas_call(
         functools.partial(bwd_kernel, ready),
@@ -430,6 +437,7 @@
         in_specs=[
             tok(gb.shape[1]),
             pl.BlockSpec((8, q), lambda i: (0, back(i))),
+            tok(width),
             tok(inner), tok(inner), halo(inner), tok(bc_width), halo(bc_width), tok(dt_width),
             tok(inner),
             pl.BlockSpec((1, half, inner), lambda i: (back(i), 0, 0)),
@@ -448,7 +456,7 @@
             dimension_semantics=("arbitrary",), vmem_limit_bytes=60 * MIB
         ),
         name="mix_backward",
-    )(gb, e_rows, gate, val, val, st, st, dt, y, ent, packed, *params, pick)
+    )(gb, e_rows, rows, gate, val, val, st, st, dt, y, ent, packed, *params, pick)
 
 
 class Step:
@@ -465,6 +473,7 @@
         self.late = False
         self.scale = False
         self.inner = False
+        self.layer = 0
         self.weights = 0
         self.grads = 0
         self.tail = 2
@@ -473,6 +482,7 @@
         self.sums = False
         self.bits = 0
         self.middle = None
+        self.lazy = ()
         self.__dict__.update(given)
 
 
@@ -485,6 +495,13 @@
 
 def when(condition):
     return pl.when(condition)
+
+
+def pack_weights(r, l):
+    start = 0
+    for part in (r.p_bc.at[l], r.p_dt.at[l], r.p_z.at[l], r.p_x.at[l], r.p_out.at[l]):
+        r.wown[:, start : start + part.shape[1]] = part[...]
+        start += part.shape[1]
 
 
 def comm_kernel(o, names, *refs):
@@ -496,6 +513,14 @@
     me = lax.axis_index("dp")
     own_bits = [(me // (1 << b)) % 2 for b in range(o.bits)]
     partner = [me + (1 - 2 * own_bits[b]) * (1 << b) for b in range(o.bits)]
+
+    lazy = []
+    for i, name in enumerate(o.lazy):
+        near = getattr(r, name + "_v")
+        lazy.append(pltpu.make_async_copy(getattr(r, name), near, r.lazy_sem.at[i]))
+        setattr(r, name, near)
+    for copy in lazy:
+        copy.start()
 
     barrier = pltpu.get_barrier_semaphore()
     for k in range(1, n):
@@ -698,7 +723,7 @@
                 fn(parity, j)
 
     def grad_items(tau):
-        @when(tau < o.grads)
+        @when((tau >= 0) & (tau < o.grads))
         def _():
             product(tau)
 
@@ -757,11 +782,10 @@
 
     line_groups, dp_groups = [], []
     if o.sums:
-        line_groups = [(r.lbank, r.lb_send, r.lb_recv)]
-        dp_groups = [(r.dbank, r.dbuf, r.db_send, r.db_recv)]
-        if r.gains:
-            line_groups.append((r.gbank, r.gb_send, r.gb_recv))
-            dp_groups.append((r.hbank, r.hbuf, r.hb_send, r.hb_recv))
+        line_groups = [(r.lbank, r.lb_send, r.lb_recv), (r.gbank, r.gb_send, r.gb_recv)]
+        dp_groups = [
+            (r.dbank, r.dbuf, r.db_send, r.db_recv), (r.hbank, r.hbuf, r.hb_send, r.hb_recv)
+        ]
 
     def sum_items(tau):
         @when(tau == 2)
@@ -773,8 +797,7 @@
                 r.dbank[0, :, off : off + v.shape[1]] = v[...]
                 off += v.shape[1]
             r.dbank[0, :, off:] = line_total(r.lbank)
-            if r.gains:
-                r.hbank[0] = line_total(r.gbank)
+            r.hbank[0] = line_total(r.gbank)
             for g in dp_groups:
                 double(*g, 0).start()
 
@@ -826,6 +849,7 @@
         for k in range(1, n):
             square_copy(k).start()
     if o.weights:
+        pack_weights(r, o.layer)
         own_weights().start()
     if o.scale:
         total = spot_of(t, r.ssq)[...]
@@ -847,12 +871,17 @@
     if o.weights:
         ends.append((o.weights + 1) // 2 + o.bits)
     if o.grads:
-        ends.append(o.grads + grad_lag(o.bits))
-        ends.append(grad_lag(o.bits) + 4)
+        ends.append(1 + o.grads + grad_lag(o.bits))
+        ends.append(grad_lag(o.bits) + 5)
     if o.sums:
         ends.append(4 + o.bits)
 
     def iteration(tau, _):
+        if lazy:
+            @when(tau == 1)
+            def _():
+                for copy in lazy:
+                    copy.wait()
         if o.partial:
             for side in range(2):
                 c = tau - o.hop * (t if side == 0 else n - 1 - t)
@@ -890,18 +919,14 @@
                 own_weights().wait()
             weight_items(tau)
         if o.grads:
-            grad_items(tau)
-            state_items(tau)
+            grad_items(tau - 1)
+            state_items(tau - 1)
         if o.sums:
             sum_items(tau)
         return 0
 
     lax.fori_loop(0, max(ends), iteration, 0)
 
-    if o.sums:
-        r.jbank[t] = r.ggain[0:1, :]
-        for k in range(1, n):
-            share(r.jbank, r.jb_send, r.jb_recv, k).start()
     if o.inner:
         spot_of(t, r.inner)[...] = r.icol[...].T[0:8, :]
         for k in range(1, n):
@@ -911,20 +936,13 @@
         for k in range(1, n):
             inner_copy(k).wait_send()
     if o.sums:
-        last = (r.kbank, r.kbuf, r.kb_send, r.kb_recv)
-        shared(r.jbank, r.jb_send, r.jb_recv)
-        r.kbank[0] = line_total(r.jbank)
-        for b in range(o.bits):
-            double(*last, b).start()
-            doubled(*last, b)
         r.sums[...] = r.dbank[o.bits]
-        r.gain_sums[0:1, :] = r.kbank[o.bits]
         for i, v in enumerate(r.gains):
-            r.gain_sums[i + 1 : i + 2, :] = r.hbank[o.bits, :, lanes(i, v)]
-        for g in line_groups + [(r.jbank, r.jb_send, r.jb_recv)]:
+            r.gain_sums[i : i + 1, :] = r.hbank[o.bits, :, lanes(i, v)]
+        for g in line_groups:
             for k in range(1, n):
                 share(*g, k).wait_send()
-        for g in dp_groups + [last]:
+        for g in dp_groups:
             for b in range(o.bits):
                 double(*g, b).wait_send()
     if o.grads:
@@ -968,6 +986,12 @@
 def comm_call(o, name, collective, inputs, outputs, **scratch):
     n, count, rows, width = o.line, o.chunks, o.rows, o.width
     dma = pltpu.SemaphoreType.DMA
+    if o.lazy:
+        for key in o.lazy:
+            value = inputs[key][0]
+            inputs[key] = (value, pl.ANY)
+            scratch[key + "_v"] = pltpu.VMEM(value.shape, value.dtype)
+        scratch.update(lazy_sem=dma((len(o.lazy),)))
     if o.partial:
         scratch.update(
             rbuf=pltpu.VMEM((n, rows, width), BF),
@@ -987,7 +1011,10 @@
             icol=pltpu.VMEM((rows, 128), F32), in_send=dma((n - 1,)), in_recv=dma((n - 1,))
         )
     if o.weights:
+        rows_of_pack = inputs["p_bc"][0].shape[1]
+        pack_width = sum(v[0].shape[2] for k, v in inputs.items() if k.startswith("p_"))
         scratch.update(
+            wown=pltpu.VMEM((rows_of_pack, pack_width), BF),
             wl_sem=dma(()),
             wg_send=dma((o.bits, o.weights)),
             wg_recv=dma((o.bits, o.weights)),
@@ -1015,17 +1042,15 @@
             return sum(v[0].shape[1] for k, v in inputs.items() if k.startswith(start))
 
         lined, early, gains = lanes_of("lsum"), lanes_of("esum"), lanes_of("gsum")
-        for name_of, tall, line_width, dp_width in (
-            ("lb db", 8, lined, lined + early), ("gb hb", 1, gains, gains), ("jb kb", 1, width, width)
+        for one, two, tall, line_width, dp_width in (
+            ("lb", "db", 8, lined, lined + early), ("gb", "hb", 1, gains, gains)
         ):
-            if line_width:
-                one, two = name_of.split()
-                scratch[one + "ank"] = pltpu.VMEM((n, tall, line_width), F32)
-                scratch[two + "ank"] = pltpu.VMEM((o.bits + 1, tall, dp_width), F32)
-                scratch[two + "uf"] = pltpu.VMEM((o.bits, tall, dp_width), F32)
-                for key, size in ((one, n - 1), (two, o.bits)):
-                    scratch[key + "_send"] = dma((size,))
-                    scratch[key + "_recv"] = dma((size,))
+            scratch[one + "ank"] = pltpu.VMEM((n, tall, line_width), F32)
+            scratch[two + "ank"] = pltpu.VMEM((o.bits + 1, tall, dp_width), F32)
+            scratch[two + "uf"] = pltpu.VMEM((o.bits, tall, dp_width), F32)
+            for key, size in ((one, n - 1), (two, o.bits)):
+                scratch[key + "_send"] = dma((size,))
+                scratch[key + "_recv"] = dma((size,))
     names = [*inputs, *outputs, *scratch]
     out = pl.pallas_call(
         functools.partial(comm_kernel, o, names),
@@ -1041,7 +1066,7 @@
     return dict(zip(outputs, out))
 
 
-def meet_kernel(n, inner_all, own_ref, out_ref, bank, send, recv):
+def meet_kernel(n, inner_all, own_ref, out_ref, scale_ref, bank, send, recv):
     t = lax.axis_index("tensor")
     barrier = pltpu.get_barrier_semaphore()
     for k in range(1, n):
@@ -1069,6 +1094,9 @@
     row = lax.broadcasted_iota(jnp.int32, total.shape, 0)
     e = scale * scale * scale * (total[1:2, :] / inner_all)
     out_ref[...] = jnp.where(row == 0, e, scale)
+    rows = scale_ref.shape[0]
+    mine = out_ref[:, pl.ds(pl.multiple_of(t * rows, rows), rows)].T
+    scale_ref[...] = jnp.broadcast_to(mine[:, 1:2], scale_ref.shape)
     for copy in copies:
         copy.wait_send()
 
@@ -1079,8 +1107,11 @@
     return pl.pallas_call(
         functools.partial(meet_kernel, n, inner_all),
         in_specs=[vmem],
-        out_specs=vmem,
-        out_shape=jax.ShapeDtypeStruct(own.shape, F32),
+        out_specs=[vmem, vmem],
+        out_shape=[
+            jax.ShapeDtypeStruct(own.shape, F32),
+            jax.ShapeDtypeStruct((own.shape[1] // n, 128), F32),
+        ],
         scratch_shapes=[pltpu.VMEM((n,) + own.shape, F32), dma((n - 1,)), dma((n - 1,))],
         compiler_params=pltpu.CompilerParams(collective_id=collective, has_side_effects=True),
         name="turn_around",
@@ -1109,13 +1140,11 @@
 
 def backward_middle(inner_all, r, at, total):
     if at is None:
-        r.ggain[...] = jnp.zeros_like(r.ggain)
         return None
     res = r.res[at, :].astype(F32)
     width = res.shape[1]
     r1 = lax.rsqrt(jnp.mean(res * res, axis=1, keepdims=True) + EPSILON)
     hat = res * r1
-    r.ggain[0:1, :] += jnp.sum(hat * total, axis=0, keepdims=True)
     dn = total * r.gain[...]
     cross = jnp.sum(dn * hat, axis=1, keepdims=True) / width
     grad = r.grad_in[at, :].astype(F32) + r1 * (dn - hat * cross)
@@ -1170,27 +1199,23 @@
     small = jnp.concatenate([conv_state.reshape(layers, -1), conv_state_bias], axis=1)
     small = jnp.pad(small, ((0, 0), (0, shard_rows - small.shape[1])))
     extra = jnp.stack([norm_gain, small], axis=1).reshape(2 * layers, shard_rows).T
-    packs = []
-    for l in range(layers):
-        packs.append(
-            jnp.concatenate(
-                [
-                    proj_bc[l],
-                    proj_dt[l],
-                    extra,
-                    jnp.zeros((shard_rows, 128 - heads - 2 * layers), BF),
-                    proj_z[l],
-                    proj_x[l],
-                    proj_out[l].T,
-                ],
-                axis=1,
-            )
-        )
+    step_block = jnp.concatenate(
+        [
+            proj_dt,
+            jnp.broadcast_to(extra[None], (layers,) + extra.shape),
+            jnp.zeros((layers, shard_rows, 128 - heads - 2 * layers), BF),
+        ],
+        axis=2,
+    )
+    out_turned = jnp.transpose(proj_out, (0, 2, 1))
     full_shape = ((2,) * bits) + (shard_rows, packed_width)
     common = dict(rows=rows_own, width=width, line=tensor_count, bits=bits)
 
-    def weight_io(l):
-        return dict(wown=(packs[l], vmem)), dict(wfull=(full_shape, BF, far))
+    weight_in = dict(
+        p_bc=(proj_bc, vmem), p_dt=(step_block, vmem), p_z=(proj_z, vmem), p_x=(proj_x, vmem),
+        p_out=(out_turned, vmem),
+    )
+    weight_out = dict(wfull=(full_shape, BF, far))
 
     vec = jnp.concatenate(
         [
@@ -1206,12 +1231,11 @@
     pick = (jnp.arange(inner)[:, None] // WIDTH == jnp.arange(128)[None, :]).astype(BF)
 
     whole_rows, own_rows = ((tokens, width), BF, vmem), ((rows_own, width), F32, vmem)
-    win, wout = weight_io(0)
     got = comm_call(
-        Step(gather=True, payload=plain_payload, weights=row_chunks, **common),
+        Step(gather=True, payload=plain_payload, weights=row_chunks, layer=0, **common),
         "gather_first", 1,
-        dict(own=(hidden_in, vmem), **win),
-        dict(full=whole_rows, **wout),
+        dict(own=(hidden_in, vmem), **weight_in),
+        dict(full=whole_rows, **weight_out),
     )
     x_rows = got["full"]
     out_grad, x_rows = lax.optimization_barrier((out_grad, x_rows))
@@ -1230,17 +1254,16 @@
     saved, rows = [out[:6]], [out[8]]
     residuals, branches, r2s = [hidden_in], [], []
     for l in range(layers - 1):
-        win, wout = weight_io(l + 1)
         got = comm_call(
             Step(
                 partial=True, gather=True, late=True, scale=inner_all, middle=forward_middle,
-                weights=row_chunks, **common,
+                weights=row_chunks, layer=l + 1, **common,
             ),
             "between_forward", 2 + l,
             dict(part=(out[6], vmem), ssq=(out[7], vmem), res=(residuals[l], vmem),
-                 gain=(gain_rows[l + 1], vmem), **win),
+                 gain=(gain_rows[l + 1], vmem), **weight_in),
             dict(full=whole_rows, branch=own_rows, res_out=own_rows,
-                 r2=((rows_own, 128), F32, vmem), **wout),
+                 r2=((rows_own, 128), F32, vmem), **weight_out),
         )
         rows.append(got["full"])
         branches.append(got["branch"])
@@ -1251,20 +1274,18 @@
         out = forward_mix(rows[-1], packed[-1], params + (gain_rows,), l + 1, gb)
         saved.append(out[:6])
     total = lax.psum_scatter(out[6], "tensor", scatter_dimension=0, tiled=True)
-    token_rows = meet(out[7], tensor_count, inner_all, 16)
-    r2_own = lax.dynamic_slice_in_dim(
-        token_rows[1], lax.axis_index("tensor") * rows_own, rows_own, 0
-    )
-    hidden_out = residuals[-1].astype(F32) + r2_own[:, None] * total.astype(F32)
+    token_rows, r2_own = meet(out[7], tensor_count, inner_all, 16)
+    hidden_out = residuals[-1].astype(F32) + r2_own[:, 0:1] * total.astype(F32)
     product = out[8]
     gradient = out_grad
     scattered, summed, gain_grads = [None] * layers, [None] * layers, [None] * layers
     for l in reversed(range(layers)):
         last = l == layers - 1
         dcat, dpart, *small_grads = backward_mix(
-            product if last else grad_rows, last, token_rows, saved[l], packed[l], params, pick, l
-        )
-        summed[l] = small_grads
+            product if last else grad_rows, last, token_rows, rows[l], saved[l], packed[l],
+            params + (gain_rows,), pick, l,
+        )
+        *summed[l], gain_grads[l] = small_grads
         more = l > 0
         inputs = dict(
             part=(dpart, vmem), res=(residuals[l], vmem), gain=(gain_rows[l], vmem),
@@ -1272,7 +1293,7 @@
             right=(dcat, vmem),
         )
         outputs = dict(
-            grad_out=own_rows, ggain=((8, width), F32, vmem),
+            grad_out=own_rows,
             gout=((shard_rows, packed_width), F32, vmem),
         )
         if more:
@@ -1283,7 +1304,7 @@
                 gvec, gst, gdt = summed[i]
                 inputs["esum%d" % i], inputs["esum_%d" % i] = (gvec, vmem), (gdt, vmem)
                 inputs["lsum%d" % i] = (gst, vmem)
-            for i in range(1, layers):
+            for i in range(layers):
                 inputs["gsum%d" % i] = (gain_grads[i], vmem)
             early = sum(v.shape[1] for i in range(layers) for v in summed[i])
             outputs.update(
@@ -1293,12 +1314,13 @@
             Step(
                 partial=True, gather=more, late=more, inner=more, grads=column_chunks,
                 states=bc_width, sums=not more,
+                lazy=("right", "lrows", "lgrad", "res", "grad_in") + (("branch",) if more else ()),
                 middle=functools.partial(backward_middle, inner_all if more else None), **common,
             ),
             "between_backward" if more else "last_backward", 17 + l, inputs, outputs,
         )
         gradient = got["grad_out"]
-        scattered[l], gain_grads[l] = got["gout"], got["ggain"]
+        scattered[l] = got["gout"]
         if more:
             grad_rows, token_rows = got["full"], got["inner"]
     gout = jnp.stack(scattered)

time: 562 us -> 550 us (0.979)
  local copies, waits for them, and re-layouts: 22.3 us -> 16.1 us
  Pallas kernels: 504 us -> 498 us
    pallas_call x4, Pallas kernels: 362 us -> 352 us  [comm_call(): pl.pallas_call(functools.partial(comm_kernel, o, names), in_specs=[pl.Blo...]
where the time goes in v5:
time: 550 us; the launch traced here: 543 us
  Pallas kernels  498 us (91%)
  local copies, waits for them, and re-layouts  16.1 us (3%)
  between operations  14.8 us (3%)
  other arithmetic  13.9 us (3%)
    pallas_call x4, Pallas kernels, comm_call(): pl.pallas_call(functools.partial(comm_kernel, o, names), in_specs=[pl.Blo...  352 us
    pallas_call x2, Pallas kernels, backward_mix(): pl.pallas_call(functools.partial(bwd_kernel, ready), grid=(blocks,), in_s...  81 us
    pallas_call x2, Pallas kernels, forward_mix(): pl.pallas_call(functools.partial(fwd_kernel, first, last), grid=(blocks,)...  56.8 us
  transfers between devices with their start and end apart: 2, of which 0 were waited for; matrix products, arithmetic and copies ran while one was open for 4% of the time, Pallas kernels for 75%

profile of v5, /device:TPU:0, one launch (start us, length us, event | category | flops | bytes accessed | tf_op | source)
XLA Modules:
  0.0 542.6 jit_solution(14922367038742098378)
XLA Ops:
  7.2 0.8 reshape.95
  8.0 0.7 fusion.17
  8.7 0.7 pad_maximum_fusion.2
  9.5 0.9 copy.46
  10.5 0.7 maximum_maximum_fusion.refs_2_.refs_5_
  11.2 61.6 %gather_first.1 = (bf16[1024,1536]{1,0:T(8,128)(2,1)}, bf16[2,2,2,192,2688]{4,3,2,1,0:T(8,128)(2,1)}) custom-call(bf16[256,1536]{1,0:T(8,128)(2,1)} %refs_1_.3, bf16[2,192,256]{2,1,0:T(8,128)(2,1)} %refs_4_.3, bf16[2,192,128]{2,1,0:T(8,128)(2,1)} %maximum_maximum_fusion.refs_2_.refs_5_, bf16[2,192,768]{2,1,0:T(8,128)(2,1)} %refs_6_.1, ...), custom_call_target="tpu_custom_call" | custom-call | tf_op jit(solution)/shard_map/gather_first/pallas_call | solution.py:1055
  72.9 1.2 slice.113
  74.1 1.4 slice.87
  75.5 1.3 slice.89
  77.5 0.7 reshape.103.cst_ref
  79.7 0.7 maximum_convert_fusion.vec_ref
  80.4 27.1 %mix_forward.2 = (f32[1024,768]{1,0:T(8,128)}, f32[1024,768]{1,0:T(8,128)}, f32[1024,256]{1,0:T(8,128)}, f32[1024,128]{1,0:T(8,128)}, f32[1024,768]{1,0:T(8,128)...) custom-call(bf16[1024,1536]{1,0:T(8,128)(2,1)} %get-tuple-element.66.row, ...), custom_call_target="tpu_custom_call" | custom-call | tf_op jit(solution)/shard_map/mix_forward/pallas_call | solution.py:226
  108.1 114.0 %between_forward.1 = (bf16[1024,1536]{1,0:T(8,128)(2,1)}, f32[256,1536]{1,0:T(8,128)}, f32[256,1536]{1,0:T(8,128)}, f32[256,128]{1,0:T(8,128)}, bf16[2,2,2,192,2688]{4,3,2,1,0:T(8,128)(2,1)}) custom-call(bf16[1024,1536]{1,0:T(8,128)(2,1)} %get-tuple-element.68.refs_0_, f32[8,1024]{1,0:T(8,128)} %get-tuple-element.69.refs_1_, bf16[256,1536]{1,0:T(8,128)(2,1)} %refs_1_.3, ...), custom_call_target="tpu_custom_call" | custom-call | tf_op jit(solution)/shard_map/between_forward/pallas_call | solution.py:1055
  222.2 29.6 %mix_forward.3 = (f32[1024,768]{1,0:T(8,128)}, f32[1024,768]{1,0:T(8,128)}, f32[1024,256]{1,0:T(8,128)}, f32[1024,128]{1,0:T(8,128)}, f32[1024,768]{1,0:T(8,128)...) custom-call(bf16[1024,1536]{1,0:T(8,128)(2,1)} %get-tuple-element.71.rows_ref.r, ...), custom_call_target="tpu_custom_call" | custom-call | tf_op jit(solution)/shard_map/mix_forward/pallas_call | solution.py:226
  251.9 0.8 fusion.4.pick_ref
  252.7 7.5 %turn_around.1 = (f32[8,1024]{1,0:T(8,128)}, f32[256,128]{1,0:T(8,128)}) custom-call(f32[8,1024]{1,0:T(8,128)} %get-tuple-element.74.own_ref), custom_call_target="tpu_custom_call" | custom-call | tf_op jit(solution)/shard_map/turn_around/pallas_call | solution.py:1107
  260.2 39.8 %mix_backward.2 = (bf16[1024,2688]{1,0:T(8,128)(2,1)}, bf16[1024,1536]{1,0:T(8,128)(2,1)}, f32[8,768]{1,0:T(8,128)}, f32[8,256]{1,0:T(8,128)}, f32[8,128]{1,0:T(8,128)}, /*index=5*/f32[8,1536]{1,0:T(8,128)}) custom-call(f32[1024,768]{1,0:T(8,128)} %get-tuple-element.77.gb_ref, f32[8,1024]{1,0:T(8,128)} %get-tuple-element.78.e_ref, ...), custom_call_target="tpu_custom_call" | custom-call | tf_op jit(solution)/shard_map/mix_backward/pallas_call | solution.py:434
  300.0 105.4 %between_backward.1 = (f32[256,1536]{1,0:T(8,128)}, f32[192,2688]{1,0:T(8,128)}, bf16[1024,1536]{1,0:T(8,128)(2,1)}, f32[8,1024]{1,0:T(8,128)}) custom-call(bf16[1024,1536]{1,0:T(8,128)(2,1)} %get-tuple-element.85.refs_0_, f32[256,1536]{1,0:T(8,128)} %get-tuple-element.70.refs_1_, f32[1,1536]{1,0:T(1,128)} %get-tuple-element.159.refs_3_.refs_2_, ...), custom_call_target="tpu_custom_call" | custom-call | tf_op jit(solution)/shard_map/between_backward/pallas_call | solution.py:1055
  405.5 41.1 %mix_backward.3 = (bf16[1024,2688]{1,0:T(8,128)(2,1)}, bf16[1024,1536]{1,0:T(8,128)(2,1)}, f32[8,768]{1,0:T(8,128)}, f32[8,256]{1,0:T(8,128)}, f32[8,128]{1,0:T(8,128)}, /*index=5*/f32[8,1536]{1,0:T(8,128)}) custom-call(bf16[1024,1536]{1,0:T(8,128)(2,1)} %get-tuple-element.89.gb_ref.refs_5_, f32[8,1024]{1,0:T(8,128)} %get-tuple-element.90.e_ref, ...), custom_call_target="tpu_custom_call" | custom-call | tf_op jit(solution)/shard_map/mix_backward/pallas_call | solution.py:434
  446.6 71.4 %last_backward.1 = (f32[256,1536]{1,0:T(8,128)}, f32[192,2688]{1,0:T(8,128)}, f32[8,2304]{1,0:T(8,128)}, f32[8,1536]{1,0:T(8,128)}) custom-call(bf16[1024,1536]{1,0:T(8,128)(2,1)} %get-tuple-element.98.refs_0_, bf16[256,1536]{1,0:T(8,128)(2,1)} %refs_1_.3, f32[1,1536]{1,0:T(1,128)} %get-tuple-element.158.refs_2_, f32[256,1536]{1,0:T(8,128)} %get-tuple-element.99.refs_3_, ...), custom_call_target="tpu_custom_call" | custom-call | tf_op jit(solution)/shard_map/last_backward/pallas_call | solution.py:1055
  518.0 0.7 slice_bitcast_fusion.2
  520.0 0.8 slice.93
  520.8 0.8 slice_bitcast_fusion
  521.7 1.1 fusion.5
  522.8 0.7 copy.62
  523.5 0.6 reduce_sum.9
  524.2 0.7 slice_bitcast_fusion.5
  525.4 0.7 constant_dynamic-slice_fusion
  526.8 1.9 fusion.3
  528.7 1.9 fusion.2
  531.1 3.0 multiply_add_fusion
  534.1 1.1 copy.73
  (56 shorter events, 6.4 us)
Async XLA Ops:
  7.2 215.0 %all-gather.2.cloned.1.call-start = ((), (), s32[]{:S(2)}) async-start(), calls=%async_computation.1 | async-start | bytes 3932160 | tf_op jit(solution)/shard_map/all_gather | solution.py:1242
  72.8 4.0 copy-start.5
  72.8 4.1 copy-start.6
  72.9 4.1 copy-start.7
  72.9 458.3 %reduce-scatter.2.cloned.1.call-start = ((), (), s32[]{:S(2)}) async-start(), calls=%async_computation.2 | async-start | bytes 3932160 | tf_op jit(solution)/shard_map/reduce_scatter | solution.py:1276
  75.5 3.6 copy-start.8
  75.5 3.6 copy-start.9
  75.5 4.2 copy-start.4
  521.7 5.0 copy-start.3
  521.7 5.1 copy-start
  526.8 1.9 copy-start.1
  530.5 3.6 copy-start.2
Sparse Core Ops, SparseCore 0:
  72.9 75.1 all-gather.1
  252.0 63.0 reduce-scatter.1

commit v6 on v5

--- a/solution.py
+++ b/solution.py
@@ -94,7 +94,7 @@
 ):
     if last:
         gb_ref, *rest = rest
-    gate_ref, val_ref, st_ref, dt_ref, y_ref, ent_ref, part_ref, ssq_ref, *rest = rest
+    gate_ref, val_ref, st_ref, dt_ref, y_ref, ent_ref, pre_ref, part_ref, ssq_ref, *rest = rest
     if first:
         normed_ref, *rest = rest
     if last:
@@ -124,7 +124,7 @@
     if first:
         rows = rows.astype(F32)
         r1 = lax.rsqrt(jnp.mean(rows * rows, axis=1, keepdims=True) + EPSILON)
-        rows = (rows * r1 * gain_ref[0]).astype(BF)
+        rows = (rows * r1 * gain_ref[0:1, :]).astype(BF)
         normed_ref[...] = rows
     gate_ref[...] = nn(rows, wz_ref[...])
     val = nn(rows, wx_ref[...])
@@ -136,7 +136,9 @@
     dt_in = nn(rows, wdt_ref[...])
     dt_ref[...] = dt_in
 
-    _, v = silu_parts(conv_pre(vpad, cv_ref, cvb_ref[...], length))
+    pre = conv_pre(vpad, cv_ref, cvb_ref[...], length)
+    pre_ref[...] = pre
+    _, v = silu_parts(pre)
     _, bc = silu_parts(conv_pre(spad, cs_ref, csb_ref[...], length))
     half = bc.shape[1] // 2
     bb = bc[:, :half].astype(BF)
@@ -195,8 +197,8 @@
 def layer_specs(params, l):
     return [
         pl.BlockSpec((1,) + p.shape[1:], lambda i: (l, 0, 0), pipeline_mode=pl.Buffered(1))
-        for p in params
-    ]
+        for p in params[:-1]
+    ] + [whole(params[-1].shape)]
 
 
 def forward_mix(rows, packed, params, l, gb=None):
@@ -216,6 +218,7 @@
         ((tokens, dt_width), F32, tok(dt_width)),
         ((tokens, inner), F32, tok(inner)),
         ((blocks, half, inner), F32, pl.BlockSpec((1, half, inner), lambda i: (i, 0, 0))),
+        ((tokens, inner), F32, tok(inner)),
         ((tokens, width), BF, tok(width)),
         ((8, tokens), F32, pl.BlockSpec((8, q), lambda i: (0, i))),
     ]
@@ -244,11 +247,16 @@
 
 
 def bwd_kernel(
-    ready, gb_ref, e_ref, rows_ref, gate_ref, val_ref, valp_ref, st_ref, stp_ref, dt_ref, y_ref,
-    ent_ref, w_ref, vec_ref, cst_ref, tiny_ref, gain_ref, pick_ref,
-    dcat_ref, dpart_ref, gvec_ref, gst_ref, gdt_ref, ggain_ref,
-    dstate, vpad, spad, dvpad, dspad,
+    ready, layer, gb_ref, e_ref, rows_ref, gate_ref, val_ref, st_ref, stp_ref, dt_ref, y_ref,
+    ent_ref, pre_ref, w_ref, vec_ref, cst_ref, tiny_ref, gain_ref, pick_ref, *rest,
 ):
+    if not ready:
+        res_ref, total_ref, scale_ref, *rest = rest
+    dcat_ref, dpart_ref, gvec_ref, gst_ref, gdt_ref, ggain_ref, *rest = rest
+    if not ready:
+        hidden_ref, *rest = rest
+        hidden_ref[...] = res_ref[...] + scale_ref[:, 0:1] * total_ref[...].astype(F32)
+    dstate, spad, dvpad, dspad = rest
     step = pl.program_id(0)
     blocks = pl.num_programs(0)
     length = gb_ref.shape[0]
@@ -278,12 +286,10 @@
         dspad[length : length + 8, :] = dspad[0:8, :]
 
     first = step == blocks - 1
-    vpad[0:8, :] = jnp.where(first, 0.0, valp_ref[...])
     spad[0:8, :] = jnp.where(first, 0.0, stp_ref[...])
-    vpad[8 : length + 8, :] = val_ref[...]
     spad[8 : length + 8, :] = st_ref[...]
 
-    pre_v = conv_pre(vpad, cv_ref, cvb_ref[...], length)
+    pre_v = pre_ref[...]
     sig_v, v = silu_parts(pre_v)
     pre_s = conv_pre(spad, cs_ref, csb_ref[...], length)
     sig_s, bc = silu_parts(pre_s)
@@ -374,11 +380,11 @@
     dpre_v = (skip * dy + dt_x * dx) * (sig_v * (1.0 + pre_v * (1.0 - sig_v)))
     dvpad[0:length, :] = dpre_v
     dval = jnp.zeros((length, inner), F32)
+    val = val_ref[...]
     for k in range(4):
-        dval = dval + cv_ref[k : k + 1, :] * dvpad[pl.ds(3 - k, length), :]
-        gvec_ref[k : k + 1, :] += jnp.sum(
-            dpre_v * vpad[pl.ds(5 + k, length), :], axis=0, keepdims=True
-        )
+        later = dvpad[pl.ds(3 - k, length), :]
+        dval = dval + cv_ref[k : k + 1, :] * later
+        gvec_ref[k : k + 1, :] += jnp.sum(later * val, axis=0, keepdims=True)
     gvec_ref[4:5, :] += jnp.sum(dpre_v, axis=0, keepdims=True)
     gvec_ref[5:6, :] += jnp.sum(gated * dm, axis=0, keepdims=True)
     gvec_ref[6:7, :] += jnp.sum(dy * v, axis=0, keepdims=True)
@@ -389,11 +395,11 @@
     dpre_s = dbc * (sig_s * (1.0 + pre_s * (1.0 - sig_s)))
     dspad[0:length, :] = dpre_s
     dst = jnp.zeros((length, bc_width), F32)
+    st = st_ref[...]
     for k in range(4):
-        dst = dst + cs_ref[k : k + 1, :] * dspad[pl.ds(3 - k, length), :]
-        gst_ref[k : k + 1, :] += jnp.sum(
-            dpre_s * spad[pl.ds(5 + k, length), :], axis=0, keepdims=True
-        )
+        later = dspad[pl.ds(3 - k, length), :]
+        dst = dst + cs_ref[k : k + 1, :] * later
+        gst_ref[k : k + 1, :] += jnp.sum(later * st, axis=0, keepdims=True)
     gst_ref[4:5, :] += jnp.sum(dpre_s, axis=0, keepdims=True)
     dstb = dst.astype(BF)
     dst_ref[...] = dstb
@@ -404,11 +410,11 @@
 
     @pl.when(step == blocks - 1)
     def _():
-        ggain_ref[0:1, :] = ggain_ref[0:1, :] / gain_ref[0]
-
-
-def backward_mix(gb, ready, e_rows, rows, kept, packed, params, pick, l):
-    gate, val, st, dt, y, ent = kept
+        ggain_ref[0:1, :] = ggain_ref[0:1, :] / gain_ref[2 * layer : 2 * layer + 1, :]
+
+
+def backward_mix(gb, ready, e_rows, rows, kept, packed, params, pick, l, last=()):
+    gate, val, st, dt, y, ent, pre = kept
     tokens, width = gb.shape[0], packed.shape[0]
     inner = params[0].shape[2]
     bc_width = params[1].shape[2]
@@ -431,23 +437,26 @@
         ((8, dt_width), F32, fixed(8, dt_width)),
         ((8, width), F32, fixed(8, width)),
     ]
+    few = [pl.BlockSpec((v.shape[0] // blocks, v.shape[1]), lambda i: (i, 0)) for v in last]
+    if last:
+        outs.append((last[0].shape, F32, few[0]))
     return pl.pallas_call(
-        functools.partial(bwd_kernel, ready),
+        functools.partial(bwd_kernel, ready, l),
         grid=(blocks,),
         in_specs=[
             tok(gb.shape[1]),
             pl.BlockSpec((8, q), lambda i: (0, back(i))),
             tok(width),
-            tok(inner), tok(inner), halo(inner), tok(bc_width), halo(bc_width), tok(dt_width),
+            tok(inner), tok(inner), tok(bc_width), halo(bc_width), tok(dt_width),
             tok(inner),
             pl.BlockSpec((1, half, inner), lambda i: (back(i), 0, 0)),
+            tok(inner),
         ]
-        + [whole(packed.shape)] + layer_specs(params, l) + [whole(pick.shape)],
+        + [whole(packed.shape)] + layer_specs(params, l) + [whole(pick.shape)] + few,
         out_specs=[o[2] for o in outs],
         out_shape=[jax.ShapeDtypeStruct(o[0], o[1]) for o in outs],
         scratch_shapes=[
             pltpu.VMEM((half, inner), F32),
-            pltpu.VMEM((q + 8, inner), F32),
             pltpu.VMEM((q + 8, bc_width), F32),
             pltpu.VMEM((q + 8, inner), F32),
             pltpu.VMEM((q + 8, bc_width), F32),
@@ -456,7 +465,7 @@
             dimension_semantics=("arbitrary",), vmem_limit_bytes=60 * MIB
         ),
         name="mix_backward",
-    )(gb, e_rows, rows, gate, val, val, st, st, dt, y, ent, packed, *params, pick)
+    )(gb, e_rows, rows, gate, val, st, st, dt, y, ent, pre, packed, *params, pick, *last)
 
 
 class Step:
@@ -474,6 +483,8 @@
         self.scale = False
         self.inner = False
         self.layer = 0
+        self.small = 0
+        self.gain_row = 0
         self.weights = 0
         self.grads = 0
         self.tail = 2
@@ -506,6 +517,7 @@
 
 def comm_kernel(o, names, *refs):
     r = types.SimpleNamespace(**dict(zip(names, refs)))
+    r.gain_row = slice(o.gain_row, o.gain_row + 1)
     r.gbuf = [v for k, v in zip(names, refs) if k.startswith("gbuf")]
     n, count, rows = o.line, o.chunks, o.rows
     size = rows // count
@@ -651,6 +663,25 @@
             src, spot, r.wg_send.at[stage, j], r.wg_recv.at[stage, j],
             {"dp": partner[order[stage]]},
         )
+
+    def small_columns():
+        lanes_at = pl.ds(o.small // 128 * 128, 128)
+        return pltpu.make_async_copy(
+            r.wfull.at[(*spots(range(o.bits)), slice(None), lanes_at)], r.columns, r.small_sem
+        )
+
+    def small_items(tau):
+        done = (o.weights + 1) // 2 + o.bits
+
+        @when(tau == done)
+        def _():
+            small_columns().start()
+
+        @when(tau == done + 1)
+        def _():
+            small_columns().wait()
+            turned = r.columns[...].reshape(o.width, 128).astype(F32).T
+            r.small[...] = turned[o.small % 128 : o.small % 128 + 8, :]
 
     def own_weights():
         return pltpu.make_async_copy(r.wown, r.wfull.at[spots([])], r.wl_sem)
@@ -699,22 +730,21 @@
             {"dp": partner[order[stage]]},
         )
 
-    def product(j):
+    def product(j, i):
         slab = o.width // 2
         inner_shape = (2,) * (o.bits - 1) + (slab >> (o.bits - 1), WCHUNK)
 
-        def slabs(left):
-            for i in range(2):
-                out = tn(left[:, pl.ds(i * slab, slab)], r.right[:, cols(j)])
-                r.grad[j, i] = out.astype(BF).reshape(inner_shape)
-
-        @when(j < o.grads - o.tail)
+        def one(left):
+            out = tn(left[:, pl.ds(i * slab, slab)], r.right[:, cols(j)])
+            r.grad[j, i] = out.astype(BF).reshape(inner_shape)
+
+        @when((j >= 0) & (j < o.grads - o.tail))
         def _():
-            slabs(r.lrows)
-
-        @when(j >= o.grads - o.tail)
+            one(r.lrows)
+
+        @when((j >= o.grads - o.tail) & (j < o.grads))
         def _():
-            slabs(r.lgrad)
+            one(r.lgrad)
 
     def each_chunk(j, fn):
         for parity in range(2):
@@ -723,9 +753,7 @@
                 fn(parity, j)
 
     def grad_items(tau):
-        @when((tau >= 0) & (tau < o.grads))
-        def _():
-            product(tau)
+        product(tau, 1)
 
         def first(parity, j):
             grad_copy(parity, 0, j).start()
@@ -869,7 +897,7 @@
     elif o.gather:
         ends.append(count + o.pass_hop * (n - 1))
     if o.weights:
-        ends.append((o.weights + 1) // 2 + o.bits)
+        ends.append((o.weights + 1) // 2 + o.bits + (2 if o.small else 0))
     if o.grads:
         ends.append(1 + o.grads + grad_lag(o.bits))
         ends.append(grad_lag(o.bits) + 5)
@@ -882,6 +910,8 @@
             def _():
                 for copy in lazy:
                     copy.wait()
+        if o.grads:
+            product(tau - 1, 0)
         if o.partial:
             for side in range(2):
                 c = tau - o.hop * (t if side == 0 else n - 1 - t)
@@ -918,6 +948,8 @@
             def _():
                 own_weights().wait()
             weight_items(tau)
+            if o.small:
+                small_items(tau)
         if o.grads:
             grad_items(tau - 1)
             state_items(tau - 1)
@@ -1014,6 +1046,8 @@
         rows_of_pack = inputs["p_bc"][0].shape[1]
         pack_width = sum(v[0].shape[2] for k, v in inputs.items() if k.startswith("p_"))
         scratch.update(
+            columns=pltpu.VMEM((*(2,) * o.bits, rows_of_pack, 128), BF),
+            small_sem=dma(()),
             wown=pltpu.VMEM((rows_of_pack, pack_width), BF),
             wl_sem=dma(()),
             wg_send=dma((o.bits, o.weights)),
@@ -1135,7 +1169,7 @@
     r.branch[at, :] = branch
     r.res_out[at, :] = residual
     r1 = lax.rsqrt(jnp.mean(residual * residual, axis=1, keepdims=True) + EPSILON)
-    return (residual * r1 * r.gain[...]).astype(BF)
+    return (residual * r1 * r.gain[r.gain_row, :]).astype(BF)
 
 
 def backward_middle(inner_all, r, at, total):
@@ -1145,7 +1179,7 @@
     width = res.shape[1]
     r1 = lax.rsqrt(jnp.mean(res * res, axis=1, keepdims=True) + EPSILON)
     hat = res * r1
-    dn = total * r.gain[...]
+    dn = total * r.gain[r.gain_row, :]
     cross = jnp.sum(dn * hat, axis=1, keepdims=True) / width
     grad = r.grad_in[at, :].astype(F32) + r1 * (dn - hat * cross)
     r.grad_out[at, :] = grad
@@ -1157,12 +1191,61 @@
     return grad.astype(BF)
 
 
-def pad_to(v, rows, columns):
-    return jnp.pad(v, ((0, rows - v.shape[0]), (0, columns - v.shape[1])))
-
-
-def rows_of(v):
-    return v.astype(F32).reshape(-1, v.shape[-1])
+def assemble_kernel(layers, dp_count, heads, bc_width, inner, *refs):
+    gouts, (sums, gains, pick), outs = refs[:layers], refs[layers : layers + 3], refs[layers + 3 :]
+    norm, gz, gx, gbc, gdt, cv, cvb, cs, csb, sb, ld, sk, gg, po = outs
+    me = lax.axis_index("dp")
+
+    def own(v):
+        share = v.shape[1] // dp_count
+        return pltpu.roll(v, v.shape[1] - me * share, 1)[:, :share]
+
+    norm[...] = own(gains[...])[0:layers]
+    for l in range(layers):
+        full = gouts[l]
+        first = bc_width + 128
+        gbc[l] = full[:, 0:bc_width]
+        gdt[:, l, :] = full[:, bc_width:first].T[0:heads, :]
+        gz[l] = full[:, first : first + inner]
+        gx[l] = full[:, first + inner : first + 2 * inner]
+        po[l] = full[:, first + 2 * inner :]
+        base = l * (inner + 128)
+        vec = sums[:, base : base + inner]
+        step = sums[:, base + inner : base + inner + 128]
+        start = layers * (inner + 128) + l * bc_width
+        state = own(sums[:, start : start + bc_width])
+        cv[l] = vec[0:4]
+        cvb[l : l + 1] = vec[4:5]
+        gg[l : l + 1] = vec[5:6]
+        one, two, three = parts3(vec)
+        head_sums = nn(one, pick[...]) + nn(two, pick[...]) + nn(three, pick[...])
+        sk[l : l + 1] = head_sums[6:7, 0:heads]
+        sb[l : l + 1] = step[0:1, 0:heads]
+        ld[l : l + 1] = step[1:2, 0:heads]
+        cs[l] = state[0:4]
+        csb[l : l + 1] = state[4:5]
+
+
+def assemble(gouts, sums, gains, pick, dp_count, heads, bc_width, inner):
+    layers, (rows, _) = len(gouts), gouts[0].shape
+    vmem = pl.BlockSpec(memory_space=pltpu.VMEM)
+    share = bc_width // dp_count
+    shapes = [
+        (layers, gains.shape[1] // dp_count),
+        (layers, rows, inner), (layers, rows, inner), (layers, rows, bc_width),
+        (heads, layers, rows), (layers, 4, inner), (layers, inner), (layers, 4, share),
+        (layers, share), (layers, heads), (layers, heads), (layers, heads), (layers, inner),
+        (layers, rows, inner),
+    ]
+    inputs = [*gouts, sums, gains, pick]
+    return pl.pallas_call(
+        functools.partial(assemble_kernel, layers, dp_count, heads, bc_width, inner),
+        in_specs=[vmem] * len(inputs),
+        out_specs=[vmem] * len(shapes),
+        out_shape=[jax.ShapeDtypeStruct(v, F32) for v in shapes],
+        compiler_params=pltpu.CompilerParams(vmem_limit_bytes=62 * MIB),
+        name="assemble",
+    )(*inputs)
 
 
 def shards(
@@ -1232,36 +1315,35 @@
 
     whole_rows, own_rows = ((tokens, width), BF, vmem), ((rows_own, width), F32, vmem)
     got = comm_call(
-        Step(gather=True, payload=plain_payload, weights=row_chunks, layer=0, **common),
+        Step(gather=True, payload=plain_payload, weights=row_chunks,
+             small=bc_width + heads, **common),
         "gather_first", 1,
         dict(own=(hidden_in, vmem), **weight_in),
-        dict(full=whole_rows, **weight_out),
+        dict(full=whole_rows, small=((8, width), F32, vmem), **weight_out),
     )
     x_rows = got["full"]
     out_grad, x_rows = lax.optimization_barrier((out_grad, x_rows))
     grad_rows = lax.all_gather(out_grad, "tensor", axis=0, tiled=True)
     packed = [got["wfull"].reshape(width, packed_width)]
-    start = bc_width + heads
-    extra_all = packed[0][:, start : start + 2 * layers].astype(F32)
-    gain_rows = extra_all[:, 0 : 2 * layers : 2].T[:, None, :]
+    small = got["small"]
     per = bc_width // dp_count
-    smalls = extra_all[:, 1 : 2 * layers : 2].reshape(dp_count, shard_rows, layers)
-    smalls = smalls[:, : 5 * per].reshape(dp_count, 5, per, layers)
-    cst = jnp.transpose(smalls, (3, 1, 0, 2)).reshape(layers, 5, bc_width)
-    params = (vec, cst, tiny)
-
-    out = forward_mix(x_rows, packed[0], params + (gain_rows,), 0)
-    saved, rows = [out[:6]], [out[8]]
+    smalls = small[1 : 2 * layers : 2].reshape(layers, dp_count, shard_rows)[:, :, : 5 * per]
+    cst = jnp.transpose(smalls.reshape(layers, dp_count, 5, per), (0, 2, 1, 3))
+    cst = cst.reshape(layers, 5, bc_width)
+    params = (vec, cst, tiny, small)
+
+    out = forward_mix(x_rows, packed[0], params, 0)
+    saved, rows = [out[:7]], [out[9]]
     residuals, branches, r2s = [hidden_in], [], []
     for l in range(layers - 1):
         got = comm_call(
             Step(
-                partial=True, gather=True, late=True, scale=inner_all, middle=forward_middle,
-                weights=row_chunks, layer=l + 1, **common,
+                partial=True, gather=True, late=True, scale=inner_all, middle=forward_middle, chunks=16,
+                weights=row_chunks, layer=l + 1, gain_row=2 * (l + 1), **common,
             ),
             "between_forward", 2 + l,
-            dict(part=(out[6], vmem), ssq=(out[7], vmem), res=(residuals[l], vmem),
-                 gain=(gain_rows[l + 1], vmem), **weight_in),
+            dict(part=(out[7], vmem), ssq=(out[8], vmem), res=(residuals[l], vmem),
+                 gain=(small, vmem), **weight_in),
             dict(full=whole_rows, branch=own_rows, res_out=own_rows,
                  r2=((rows_own, 128), F32, vmem), **weight_out),
         )
@@ -1271,24 +1353,24 @@
         r2s.append(got["r2"])
         packed.append(got["wfull"].reshape(width, packed_width))
         gb = grad_rows if l + 1 == layers - 1 else None
-        out = forward_mix(rows[-1], packed[-1], params + (gain_rows,), l + 1, gb)
-        saved.append(out[:6])
-    total = lax.psum_scatter(out[6], "tensor", scatter_dimension=0, tiled=True)
-    token_rows, r2_own = meet(out[7], tensor_count, inner_all, 16)
-    hidden_out = residuals[-1].astype(F32) + r2_own[:, 0:1] * total.astype(F32)
-    product = out[8]
+        out = forward_mix(rows[-1], packed[-1], params, l + 1, gb)
+        saved.append(out[:7])
+    total = lax.psum_scatter(out[7], "tensor", scatter_dimension=0, tiled=True)
+    token_rows, r2_own = meet(out[8], tensor_count, inner_all, 16)
+    product = out[9]
     gradient = out_grad
     scattered, summed, gain_grads = [None] * layers, [None] * layers, [None] * layers
     for l in reversed(range(layers)):
         last = l == layers - 1
         dcat, dpart, *small_grads = backward_mix(
             product if last else grad_rows, last, token_rows, rows[l], saved[l], packed[l],
-            params + (gain_rows,), pick, l,
-        )
-        *summed[l], gain_grads[l] = small_grads
+            params, pick, l, () if last else (residuals[-1], total, r2_own),
+        )
+        summed[l], gain_grads[l] = small_grads[:3], small_grads[3]
+        hidden_out = small_grads[-1]
         more = l > 0
         inputs = dict(
-            part=(dpart, vmem), res=(residuals[l], vmem), gain=(gain_rows[l], vmem),
+            part=(dpart, vmem), res=(residuals[l], vmem), gain=(small, vmem),
             grad_in=(gradient, vmem), lrows=(rows[l], vmem), lgrad=(grad_rows, vmem),
             right=(dcat, vmem),
         )
@@ -1313,7 +1395,8 @@
         got = comm_call(
             Step(
                 partial=True, gather=more, late=more, inner=more, grads=column_chunks,
-                states=bc_width, sums=not more,
+                chunks=16 if more else 8, lag=2 if more else 1,
+                states=bc_width, sums=not more, gain_row=2 * l,
                 lazy=("right", "lrows", "lgrad", "res", "grad_in") + (("branch",) if more else ()),
                 middle=functools.partial(backward_middle, inner_all if more else None), **common,
             ),
@@ -1323,37 +1406,12 @@
         scattered[l] = got["gout"]
         if more:
             grad_rows, token_rows = got["full"], got["inner"]
-    gout = jnp.stack(scattered)
-    sums, ggain = got["sums"], got["gain_sums"][:layers]
-    each = inner + 128
-    gvec = jnp.stack([sums[:, i * each : i * each + inner] for i in range(layers)])
-    gdt = jnp.stack([sums[:, i * each + inner : (i + 1) * each] for i in range(layers)])
-    gst = jnp.stack(
-        [sums[:, layers * each + i * bc_width :][:, :bc_width] for i in range(layers)]
+    grads = list(
+        assemble(scattered, got["sums"], got["gain_sums"], pick, dp_count, heads, bc_width, inner)
     )
-    own = lambda v, axis: lax.dynamic_slice_in_dim(
-        v, lax.axis_index("dp") * (v.shape[axis] // dp_count), v.shape[axis] // dp_count, axis
-    )
-    gst = own(gst, 2)
-    first = bc_width + 128
-    return (
-        hidden_out,
-        gradient,
-        own(ggain, 1),
-        gout[:, :, first : first + inner],
-        gout[:, :, first + inner : first + 2 * inner],
-        gout[:, :, :bc_width],
-        gout[:, :, bc_width : bc_width + heads],
-        gvec[:, 0:4],
-        gvec[:, 4],
-        gst[:, 0:4],
-        gst[:, 4],
-        gdt[:, 0, :heads],
-        gdt[:, 1, :heads],
-        jnp.sum(gvec[:, 6].reshape(layers, heads, WIDTH), axis=2),
-        gvec[:, 5],
-        jnp.transpose(gout[:, :, first + 2 * inner :], (0, 2, 1)),
-    )
+    grads[4] = jnp.transpose(grads[4], (1, 2, 0))
+    grads[-1] = jnp.transpose(grads[-1], (0, 2, 1))
+    return (hidden_out, gradient, *grads)
 
 
 def solution(mesh):

time: 550 us -> 532 us (0.967)
  local copies, waits for them, and re-layouts: 16.1 us -> 4.9 us
  other arithmetic: 13.9 us -> 4.2 us
    slice x8 -> x1, local copies, waits for them, and re-layouts: 6.57 us -> 0.82 us  [shards(): small[1:2 * layers:2].reshape(layers, dp_count, shard_rows)[:, :, :5 * per]]
    pallas_call x2 -> x3, Pallas kernels: 81 us -> 78.9 us  [the longest x2 74.3 us: backward_mix(): pl.pallas_call(functools.partial(bwd_kernel, ready, l), grid=(blocks,), i...]
  transfers between devices with their start and end apart: 2 -> 2, of which waited for: 0 -> 0; matrix products, arithmetic and copies ran while one was open for 4% -> 1% of each run, Pallas kernels for 75% -> 56%
where the time goes in v6:
time: 532 us; the launch traced here: 525 us
  Pallas kernels  501 us (94%)
  between operations  14.7 us (3%)
    pallas_call x4, Pallas kernels, comm_call(): pl.pallas_call(functools.partial(comm_kernel, o, names), in_specs=[pl.Blo...  357 us
    pallas_call x2, Pallas kernels, backward_mix(): pl.pallas_call(functools.partial(bwd_kernel, ready, l), grid=(blocks,), i...  74.3 us
    pallas_call x2, Pallas kernels, forward_mix(): pl.pallas_call(functools.partial(fwd_kernel, first, last), grid=(blocks,)...  57.9 us
  transfers between devices with their start and end apart: 2, of which 0 were waited for; matrix products, arithmetic and copies ran while one was open for 1% of the time, Pallas kernels for 56%

profile of v6, /device:TPU:0, one launch (start us, length us, event | category | flops | bytes accessed | tf_op | source)
XLA Modules:
  0.0 525.5 jit_solution(9115255702089028801)
XLA Ops:
  7.2 0.0 all-gather.2.cloned.1.call-start
  7.3 0.8 reshape.91
  8.1 0.7 fusion.7
  8.7 0.7 pad_maximum_fusion
  9.4 0.1 copy.36
  9.6 0.9 copy.37
  10.5 0.1 pad.18.clone
  10.6 0.7 maximum_maximum_fusion.refs_2_.refs_5_
  11.3 61.7 %gather_first.1 = (bf16[1024,1536]{1,0:T(8,128)(2,1)}, f32[8,1536]{1,0:T(8,128)}, bf16[2,2,2,192,2688]{4,3,2,1,0:T(8,128)(2,1)}) custom-call(bf16[256,1536]{1,0:T(8,128)(2,1)} %refs_1_.3, bf16[2,192,256]{2,1,0:T(8,128)(2,1)} %refs_4_.3, bf16[2,192,128]{2,1,0:T(8,128)(2,1)} %maximum_maximum_fusion.refs_2_.refs_5_, bf16[2,192,768]{2,1,0:T(8,128)(2,1)} %refs_6_.1, ...), custom_call_target="tpu_custom_call" | custom-call | tf_op jit(solution)/shard_map/gather_first/pallas_call | solution.py:1089
  73.0 0.0 all-gather.2.cloned.1.call-update
  73.1 0.0 reduce-scatter.2.cloned.1.call-start
  73.2 0.1 broadcast_in_dim.23
  73.2 0.1 broadcast_in_dim_reshape.4
  73.3 0.8 slice.6
  74.2 0.1 reshape.94
  74.2 0.1 reshape.95
  74.3 0.7 reshape.99.cst_ref
  75.0 0.6 select_maximum_fusion.tiny_ref
  75.6 0.6 maximum_convert_fusion.vec_ref
  76.3 27.9 %mix_forward.2 = (f32[1024,768]{1,0:T(8,128)}, f32[1024,768]{1,0:T(8,128)}, f32[1024,256]{1,0:T(8,128)}, f32[1024,128]{1,0:T(8,128)}, f32[1024,768]{1,0:T(8,128)...) custom-call(bf16[1024,1536]{1,0:T(8,128)(2,1)} %get-tuple-element.84, ...), custom_call_target="tpu_custom_call" | custom-call | tf_op jit(solution)/shard_map/mix_forward/pallas_call | solution.py:229
  104.2 116.6 %between_forward.1 = (bf16[1024,1536]{1,0:T(8,128)(2,1)}, f32[256,1536]{1,0:T(8,128)}, f32[256,1536]{1,0:T(8,128)}, f32[256,128]{1,0:T(8,128)}, bf16[2,2,2,192,2688]{4,3,2,1,0:T(8,128)(2,1)}) custom-call(bf16[1024,1536]{1,0:T(8,128)(2,1)} %get-tuple-element.87.refs_0_, f32[8,1024]{1,0:T(8,128)} %get-tuple-element.88.refs_1_, bf16[256,1536]{1,0:T(8,128)(2,1)} %refs_1_.3, ...), custom_call_target="tpu_custom_call" | custom-call | tf_op jit(solution)/shard_map/between_forward/pallas_call | solution.py:1089
  220.8 0.0 all-gather.2.cloned.1.call-done.rest_0_.refs_5_
  220.8 30.0 %mix_forward.3 = (f32[1024,768]{1,0:T(8,128)}, f32[1024,768]{1,0:T(8,128)}, f32[1024,256]{1,0:T(8,128)}, f32[1024,128]{1,0:T(8,128)}, f32[1024,768]{1,0:T(8,128)...) custom-call(bf16[1024,1536]{1,0:T(8,128)(2,1)} %get-tuple-element.89, ...), custom_call_target="tpu_custom_call" | custom-call | tf_op jit(solution)/shard_map/mix_forward/pallas_call | solution.py:229
  250.9 0.9 fusion.pick_ref.refs_4_
  251.7 7.5 %turn_around.1 = (f32[8,1024]{1,0:T(8,128)}, f32[256,128]{1,0:T(8,128)}) custom-call(f32[8,1024]{1,0:T(8,128)} %get-tuple-element.93.own_ref), custom_call_target="tpu_custom_call" | custom-call | tf_op jit(solution)/shard_map/turn_around/pallas_call | solution.py:1141
  259.2 36.0 %mix_backward.2 = (bf16[1024,2688]{1,0:T(8,128)(2,1)}, bf16[1024,1536]{1,0:T(8,128)(2,1)}, f32[8,768]{1,0:T(8,128)}, f32[8,256]{1,0:T(8,128)}, f32[8,128]{1,0:T(8,128)}, /*index=5*/f32[8,1536]{1,0:T(8,128)}) custom-call(f32[1024,768]{1,0:T(8,128)} %get-tuple-element.92.gb_ref, f32[8,1024]{1,0:T(8,128)} %get-tuple-element.94.e_ref, ...), custom_call_target="tpu_custom_call" | custom-call | tf_op jit(solution)/shard_map/mix_backward/pallas_call | solution.py:443
  295.2 107.6 %between_backward.1 = (f32[256,1536]{1,0:T(8,128)}, f32[192,2688]{1,0:T(8,128)}, bf16[1024,1536]{1,0:T(8,128)(2,1)}, f32[8,1024]{1,0:T(8,128)}) custom-call(bf16[1024,1536]{1,0:T(8,128)(2,1)} %get-tuple-element.102.refs_0_, f32[256,1536]{1,0:T(8,128)} %get-tuple-element.103.refs_1_.rest_0_, f32[8,1536]{1,0:T(8,128)} %get-tuple-element.86.gain_ref.refs_3_.refs_2_, ...), custom_call_target="tpu_custom_call" | custom-call | tf_op jit(solution)/shard_map/between_backward/pallas_call | solution.py:1089
  402.8 0.0 reduce-scatter.2.cloned.1.call-done.rest_1_
  402.8 38.2 %mix_backward.3 = (bf16[1024,2688]{1,0:T(8,128)(2,1)}, bf16[1024,1536]{1,0:T(8,128)(2,1)}, f32[8,768]{1,0:T(8,128)}, f32[8,256]{1,0:T(8,128)}, f32[8,128]{1,0:T(...) custom-call(bf16[1024,1536]{1,0:T(8,128)(2,1)} %get-tuple-element.107.gb_ref.refs_5_, ...), custom_call_target="tpu_custom_call" | custom-call | tf_op jit(solution)/shard_map/mix_backward/pallas_call | solution.py:443
  441.1 71.3 %last_backward.1 = (f32[256,1536]{1,0:T(8,128)}, f32[192,2688]{1,0:T(8,128)}, f32[8,2304]{1,0:T(8,128)}, f32[8,1536]{1,0:T(8,128)}) custom-call(bf16[1024,1536]{1,0:T(8,128)(2,1)} %get-tuple-element.120.refs_0_, bf16[256,1536]{1,0:T(8,128)(2,1)} %refs_1_.3, f32[8,1536]{1,0:T(8,128)} %get-tuple-element.86.gain_ref.refs_3_.refs_2_, ...), custom_call_target="tpu_custom_call" | custom-call | tf_op jit(solution)/shard_map/last_backward/pallas_call | solution.py:1089
  512.4 4.6 assemble.1
  517.0 1.1 copy.51
  (25 shorter events, 0.1 us)
Async XLA Ops:
  7.2 65.9 %copy-start.2 = (bf16[2,768]{1,0:T(2,128)(2,1)S(1)}, bf16[2,768]{1,0:T(2,128)(2,1)}, u32[]{:S(2)}) copy-start(bf16[2,768]{1,0:T(2,128)(2,1)} %param.24) | copy-start | bytes 9220
  7.2 65.9 %copy-start.3 = (bf16[2,768]{1,0:T(2,128)(2,1)S(1)}, bf16[2,768]{1,0:T(2,128)(2,1)}, u32[]{:S(2)}) copy-start(bf16[2,768]{1,0:T(2,128)(2,1)} %param.30) | copy-start | bytes 9220
  7.2 66.0 %copy-start.4 = (bf16[2,12]{1,0:T(2,128)(2,1)S(1)}, bf16[2,12]{1,0:T(2,128)(2,1)}, u32[]{:S(2)}) copy-start(bf16[2,12]{1,0:T(2,128)(2,1)} %param.29) | copy-start | bytes 148
  7.2 67.8 %copy-start.5 = (bf16[2,12]{1,0:T(2,128)(2,1)S(1)}, bf16[2,12]{1,0:T(2,128)(2,1)}, u32[]{:S(2)}) copy-start(bf16[2,12]{1,0:T(2,128)(2,1)} %param.27) | copy-start | bytes 148
  7.2 67.8 %copy-start.6 = (bf16[2,12]{1,0:T(2,128)(2,1)S(1)}, bf16[2,12]{1,0:T(2,128)(2,1)}, u32[]{:S(2)}) copy-start(bf16[2,12]{1,0:T(2,128)(2,1)} %param.28) | copy-start | bytes 148
  7.2 68.4 %copy-start.1 = (bf16[2,4,768]{2,1,0:T(4,128)(2,1)S(1)}, bf16[2,4,768]{2,1,0:T(4,128)(2,1)}, u32[]{:S(2)}) copy-start(bf16[2,4,768]{2,1,0:T(4,128)(2,1)} %param.23) | copy-start | bytes 36868
  7.2 213.6 %all-gather.2.cloned.1.call-start = ((), (), s32[]{:S(2)}) async-start(), calls=%async_computation.1 | async-start | bytes 3932160 | tf_op jit(solution)/shard_map/all_gather | solution.py:1326
  73.1 329.8 %reduce-scatter.2.cloned.1.call-start = ((), (), s32[]{:S(2)}) async-start(), calls=%async_computation.2 | async-start | bytes 3932160 | tf_op jit(solution)/shard_map/reduce_scatter | solution.py:1358
  512.4 4.6 copy-start
Sparse Core Ops, SparseCore 0:
  73.2 79.6 all-gather.1
  251.0 66.4 reduce-scatter.1

commit v7 on v6

--- a/solution.py
+++ b/solution.py
@@ -4,6 +4,7 @@
 import jax
 import jax.numpy as jnp
 from jax import lax
+import numpy as np
 from jax.sharding import PartitionSpec as P
 import jax.experimental.pallas as pl
 import jax.experimental.pallas.tpu as pltpu
@@ -94,11 +95,11 @@
 ):
     if last:
         gb_ref, *rest = rest
-    gate_ref, val_ref, st_ref, dt_ref, y_ref, ent_ref, pre_ref, part_ref, ssq_ref, *rest = rest
+    gate_ref, val_ref, st_ref, dt_ref, y_ref, ent_ref, pre_ref, ssq_ref, part_ref, *rest = rest
     if first:
         normed_ref, *rest = rest
     if last:
-        dm_ref, *rest = rest
+        part2_ref, dm_ref, mixed_ref, *rest = rest
     state, vpad, spad = rest[-3:]
     step = pl.program_id(0)
     length = rows_ref.shape[0]
@@ -181,13 +182,24 @@
     square = (gated * gated).astype(BF)
     ssq_ref[...] = nt(jnp.ones((8, inner), BF), square)
     mixed = (gated * gg_ref[...]).astype(BF)
-    part_ref[...] = nt(mixed, wot_ref[...]).astype(BF)
-    if last:
-        dm = nn(gb_ref[...], wot_ref[...])
-        dm_ref[...] = dm
-        dots = nt(jnp.ones((8, inner), BF), (dm * gg_ref[...] * gated).astype(BF))
-        row = lax.broadcasted_iota(jnp.int32, dots.shape, 0)
-        ssq_ref[...] = jnp.where(row == 0, ssq_ref[...], dots)
+    part = nt(mixed, wot_ref[...]).astype(BF)
+    if not last:
+        part_ref[...] = part
+    else:
+        cut = length // 2
+        part_ref[0], part2_ref[0] = part[:cut], part[cut:]
+        mixed_ref[0] = mixed[cut:]
+        dm = nn(gb_ref[0], wot_ref[...])
+        dm_ref[0] = dm
+        dots = token_dots(dm, mixed[:cut])
+        row = lax.broadcasted_iota(jnp.int32, (8, length), 0)
+        ssq_ref[...] = jnp.where(row == 0, ssq_ref[...], 0.0)
+        ssq_ref[1:2, 0:cut] = dots[0:1]
+
+
+def token_dots(dm, mixed):
+    product = (dm * mixed.astype(F32)).astype(BF)
+    return nt(jnp.ones((8, product.shape[1]), BF), product)
 
 
 def whole(shape):
@@ -219,19 +231,22 @@
         ((tokens, inner), F32, tok(inner)),
         ((blocks, half, inner), F32, pl.BlockSpec((1, half, inner), lambda i: (i, 0, 0))),
         ((tokens, inner), F32, tok(inner)),
-        ((tokens, width), BF, tok(width)),
         ((8, tokens), F32, pl.BlockSpec((8, q), lambda i: (0, i))),
     ]
+    half_of = lambda n: pl.BlockSpec((1, q // 2, n), lambda i: (i, 0, 0))
+    if not last:
+        outs.append(((tokens, width), BF, tok(width)))
     if first:
         outs.append(((tokens, width), BF, tok(width)))
     if last:
-        outs.append(((tokens, inner), F32, tok(inner)))
+        for n, kind in ((width, BF), (width, BF), (inner, F32), (inner, BF)):
+            outs.append(((blocks, q // 2, n), kind, half_of(n)))
     return pl.pallas_call(
         functools.partial(fwd_kernel, first, last),
         grid=(blocks,),
         in_specs=[tok(width), whole(packed.shape)]
         + layer_specs(params, l)
-        + ([tok(width)] if last else []),
+        + ([half_of(width)] if last else []),
         out_specs=[o[2] for o in outs],
         out_shape=[jax.ShapeDtypeStruct(o[0], o[1]) for o in outs],
         scratch_shapes=[
@@ -250,16 +265,13 @@
     ready, layer, gb_ref, e_ref, rows_ref, gate_ref, val_ref, st_ref, stp_ref, dt_ref, y_ref,
     ent_ref, pre_ref, w_ref, vec_ref, cst_ref, tiny_ref, gain_ref, pick_ref, *rest,
 ):
-    if not ready:
-        res_ref, total_ref, scale_ref, *rest = rest
+    if ready:
+        dm2_ref, *rest = rest
     dcat_ref, dpart_ref, gvec_ref, gst_ref, gdt_ref, ggain_ref, *rest = rest
-    if not ready:
-        hidden_ref, *rest = rest
-        hidden_ref[...] = res_ref[...] + scale_ref[:, 0:1] * total_ref[...].astype(F32)
     dstate, spad, dvpad, dspad = rest
     step = pl.program_id(0)
     blocks = pl.num_programs(0)
-    length = gb_ref.shape[0]
+    length = y_ref.shape[0]
     cv_ref, cvb_ref, skip_ref, gg_ref, cs_ref, csb_ref, sb_ref, rate_ref = small_refs(
         vec_ref, cst_ref, tiny_ref
     )
@@ -316,7 +328,10 @@
     gated = y * sgate
     per_token = e_ref[...].T
     e, r2 = per_token[:, 0:1], per_token[:, 1:2]
-    dm = (gb_ref[...] if ready else nn(gb_ref[...], wot_ref[...])) * r2
+    if ready:
+        dm = jnp.concatenate([gb_ref[0], dm2_ref[0]], axis=0) * r2
+    else:
+        dm = nn(gb_ref[...], wot_ref[...]) * r2
     dgated = dm * gg_ref[...] - e * gated
     mixed_ref[...] = (gated * r2 * gg_ref[...]).astype(BF)
     dgate = (dgated * y * (sig_g * (1.0 + gate * (1.0 - sig_g)))).astype(BF)
@@ -413,9 +428,9 @@
         ggain_ref[0:1, :] = ggain_ref[0:1, :] / gain_ref[2 * layer : 2 * layer + 1, :]
 
 
-def backward_mix(gb, ready, e_rows, rows, kept, packed, params, pick, l, last=()):
+def backward_mix(gb, ready, e_rows, rows, kept, packed, params, pick, l):
     gate, val, st, dt, y, ent, pre = kept
-    tokens, width = gb.shape[0], packed.shape[0]
+    tokens, width = y.shape[0], packed.shape[0]
     inner = params[0].shape[2]
     bc_width = params[1].shape[2]
     dt_width = 128
@@ -437,14 +452,13 @@
         ((8, dt_width), F32, fixed(8, dt_width)),
         ((8, width), F32, fixed(8, width)),
     ]
-    few = [pl.BlockSpec((v.shape[0] // blocks, v.shape[1]), lambda i: (i, 0)) for v in last]
-    if last:
-        outs.append((last[0].shape, F32, few[0]))
+    half_of = pl.BlockSpec((1, q // 2, inner), lambda i: (back(i), 0, 0))
+    gb, more = (gb[0], [gb[1]]) if ready else (gb, [])
     return pl.pallas_call(
         functools.partial(bwd_kernel, ready, l),
         grid=(blocks,),
         in_specs=[
-            tok(gb.shape[1]),
+            half_of if ready else tok(width),
             pl.BlockSpec((8, q), lambda i: (0, back(i))),
             tok(width),
             tok(inner), tok(inner), tok(bc_width), halo(bc_width), tok(dt_width),
@@ -452,7 +466,8 @@
             pl.BlockSpec((1, half, inner), lambda i: (back(i), 0, 0)),
             tok(inner),
         ]
-        + [whole(packed.shape)] + layer_specs(params, l) + [whole(pick.shape)] + few,
+        + [whole(packed.shape)] + layer_specs(params, l) + [whole(pick.shape)]
+        + [half_of] * len(more),
         out_specs=[o[2] for o in outs],
         out_shape=[jax.ShapeDtypeStruct(o[0], o[1]) for o in outs],
         scratch_shapes=[
@@ -465,7 +480,7 @@
             dimension_semantics=("arbitrary",), vmem_limit_bytes=60 * MIB
         ),
         name="mix_backward",
-    )(gb, e_rows, rows, gate, val, st, st, dt, y, ent, pre, packed, *params, pick, *last)
+    )(gb, e_rows, rows, gate, val, st, st, dt, y, ent, pre, packed, *params, pick, *more)
 
 
 class Step:
@@ -487,12 +502,14 @@
         self.gain_row = 0
         self.weights = 0
         self.grads = 0
+        self.double = 2
         self.tail = 2
         self.lag = 1
         self.states = 0
         self.sums = False
         self.bits = 0
         self.middle = None
+        self.halves = False
         self.lazy = ()
         self.__dict__.update(given)
 
@@ -531,6 +548,9 @@
         near = getattr(r, name + "_v")
         lazy.append(pltpu.make_async_copy(getattr(r, name), near, r.lazy_sem.at[i]))
         setattr(r, name, near)
+    if o.halves:
+        for i, far in enumerate((r.half0, r.half1)):
+            lazy.append(pltpu.make_async_copy(far, r.lgrad.at[:, i], r.half_sem.at[i]))
     for copy in lazy:
         copy.start()
 
@@ -730,12 +750,20 @@
             {"dp": partner[order[stage]]},
         )
 
+    def products(turn, i):
+        product(jnp.where(turn >= 0, chunk_of(turn), -1), i)
+
+        @when((turn >= 0) & (turn < o.double))
+        def _():
+            product(2 * turn + 1, i)
+
     def product(j, i):
         slab = o.width // 2
         inner_shape = (2,) * (o.bits - 1) + (slab >> (o.bits - 1), WCHUNK)
 
         def one(left):
-            out = tn(left[:, pl.ds(i * slab, slab)], r.right[:, cols(j)])
+            rows_of_slab = left[..., pl.ds(i * slab, slab)].reshape(-1, slab)
+            out = tn(rows_of_slab, r.right[:, cols(j)])
             r.grad[j, i] = out.astype(BF).reshape(inner_shape)
 
         @when((j >= 0) & (j < o.grads - o.tail))
@@ -746,14 +774,22 @@
         def _():
             one(r.lgrad)
 
-    def each_chunk(j, fn):
+    def chunk_of(turn):
+        return jnp.where(turn < o.double, 2 * turn, turn + o.double)
+
+    def each_chunk(turn, fn):
+        j = chunk_of(turn)
         for parity in range(2):
-            @when((j >= 0) & (j < o.grads) & (lax.rem(j, 2) == parity))
+            @when((turn >= 0) & (j < o.grads) & (lax.rem(j, 2) == parity))
             def _():
                 fn(parity, j)
 
+        @when((turn >= 0) & (turn < o.double))
+        def _():
+            fn(1, 2 * turn + 1)
+
     def grad_items(tau):
-        product(tau, 1)
+        products(tau, 1)
 
         def first(parity, j):
             grad_copy(parity, 0, j).start()
@@ -899,7 +935,7 @@
     if o.weights:
         ends.append((o.weights + 1) // 2 + o.bits + (2 if o.small else 0))
     if o.grads:
-        ends.append(1 + o.grads + grad_lag(o.bits))
+        ends.append(1 + o.grads - o.double + grad_lag(o.bits))
         ends.append(grad_lag(o.bits) + 5)
     if o.sums:
         ends.append(4 + o.bits)
@@ -911,7 +947,7 @@
                 for copy in lazy:
                     copy.wait()
         if o.grads:
-            product(tau - 1, 0)
+            products(tau - 1, 0)
         if o.partial:
             for side in range(2):
                 c = tau - o.hop * (t if side == 0 else n - 1 - t)
@@ -1024,6 +1060,8 @@
             inputs[key] = (value, pl.ANY)
             scratch[key + "_v"] = pltpu.VMEM(value.shape, value.dtype)
         scratch.update(lazy_sem=dma((len(o.lazy),)))
+    if o.halves:
+        scratch.update(lgrad=pltpu.VMEM((n, 2, rows // 2, width), BF), half_sem=dma((2,)))
     if o.partial:
         scratch.update(
             rbuf=pltpu.VMEM((n, rows, width), BF),
@@ -1100,26 +1138,39 @@
     return dict(zip(outputs, out))
 
 
-def meet_kernel(n, inner_all, own_ref, out_ref, scale_ref, bank, send, recv):
+def meet_kernel(
+    n, inner_all, own_ref, grad_ref, mixed_ref, w_ref,
+    out_ref, scale_ref, dm_ref, stage, near, bank, send, recv, sem,
+):
     t = lax.axis_index("tensor")
+    inner = near.shape[1]
+    weight = pltpu.make_async_copy(w_ref.at[:, pl.ds(w_ref.shape[1] - inner, inner)], near, sem)
+    weight.start()
     barrier = pltpu.get_barrier_semaphore()
     for k in range(1, n):
         pl.semaphore_signal(
             barrier, inc=1, device_id={"tensor": lax.rem(t + k, n)},
             device_id_type=pl.DeviceIdType.MESH,
         )
+    stage[...] = own_ref[...]
+    rows, cut = scale_ref.shape[0], grad_ref.shape[1]
+    weight.wait()
+    for s in range(n):
+        dm = nn(grad_ref[s], near[...])
+        dm_ref[s] = dm
+        stage[1:2, (s + 1) * rows - cut : (s + 1) * rows] = token_dots(dm, mixed_ref[s])[0:1]
     pl.semaphore_wait(barrier, n - 1)
     copies = [
-        remote(own_ref, bank.at[t], send.at[k - 1], recv.at[k - 1], {"tensor": lax.rem(t + k, n)})
+        remote(stage, bank.at[t], send.at[k - 1], recv.at[k - 1], {"tensor": lax.rem(t + k, n)})
         for k in range(1, n)
     ]
     for copy in copies:
         copy.start()
-    bank[t] = own_ref[...]
+    bank[t] = stage[...]
     for k in range(1, n):
         source = lax.rem(t + n - k, n)
         remote(
-            own_ref, bank.at[source], send.at[k - 1], recv.at[k - 1], {"tensor": source}
+            stage, bank.at[source], send.at[k - 1], recv.at[k - 1], {"tensor": source}
         ).wait_recv()
     total = bank[0]
     for s in range(1, n):
@@ -1128,28 +1179,34 @@
     row = lax.broadcasted_iota(jnp.int32, total.shape, 0)
     e = scale * scale * scale * (total[1:2, :] / inner_all)
     out_ref[...] = jnp.where(row == 0, e, scale)
-    rows = scale_ref.shape[0]
     mine = out_ref[:, pl.ds(pl.multiple_of(t * rows, rows), rows)].T
     scale_ref[...] = jnp.broadcast_to(mine[:, 1:2], scale_ref.shape)
     for copy in copies:
         copy.wait_send()
 
 
-def meet(own, n, inner_all, collective):
+def meet(own, grad, mixed, packed, n, inner_all, collective):
     vmem = pl.BlockSpec(memory_space=pltpu.VMEM)
     dma = pltpu.SemaphoreType.DMA
+    inner = mixed.shape[2]
     return pl.pallas_call(
         functools.partial(meet_kernel, n, inner_all),
-        in_specs=[vmem],
-        out_specs=[vmem, vmem],
+        in_specs=[vmem, vmem, vmem, pl.BlockSpec(memory_space=pl.ANY)],
+        out_specs=[vmem, vmem, vmem],
         out_shape=[
             jax.ShapeDtypeStruct(own.shape, F32),
             jax.ShapeDtypeStruct((own.shape[1] // n, 128), F32),
+            jax.ShapeDtypeStruct(mixed.shape, F32),
         ],
-        scratch_shapes=[pltpu.VMEM((n,) + own.shape, F32), dma((n - 1,)), dma((n - 1,))],
-        compiler_params=pltpu.CompilerParams(collective_id=collective, has_side_effects=True),
+        scratch_shapes=[
+            pltpu.VMEM(own.shape, F32), pltpu.VMEM((packed.shape[0], inner), BF),
+            pltpu.VMEM((n,) + own.shape, F32), dma((n - 1,)), dma((n - 1,)), dma(()),
+        ],
+        compiler_params=pltpu.CompilerParams(
+            collective_id=collective, has_side_effects=True, vmem_limit_bytes=62 * MIB
+        ),
         name="turn_around",
-    )(own)
+    )(own, grad, mixed, packed)
 
 
 def plain_payload(r):
@@ -1192,9 +1249,14 @@
 
 
 def assemble_kernel(layers, dp_count, heads, bc_width, inner, *refs):
-    gouts, (sums, gains, pick), outs = refs[:layers], refs[layers : layers + 3], refs[layers + 3 :]
-    norm, gz, gx, gbc, gdt, cv, cvb, cs, csb, sb, ld, sk, gg, po = outs
+    gouts, (sums, gains, pick), refs = refs[:layers], refs[layers : layers + 3], refs[layers + 3 :]
+    res, scale, *halves = refs[:4]
+    norm, gz, gx, gbc, gdt, cv, cvb, cs, csb, sb, ld, sk, gg, po, hidden = refs[4:]
     me = lax.axis_index("dp")
+    cut = halves[0].shape[0]
+    for i, half in enumerate(halves):
+        at = slice(i * cut, (i + 1) * cut)
+        hidden[at, :] = res[at, :] + scale[at, 0:1] * half[...].astype(F32)
 
     def own(v):
         share = v.shape[1] // dp_count
@@ -1226,7 +1288,7 @@
         csb[l : l + 1] = state[4:5]
 
 
-def assemble(gouts, sums, gains, pick, dp_count, heads, bc_width, inner):
+def assemble(gouts, sums, gains, pick, dp_count, heads, bc_width, inner, hidden):
     layers, (rows, _) = len(gouts), gouts[0].shape
     vmem = pl.BlockSpec(memory_space=pltpu.VMEM)
     share = bc_width // dp_count
@@ -1235,9 +1297,9 @@
         (layers, rows, inner), (layers, rows, inner), (layers, rows, bc_width),
         (heads, layers, rows), (layers, 4, inner), (layers, inner), (layers, 4, share),
         (layers, share), (layers, heads), (layers, heads), (layers, heads), (layers, inner),
-        (layers, rows, inner),
+        (layers, rows, inner), hidden[0].shape,
     ]
-    inputs = [*gouts, sums, gains, pick]
+    inputs = [*gouts, sums, gains, pick, *hidden]
     return pl.pallas_call(
         functools.partial(assemble_kernel, layers, dp_count, heads, bc_width, inner),
         in_specs=[vmem] * len(inputs),
@@ -1311,7 +1373,7 @@
     ).astype(F32)
     tiny = jnp.stack([step_bias.astype(F32), -jnp.exp(log_decay.astype(F32))], axis=1)
     tiny = jnp.pad(tiny, ((0, 0), (0, 0), (0, 128 - heads)))
-    pick = (jnp.arange(inner)[:, None] // WIDTH == jnp.arange(128)[None, :]).astype(BF)
+    pick = jnp.asarray(np.arange(inner)[:, None] // WIDTH == np.arange(128)[None, :], BF)
 
     whole_rows, own_rows = ((tokens, width), BF, vmem), ((rows_own, width), F32, vmem)
     got = comm_call(
@@ -1323,7 +1385,12 @@
     )
     x_rows = got["full"]
     out_grad, x_rows = lax.optimization_barrier((out_grad, x_rows))
-    grad_rows = lax.all_gather(out_grad, "tensor", axis=0, tiled=True)
+    cut = rows_own // 2
+
+    def gather_half(v):
+        return lax.all_gather(v, "tensor", axis=0)
+
+    first_half = gather_half(out_grad[:cut])
     packed = [got["wfull"].reshape(width, packed_width)]
     small = got["small"]
     per = bc_width // dp_count
@@ -1342,38 +1409,50 @@
                 weights=row_chunks, layer=l + 1, gain_row=2 * (l + 1), **common,
             ),
             "between_forward", 2 + l,
-            dict(part=(out[7], vmem), ssq=(out[8], vmem), res=(residuals[l], vmem),
+            dict(part=(out[8], vmem), ssq=(out[7], vmem), res=(residuals[l], vmem),
                  gain=(small, vmem), **weight_in),
             dict(full=whole_rows, branch=own_rows, res_out=own_rows,
                  r2=((rows_own, 128), F32, vmem), **weight_out),
         )
+        if l + 1 == layers - 1:
+            last_grad, got["full"] = lax.optimization_barrier((out_grad[cut:], got["full"]))
+            second_half = gather_half(last_grad)
         rows.append(got["full"])
         branches.append(got["branch"])
         residuals.append(got["res_out"])
         r2s.append(got["r2"])
         packed.append(got["wfull"].reshape(width, packed_width))
-        gb = grad_rows if l + 1 == layers - 1 else None
+        gb = first_half if l + 1 == layers - 1 else None
         out = forward_mix(rows[-1], packed[-1], params, l + 1, gb)
         saved.append(out[:7])
-    total = lax.psum_scatter(out[7], "tensor", scatter_dimension=0, tiled=True)
-    token_rows, r2_own = meet(out[8], tensor_count, inner_all, 16)
-    product = out[9]
+    def scatter_half(v):
+        return lax.psum_scatter(
+            v.reshape(-1, width), "tensor", scatter_dimension=0, tiled=True
+        )
+
+    branch_halves = [scatter_half(out[8])]
+    token_rows, r2_own, second_product = meet(
+        out[7], second_half, out[11], packed[-1], tensor_count, inner_all, 16
+    )
+    grad_rows = None
     gradient = out_grad
     scattered, summed, gain_grads = [None] * layers, [None] * layers, [None] * layers
     for l in reversed(range(layers)):
         last = l == layers - 1
         dcat, dpart, *small_grads = backward_mix(
-            product if last else grad_rows, last, token_rows, rows[l], saved[l], packed[l],
-            params, pick, l, () if last else (residuals[-1], total, r2_own),
+            (out[10], second_product) if last else grad_rows, last, token_rows, rows[l], saved[l],
+            packed[l], params, pick, l,
         )
         summed[l], gain_grads[l] = small_grads[:3], small_grads[3]
-        hidden_out = small_grads[-1]
         more = l > 0
         inputs = dict(
             part=(dpart, vmem), res=(residuals[l], vmem), gain=(small, vmem),
-            grad_in=(gradient, vmem), lrows=(rows[l], vmem), lgrad=(grad_rows, vmem),
-            right=(dcat, vmem),
-        )
+            grad_in=(gradient, vmem), lrows=(rows[l], vmem), right=(dcat, vmem),
+        )
+        if last:
+            inputs.update(half0=(first_half, far), half1=(second_half, far))
+        else:
+            inputs.update(lgrad=(grad_rows, vmem))
         outputs = dict(
             grad_out=own_rows,
             gout=((shard_rows, packed_width), F32, vmem),
@@ -1397,7 +1476,9 @@
                 partial=True, gather=more, late=more, inner=more, grads=column_chunks,
                 chunks=16 if more else 8, lag=2 if more else 1,
                 states=bc_width, sums=not more, gain_row=2 * l,
-                lazy=("right", "lrows", "lgrad", "res", "grad_in") + (("branch",) if more else ()),
+                halves=last, double=0 if more else 2,
+                lazy=("right", "lrows", "res", "grad_in")
+                + (() if last else ("lgrad",)) + (("branch",) if more else ()),
                 middle=functools.partial(backward_middle, inner_all if more else None), **common,
             ),
             "between_backward" if more else "last_backward", 17 + l, inputs, outputs,
@@ -1406,9 +1487,16 @@
         scattered[l] = got["gout"]
         if more:
             grad_rows, token_rows = got["full"], got["inner"]
+        if last:
+            second_part, gradient = lax.optimization_barrier((out[9], gradient))
+            branch_halves.append(scatter_half(second_part))
     grads = list(
-        assemble(scattered, got["sums"], got["gain_sums"], pick, dp_count, heads, bc_width, inner)
+        assemble(
+            scattered, got["sums"], got["gain_sums"], pick, dp_count, heads, bc_width, inner,
+            [residuals[-1], r2_own, *branch_halves],
+        )
     )
+    hidden_out = grads.pop()
     grads[4] = jnp.transpose(grads[4], (1, 2, 0))
     grads[-1] = jnp.transpose(grads[-1], (0, 2, 1))
     return (hidden_out, gradient, *grads)

time: 532 us -> 521 us (0.979)
  Pallas kernels: 501 us -> 483 us
  waiting for transfers between devices: 0.08 us -> 7.23 us
    pallas_call x4, Pallas kernels: 357 us -> 336 us  [comm_call(): pl.pallas_call(functools.partial(comm_kernel, o, names), in_specs=[pl.Blo...]
    all_gather x1 -> x2, waiting for transfers between devices: 0.02 us -> 7.13 us  [gather_half(): return lax.all_gather(v, 'tensor', axis=0)]
  transfers between devices with their start and end apart: 2 -> 4, of which waited for: 0 -> 1; matrix products, arithmetic and copies ran while one was open for 1% -> 1% of each run, Pallas kernels for 56% -> 81%
where the time goes in v7:
time: 521 us; the launch traced here: 514 us
  Pallas kernels  483 us (93%)
  between operations  14.2 us (3%)
  waiting for transfers between devices  7.23 us (1%)
  local copies, waits for them, and re-layouts  5.92 us (1%)
    pallas_call x4, Pallas kernels, comm_call(): pl.pallas_call(functools.partial(comm_kernel, o, names), in_specs=[pl.Blo...  336 us
    pallas_call x2, Pallas kernels, backward_mix(): pl.pallas_call(functools.partial(bwd_kernel, ready, l), grid=(blocks,), i...  73.5 us
    pallas_call x2, Pallas kernels, forward_mix(): pl.pallas_call(functools.partial(fwd_kernel, first, last), grid=(blocks,)...  56.2 us
    pallas_call x1, Pallas kernels, meet(): pl.pallas_call(functools.partial(meet_kernel, n, inner_all), in_specs=[vm...  11.5 us
  transfers between devices with their start and end apart: 4, of which 1 were waited for; matrix products, arithmetic and copies ran while one was open for 1% of the time, Pallas kernels for 81%

profile of v7, /device:TPU:0, one launch (start us, length us, event | category | flops | bytes accessed | tf_op | source)
XLA Modules:
  0.0 514.0 jit_solution(9133887372435882525)
XLA Ops:
  7.3 0.0 all-gather.5.cloned.1.call-start
  7.3 0.8 reshape.60
  8.1 0.7 fusion.3
  8.8 0.7 pad_maximum_fusion
  9.5 0.1 copy.37
  9.7 0.9 copy.38
  10.5 0.1 pad.18.clone
  10.6 0.7 maximum_maximum_fusion.refs_2_.refs_5_
  11.4 61.7 %gather_first.1 = (bf16[1024,1536]{1,0:T(8,128)(2,1)}, f32[8,1536]{1,0:T(8,128)}, bf16[2,2,2,192,2688]{4,3,2,1,0:T(8,128)(2,1)}) custom-call(bf16[256,1536]{1,0:T(8,128)(2,1)} %refs_1_.3, bf16[2,192,256]{2,1,0:T(8,128)(2,1)} %refs_4_.4, bf16[2,192,128]{2,1,0:T(8,128)(2,1)} %maximum_maximum_fusion.refs_2_.refs_5_, bf16[2,192,768]{2,1,0:T(8,128)(2,1)} %refs_6_.1, ...), custom_call_target="tpu_custom_call" | custom-call | tf_op jit(solution)/shard_map/gather_first/pallas_call | solution.py:1127
  73.1 0.9 fusion.4
  74.1 0.0 all-gather.7.cloned.1.call-start
  74.2 0.1 broadcast_in_dim.21
  74.3 0.1 broadcast_in_dim_reshape.4
  74.4 0.8 slice.13
  75.2 0.1 reshape.63
  75.3 0.1 reshape.64
  75.4 0.7 reshape.72.cst_ref
  76.1 0.6 select_maximum_fusion.tiny_ref
  76.7 0.6 maximum_convert_fusion.vec_ref
  77.3 27.6 %mix_forward.2 = (f32[1024,768]{1,0:T(8,128)}, f32[1024,768]{1,0:T(8,128)}, f32[1024,256]{1,0:T(8,128)}, f32[1024,128]{1,0:T(8,128)}, f32[1024,768]{1,0:T(8,128)...) custom-call(bf16[1024,1536]{1,0:T(8,128)(2,1)} %get-tuple-element.92, ...), custom_call_target="tpu_custom_call" | custom-call | tf_op jit(solution)/shard_map/mix_forward/pallas_call | solution.py:244
  104.9 101.3 %between_forward.1 = (bf16[1024,1536]{1,0:T(8,128)(2,1)}, f32[256,1536]{1,0:T(8,128)}, f32[256,1536]{1,0:T(8,128)}, f32[256,128]{1,0:T(8,128)}, bf16[2,2,2,192,2688]{4,3,2,1,0:T(8,128)(2,1)}) custom-call(bf16[1024,1536]{1,0:T(8,128)(2,1)} %get-tuple-element.95.refs_0_, f32[8,1024]{1,0:T(8,128)} %get-tuple-element.96.refs_1_, bf16[256,1536]{1,0:T(8,128)(2,1)} %refs_1_.3, ...), custom_call_target="tpu_custom_call" | custom-call | tf_op jit(solution)/shard_map/between_forward/pallas_call | solution.py:1127
  206.2 0.3 reduce-scatter.3.cloned.1.call-start
  206.5 28.6 %mix_forward.3 = (f32[1024,768]{1,0:T(8,128)}, f32[1024,768]{1,0:T(8,128)}, f32[1024,256]{1,0:T(8,128)}, f32[1024,128]{1,0:T(8,128)}, f32[1024,768]{1,0:T(8,128)...) custom-call(bf16[1024,1536]{1,0:T(8,128)(2,1)} %get-tuple-element.98, ...), custom_call_target="tpu_custom_call" | custom-call | tf_op jit(solution)/shard_map/mix_forward/pallas_call | solution.py:244
  235.2 0.3 reduce-scatter.5.cloned.1.call-start
  235.5 7.1 %all-gather.7.cloned.1.call-done = bf16[512,1536]{1,0:T(8,128)(2,1)} async-done(((bf16[128,1536]{1,0:T(8,128)(2,1)}), bf16[512,1536]{1,0:T(8,128)(2,1)}) %all-gather.7.cloned.1.call-update) | async-done | bytes 1572880 | tf_op jit(solution)/shard_map/all_gather | solution.py:1391
  242.6 11.5 %turn_around.1 = (f32[8,1024]{1,0:T(8,128)}, f32[256,128]{1,0:T(8,128)}, f32[4,128,768]{2,1,0:T(8,128)}) custom-call(f32[8,1024]{1,0:T(8,128)} %get-tuple-element.101.own_ref, bf16[4,128,1536]{2,1,0:T(8,128)(2,1)} %bitcast.33, bf16[4,128,768]{2,1,0:T(8,128)(2,1)} %get-tuple-element.103.mixed_ref, bf16[1536,2688]{1,0:T(8,128)(2,1)} %bitcast.27), custom_call_target="tpu_custom_call" | custom-call | tf_op jit(solution)/shard_map/turn_around/pallas_call | solution.py:1192
  254.1 35.8 %mix_backward.2 = (bf16[1024,2688]{1,0:T(8,128)(2,1)}, bf16[1024,1536]{1,0:T(8,128)(2,1)}, f32[8,768]{1,0:T(8,128)}, f32[8,256]{1,0:T(8,128)}, f32[8,128]{1,0:T(8,128)}, /*index=5*/f32[8,1536]{1,0:T(8,128)}) custom-call(f32[4,128,768]{2,1,0:T(8,128)} %get-tuple-element.100.gb_ref, f32[8,1024]{1,0:T(8,128)} %get-tuple-element.104.e_ref, ...), custom_call_target="tpu_custom_call" | custom-call | tf_op jit(solution)/shard_map/mix_backward/pallas_call | solution.py:457
  290.0 102.0 %between_backward.1 = (f32[256,1536]{1,0:T(8,128)}, f32[192,2688]{1,0:T(8,128)}, bf16[1024,1536]{1,0:T(8,128)(2,1)}, f32[8,1024]{1,0:T(8,128)}) custom-call(bf16[1024,1536]{1,0:T(8,128)(2,1)} %get-tuple-element.113.refs_0_, f32[256,1536]{1,0:T(8,128)} %get-tuple-element.114.refs_1_.refs_5_, f32[8,1536]{1,0:T(8,128)} %get-tuple-element.94.gain_ref.refs_3_.refs_2_, ...), custom_call_target="tpu_custom_call" | custom-call | tf_op jit(solution)/shard_map/between_backward/pallas_call | solution.py:1127
  392.0 37.6 %mix_backward.3 = (bf16[1024,2688]{1,0:T(8,128)(2,1)}, bf16[1024,1536]{1,0:T(8,128)(2,1)}, f32[8,768]{1,0:T(8,128)}, f32[8,256]{1,0:T(8,128)}, f32[8,128]{1,0:T(8,128)}, /*index=5*/f32[8,1536]{1,0:T(8,128)}) custom-call(bf16[1024,1536]{1,0:T(8,128)(2,1)} %get-tuple-element.118.gb_ref.refs_6_, f32[8,1024]{1,0:T(8,128)} %get-tuple-element.119.e_ref, ...), custom_call_target="tpu_custom_call" | custom-call | tf_op jit(solution)/shard_map/mix_backward/pallas_call | solution.py:457
  429.6 70.5 %last_backward.1 = (f32[256,1536]{1,0:T(8,128)}, f32[192,2688]{1,0:T(8,128)}, f32[8,2304]{1,0:T(8,128)}, f32[8,1536]{1,0:T(8,128)}) custom-call(bf16[1024,1536]{1,0:T(8,128)(2,1)} %get-tuple-element.128.refs_0_, bf16[256,1536]{1,0:T(8,128)(2,1)} %refs_1_.3, f32[8,1536]{1,0:T(8,128)} %get-tuple-element.94.gain_ref.refs_3_.refs_2_, ...), custom_call_target="tpu_custom_call" | custom-call | tf_op jit(solution)/shard_map/last_backward/pallas_call | solution.py:1127
  500.2 5.9 %assemble.1 = (f32[2,192]{1,0:T(2,128)}, f32[2,192,768]{2,1,0:T(8,128)}, f32[2,192,768]{2,1,0:T(8,128)}, f32[2,192,256]{2,1,0:T(8,128)}, f32[12,2,192]{2,1,0:T(2...) custom-call(f32[192,2688]{1,0:T(8,128)} %get-tuple-element.141.refs_, ...), custom_call_target="tpu_custom_call" | custom-call | tf_op jit(solution)/shard_map/assemble/pallas_call | solution.py:1303
  506.1 1.1 copy.52
  (32 shorter events, 0.2 us)
Async XLA Ops:
  7.2 65.9 %copy-start = (bf16[256,1536]{1,0:T(8,128)(2,1)S(1)}, bf16[256,1536]{1,0:T(8,128)(2,1)}, u32[]{:S(2)}) copy-start(bf16[256,1536]{1,0:T(8,128)(2,1)} %refs_3_.2) | copy-start | bytes 2359300
  7.2 67.0 %copy-start.3 = (bf16[2,768]{1,0:T(2,128)(2,1)S(1)}, bf16[2,768]{1,0:T(2,128)(2,1)}, u32[]{:S(2)}) copy-start(bf16[2,768]{1,0:T(2,128)(2,1)} %param.25) | copy-start | bytes 9220
  7.2 67.0 %copy-start.4 = (bf16[2,768]{1,0:T(2,128)(2,1)S(1)}, bf16[2,768]{1,0:T(2,128)(2,1)}, u32[]{:S(2)}) copy-start(bf16[2,768]{1,0:T(2,128)(2,1)} %param.31) | copy-start | bytes 9220
  7.2 67.0 %copy-start.5 = (bf16[2,12]{1,0:T(2,128)(2,1)S(1)}, bf16[2,12]{1,0:T(2,128)(2,1)}, u32[]{:S(2)}) copy-start(bf16[2,12]{1,0:T(2,128)(2,1)} %param.30) | copy-start | bytes 148
  7.2 68.8 %copy-start.6 = (bf16[2,12]{1,0:T(2,128)(2,1)S(1)}, bf16[2,12]{1,0:T(2,128)(2,1)}, u32[]{:S(2)}) copy-start(bf16[2,12]{1,0:T(2,128)(2,1)} %param.28) | copy-start | bytes 148
  7.2 68.8 %copy-start.7 = (bf16[2,12]{1,0:T(2,128)(2,1)S(1)}, bf16[2,12]{1,0:T(2,128)(2,1)}, u32[]{:S(2)}) copy-start(bf16[2,12]{1,0:T(2,128)(2,1)} %param.29) | copy-start | bytes 148
  7.2 69.4 %copy-start.2 = (bf16[2,4,768]{2,1,0:T(4,128)(2,1)S(1)}, bf16[2,4,768]{2,1,0:T(4,128)(2,1)}, u32[]{:S(2)}) copy-start(bf16[2,4,768]{2,1,0:T(4,128)(2,1)} %param.24) | copy-start | bytes 36868
  7.3 199.3 %all-gather.5.cloned.1.call-start = ((), (), s32[]{:S(2)}) async-start(), calls=%async_computation.4 | async-start | bytes 1966080 | tf_op jit(solution)/shard_map/all_gather | solution.py:1391
  74.1 168.5 %all-gather.7.cloned.1.call-start = ((), (), s32[]{:S(2)}) async-start(), calls=%async_computation.5 | async-start | bytes 1966080 | tf_op jit(solution)/shard_map/all_gather | solution.py:1391
  206.2 293.9 %reduce-scatter.3.cloned.1.call-start = ((), (), s32[]{:S(2)}) async-start(), calls=%async_computation.2 | async-start | bytes 1966080 | tf_op jit(solution)/shard_map/reduce_scatter | solution.py:1429
  235.2 265.0 %reduce-scatter.5.cloned.1.call-start = ((), (), s32[]{:S(2)}) async-start(), calls=%async_computation.3 | async-start | bytes 1966080 | tf_op jit(solution)/shard_map/reduce_scatter | solution.py:1429
  500.2 5.9 %copy-start.1 = (f32[256,1536]{1,0:T(8,128)S(1)}, f32[256,1536]{1,0:T(8,128)}, u32[]{:S(2)}) copy-start(f32[256,1536]{1,0:T(8,128)} %get-tuple-element.183) | copy-start | bytes 4718596
Sparse Core Ops, SparseCore 0:
  74.2 36.3 all-gather.4
  206.4 36.1 all-gather.6
  244.9 34.1 reduce-scatter.2
  392.1 35.2 reduce-scatter.4

commit v8 on v7

--- a/solution.py
+++ b/solution.py
@@ -14,6 +14,7 @@
 BF = jnp.bfloat16
 F32 = jnp.float32
 WIDTH = 64
+GAIN_ROWS = 6
 MIB = 1024 * 1024
 WCHUNK = 384
 
@@ -186,8 +187,8 @@
     if not last:
         part_ref[...] = part
     else:
-        cut = length // 2
-        part_ref[0], part2_ref[0] = part[:cut], part[cut:]
+        part_ref[0], part2_ref[0] = part[: length // 2], part[length // 2 :]
+        cut = gb_ref.shape[1]
         mixed_ref[0] = mixed[cut:]
         dm = nn(gb_ref[0], wot_ref[...])
         dm_ref[0] = dm
@@ -233,20 +234,23 @@
         ((tokens, inner), F32, tok(inner)),
         ((8, tokens), F32, pl.BlockSpec((8, q), lambda i: (0, i))),
     ]
-    half_of = lambda n: pl.BlockSpec((1, q // 2, n), lambda i: (i, 0, 0))
+    half_of = lambda rows, n: pl.BlockSpec((1, rows, n), lambda i: (i, 0, 0))
     if not last:
         outs.append(((tokens, width), BF, tok(width)))
     if first:
         outs.append(((tokens, width), BF, tok(width)))
     if last:
-        for n, kind in ((width, BF), (width, BF), (inner, F32), (inner, BF)):
-            outs.append(((blocks, q // 2, n), kind, half_of(n)))
+        cut = gb.shape[1]
+        for r, n, kind in (
+            (q // 2, width, BF), (q // 2, width, BF), (cut, inner, F32), (q - cut, inner, BF)
+        ):
+            outs.append(((blocks, r, n), kind, half_of(r, n)))
     return pl.pallas_call(
         functools.partial(fwd_kernel, first, last),
         grid=(blocks,),
         in_specs=[tok(width), whole(packed.shape)]
         + layer_specs(params, l)
-        + ([half_of(width)] if last else []),
+        + ([half_of(cut, width)] if last else []),
         out_specs=[o[2] for o in outs],
         out_shape=[jax.ShapeDtypeStruct(o[0], o[1]) for o in outs],
         scratch_shapes=[
@@ -425,7 +429,7 @@
 
     @pl.when(step == blocks - 1)
     def _():
-        ggain_ref[0:1, :] = ggain_ref[0:1, :] / gain_ref[2 * layer : 2 * layer + 1, :]
+        ggain_ref[0:1, :] = ggain_ref[0:1, :] / gain_ref[GAIN_ROWS * layer : GAIN_ROWS * layer + 1, :]
 
 
 def backward_mix(gb, ready, e_rows, rows, kept, packed, params, pick, l):
@@ -452,13 +456,13 @@
         ((8, dt_width), F32, fixed(8, dt_width)),
         ((8, width), F32, fixed(8, width)),
     ]
-    half_of = pl.BlockSpec((1, q // 2, inner), lambda i: (back(i), 0, 0))
+    half_of = lambda v: pl.BlockSpec((1,) + v.shape[1:], lambda i: (back(i), 0, 0))
     gb, more = (gb[0], [gb[1]]) if ready else (gb, [])
     return pl.pallas_call(
         functools.partial(bwd_kernel, ready, l),
         grid=(blocks,),
         in_specs=[
-            half_of if ready else tok(width),
+            half_of(gb) if ready else tok(width),
             pl.BlockSpec((8, q), lambda i: (0, back(i))),
             tok(width),
             tok(inner), tok(inner), tok(bc_width), halo(bc_width), tok(dt_width),
@@ -467,7 +471,7 @@
             tok(inner),
         ]
         + [whole(packed.shape)] + layer_specs(params, l) + [whole(pick.shape)]
-        + [half_of] * len(more),
+        + [half_of(v) for v in more],
         out_specs=[o[2] for o in outs],
         out_shape=[jax.ShapeDtypeStruct(o[0], o[1]) for o in outs],
         scratch_shapes=[
@@ -509,6 +513,7 @@
         self.sums = False
         self.bits = 0
         self.middle = None
+        self.early = ()
         self.halves = False
         self.lazy = ()
         self.__dict__.update(given)
@@ -548,9 +553,17 @@
         near = getattr(r, name + "_v")
         lazy.append(pltpu.make_async_copy(getattr(r, name), near, r.lazy_sem.at[i]))
         setattr(r, name, near)
+    leaving = []
+    for i, name in enumerate(o.early):
+        near = getattr(r, name + "_v")
+        leaving.append((near, getattr(r, name), r.early_sem.at[i]))
+        setattr(r, name, near)
     if o.halves:
+        start = 0
         for i, far in enumerate((r.half0, r.half1)):
-            lazy.append(pltpu.make_async_copy(far, r.lgrad.at[:, i], r.half_sem.at[i]))
+            near = r.lgrad.at[:, pl.ds(start, far.shape[1])]
+            lazy.append(pltpu.make_async_copy(far, near, r.half_sem.at[i]))
+            start += far.shape[1]
     for copy in lazy:
         copy.start()
 
@@ -701,7 +714,7 @@
         def _():
             small_columns().wait()
             turned = r.columns[...].reshape(o.width, 128).astype(F32).T
-            r.small[...] = turned[o.small % 128 : o.small % 128 + 8, :]
+            r.small[...] = turned[o.small % 128 : o.small % 128 + 16, :]
 
     def own_weights():
         return pltpu.make_async_copy(r.wown, r.wfull.at[spots([])], r.wl_sem)
@@ -810,10 +823,17 @@
                     if stage < o.bits:
                         r.grad[(j, *full)] = total.astype(BF)
                     else:
-                        r.gout[:, cols(j)] = total
+                        r.gnear[:, cols(j)] = total
+
+                        @when(j > 0)
+                        def _():
+                            grad_leave(j).start()
                 if stage < o.bits:
                     grad_copy(parity, stage, j).start()
             each_chunk(tau - grad_lag(stage), run)
+
+    def grad_leave(j):
+        return pltpu.make_async_copy(r.gnear.at[:, cols(j)], r.gout.at[:, cols(j)], r.leave_sem)
 
     def grad_lag(stage):
         return o.lag * (2 * stage - 1) if stage else 0
@@ -880,7 +900,7 @@
         @when(tau == at_first)
         def _():
             for s in range(n):
-                r.qsend[s] = r.gout[s * quarter : (s + 1) * quarter, 0 : o.states].astype(BF)
+                r.qsend[s] = r.gnear[s * quarter : (s + 1) * quarter, 0 : o.states].astype(BF)
             for k in range(1, n):
                 state_out(k).start()
 
@@ -962,6 +982,9 @@
             def _():
                 own_total(c_own)
                 out = o.middle(r, piece(c_own), r.acc[...])
+                for near, far, sem in leaving:
+                    spot = piece(c_own)
+                    pltpu.make_async_copy(near.at[spot], far.at[spot], sem).start()
                 if o.late:
                     r.full[at(t, c_own), :] = out
         if o.gather:
@@ -1017,7 +1040,8 @@
         shared(r.qall, r.qa_send, r.qa_recv)
         quarter = r.gout.shape[0] // n
         for s in range(n):
-            r.gout[s * quarter : (s + 1) * quarter, 0 : o.states] = r.qall[s].astype(F32)
+            r.gnear[s * quarter : (s + 1) * quarter, 0 : o.states] = r.qall[s].astype(F32)
+        grad_leave(jnp.int32(0)).start()
         for k in range(1, n):
             state_out(k).wait_send()
             share(r.qall, r.qa_send, r.qa_recv, k).wait_send()
@@ -1049,6 +1073,10 @@
     for j in range(o.grads):
         for stage in range(o.bits):
             grad_copy(j % 2, stage, jnp.int32(j)).wait_send()
+    if o.grads:
+        pltpu.make_async_copy(r.gnear, r.gout, r.leave_sem).wait()
+    for near, far, sem in leaving:
+        pltpu.make_async_copy(near, far, sem).wait()
 
 
 def comm_call(o, name, collective, inputs, outputs, **scratch):
@@ -1060,8 +1088,14 @@
             inputs[key] = (value, pl.ANY)
             scratch[key + "_v"] = pltpu.VMEM(value.shape, value.dtype)
         scratch.update(lazy_sem=dma((len(o.lazy),)))
+    if o.early:
+        for key in o.early:
+            shape, kind, _ = outputs[key]
+            outputs[key] = (shape, kind, pl.ANY)
+            scratch[key + "_v"] = pltpu.VMEM(shape, kind)
+        scratch.update(early_sem=dma((len(o.early),)))
     if o.halves:
-        scratch.update(lgrad=pltpu.VMEM((n, 2, rows // 2, width), BF), half_sem=dma((2,)))
+        scratch.update(lgrad=pltpu.VMEM((n, rows, width), BF), half_sem=dma((2,)))
     if o.partial:
         scratch.update(
             rbuf=pltpu.VMEM((n, rows, width), BF),
@@ -1102,6 +1136,9 @@
             scratch["gbuf%d" % stage] = pltpu.VMEM(
                 (o.grads, *(2,) * (o.bits - 1 - stage), depth, WCHUNK), BF
             )
+        scratch.update(
+            gnear=pltpu.VMEM(outputs["gout"][0], F32), leave_sem=dma(()),
+        )
         part = (n, (width >> o.bits) // n, o.states)
         scratch.update(
             qsend=pltpu.VMEM(part, BF), qall=pltpu.VMEM(part, BF),
@@ -1253,9 +1290,10 @@
     res, scale, *halves = refs[:4]
     norm, gz, gx, gbc, gdt, cv, cvb, cs, csb, sb, ld, sk, gg, po, hidden = refs[4:]
     me = lax.axis_index("dp")
-    cut = halves[0].shape[0]
-    for i, half in enumerate(halves):
-        at = slice(i * cut, (i + 1) * cut)
+    start = 0
+    for half in halves:
+        at = slice(start, start + half.shape[0])
+        start += half.shape[0]
         hidden[at, :] = res[at, :] + scale[at, 0:1] * half[...].astype(F32)
 
     def own(v):
@@ -1341,14 +1379,16 @@
     column_chunks, row_chunks = packed_width // WCHUNK, shard_rows // 16
     vmem, far = pltpu.VMEM, pl.ANY
 
-    small = jnp.concatenate([conv_state.reshape(layers, -1), conv_state_bias], axis=1)
-    small = jnp.pad(small, ((0, 0), (0, shard_rows - small.shape[1])))
-    extra = jnp.stack([norm_gain, small], axis=1).reshape(2 * layers, shard_rows).T
+    taps = jnp.concatenate([conv_state, conv_state_bias[:, None]], axis=1)
+    taps = jnp.pad(taps, ((0, 0), (0, 0), (0, shard_rows - taps.shape[2])))
+    extra = jnp.concatenate([norm_gain[:, None], taps], axis=1)
+    per_layer = extra.shape[1]
+    extra = extra.reshape(per_layer * layers, shard_rows).T
     step_block = jnp.concatenate(
         [
             proj_dt,
             jnp.broadcast_to(extra[None], (layers,) + extra.shape),
-            jnp.zeros((layers, shard_rows, 128 - heads - 2 * layers), BF),
+            jnp.zeros((layers, shard_rows, 128 - heads - extra.shape[1]), BF),
         ],
         axis=2,
     )
@@ -1381,11 +1421,11 @@
              small=bc_width + heads, **common),
         "gather_first", 1,
         dict(own=(hidden_in, vmem), **weight_in),
-        dict(full=whole_rows, small=((8, width), F32, vmem), **weight_out),
+        dict(full=whole_rows, small=((16, width), F32, vmem), **weight_out),
     )
     x_rows = got["full"]
     out_grad, x_rows = lax.optimization_barrier((out_grad, x_rows))
-    cut = rows_own // 2
+    cut = rows_own * 5 // 8
 
     def gather_half(v):
         return lax.all_gather(v, "tensor", axis=0)
@@ -1394,9 +1434,8 @@
     packed = [got["wfull"].reshape(width, packed_width)]
     small = got["small"]
     per = bc_width // dp_count
-    smalls = small[1 : 2 * layers : 2].reshape(layers, dp_count, shard_rows)[:, :, : 5 * per]
-    cst = jnp.transpose(smalls.reshape(layers, dp_count, 5, per), (0, 2, 1, 3))
-    cst = cst.reshape(layers, 5, bc_width)
+    smalls = small[: per_layer * layers].reshape(layers, per_layer, dp_count, shard_rows)
+    cst = smalls[:, 1:, :, :per].reshape(layers, per_layer - 1, bc_width)
     params = (vec, cst, tiny, small)
 
     out = forward_mix(x_rows, packed[0], params, 0)
@@ -1406,7 +1445,8 @@
         got = comm_call(
             Step(
                 partial=True, gather=True, late=True, scale=inner_all, middle=forward_middle, chunks=16,
-                weights=row_chunks, layer=l + 1, gain_row=2 * (l + 1), **common,
+                early=("branch", "res_out"),
+                weights=row_chunks, layer=l + 1, gain_row=per_layer * (l + 1), **common,
             ),
             "between_forward", 2 + l,
             dict(part=(out[8], vmem), ssq=(out[7], vmem), res=(residuals[l], vmem),
@@ -1455,7 +1495,7 @@
             inputs.update(lgrad=(grad_rows, vmem))
         outputs = dict(
             grad_out=own_rows,
-            gout=((shard_rows, packed_width), F32, vmem),
+            gout=((shard_rows, packed_width), F32, far),
         )
         if more:
             inputs.update(r2=(r2s[l - 1], vmem), branch=(branches[l - 1], vmem))
@@ -1475,8 +1515,8 @@
             Step(
                 partial=True, gather=more, late=more, inner=more, grads=column_chunks,
                 chunks=16 if more else 8, lag=2 if more else 1,
-                states=bc_width, sums=not more, gain_row=2 * l,
-                halves=last, double=0 if more else 2,
+                states=bc_width, sums=not more, gain_row=per_layer * l,
+                early=("grad_out",), halves=last, double=0 if more else 2,
                 lazy=("right", "lrows", "res", "grad_in")
                 + (() if last else ("lgrad",)) + (("branch",) if more else ()),
                 middle=functools.partial(backward_middle, inner_all if more else None), **common,

time: 521 us -> 515 us (0.988)
  waiting for transfers between devices: 7.23 us -> 0.14 us
    all_gather x2, waiting for transfers between devices: 7.13 us -> 0.04 us  [gather_half(): return lax.all_gather(v, 'tensor', axis=0)]
  transfers between devices with their start and end apart: 4 -> 4, of which waited for: 1 -> 0; matrix products, arithmetic and copies ran while one was open for 1% -> 1% of each run, Pallas kernels for 81% -> 82%
where the time goes in v8:
time: 515 us; the launch traced here: 509 us
  Pallas kernels  484 us (94%)
  between operations  14.2 us (3%)
  local copies, waits for them, and re-layouts  7.05 us (1%)
    pallas_call x4, Pallas kernels, comm_call(): pl.pallas_call(functools.partial(comm_kernel, o, names), in_specs=[pl.Blo...  336 us
    pallas_call x2, Pallas kernels, backward_mix(): pl.pallas_call(functools.partial(bwd_kernel, ready, l), grid=(blocks,), i...  73.7 us
    pallas_call x2, Pallas kernels, forward_mix(): pl.pallas_call(functools.partial(fwd_kernel, first, last), grid=(blocks,)...  56.5 us
    pallas_call x1, Pallas kernels, meet(): pl.pallas_call(functools.partial(meet_kernel, n, inner_all), in_specs=[vm...  11.4 us
  transfers between devices with their start and end apart: 4, of which 0 were waited for; matrix products, arithmetic and copies ran while one was open for 1% of the time, Pallas kernels for 82%

profile of v8, /device:TPU:0, one launch (start us, length us, event | category | flops | bytes accessed | tf_op | source)
XLA Modules:
  0.0 508.7 jit_solution(8075785454803928192)
XLA Ops:
  7.3 0.0 all-gather.5.cloned.1.call-start
  7.3 0.7 copy.38
  8.0 0.7 copy.39
  8.7 0.7 fusion.2
  9.4 0.1 copy.40
  9.6 0.9 copy.41
  10.4 0.1 pad.18.clone
  10.5 0.7 maximum_maximum_fusion.refs_2_.refs_5_
  11.3 61.8 %gather_first.1 = (bf16[1024,1536]{1,0:T(8,128)(2,1)}, f32[16,1536]{1,0:T(8,128)}, bf16[2,2,2,192,2688]{4,3,2,1,0:T(8,128)(2,1)}) custom-call(bf16[256,1536]{1,0:T(8,128)(2,1)} %refs_1_.3, bf16[2,192,256]{2,1,0:T(8,128)(2,1)} %refs_4_.4, bf16[2,192,128]{2,1,0:T(8,128)(2,1)} %maximum_maximum_fusion.refs_2_.refs_5_, bf16[2,192,768]{2,1,0:T(8,128)(2,1)} %refs_6_.1, ...), custom_call_target="tpu_custom_call" | custom-call | tf_op jit(solution)/shard_map/gather_first/pallas_call | solution.py:1164
  73.0 0.8 slice.15
  73.9 0.0 all-gather.7.cloned.1.call-start
  73.9 0.7 slice.12
  74.7 0.1 broadcast_in_dim.29
  74.8 0.1 broadcast_in_dim_reshape.4
  74.9 1.0 reshape.56
  75.9 0.7 reshape.64.cst_ref
  76.6 0.6 select_maximum_fusion.tiny_ref
  77.2 0.6 maximum_convert_fusion.vec_ref
  77.8 27.8 %mix_forward.2 = (f32[1024,768]{1,0:T(8,128)}, f32[1024,768]{1,0:T(8,128)}, f32[1024,256]{1,0:T(8,128)}, f32[1024,128]{1,0:T(8,128)}, f32[1024,768]{1,0:T(8,128)...) custom-call(bf16[1024,1536]{1,0:T(8,128)(2,1)} %get-tuple-element.92, ...), custom_call_target="tpu_custom_call" | custom-call | tf_op jit(solution)/shard_map/mix_forward/pallas_call | solution.py:248
  105.6 102.6 %between_forward.1 = (bf16[1024,1536]{1,0:T(8,128)(2,1)}, f32[256,1536]{1,0:T(8,128)}, f32[256,1536]{1,0:T(8,128)}, f32[256,128]{1,0:T(8,128)}, bf16[2,2,2,192,2688]{4,3,2,1,0:T(8,128)(2,1)}) custom-call(bf16[1024,1536]{1,0:T(8,128)(2,1)} %get-tuple-element.95.refs_0_, f32[8,1024]{1,0:T(8,128)} %get-tuple-element.96.refs_1_, bf16[256,1536]{1,0:T(8,128)(2,1)} %refs_1_.3, ...), custom_call_target="tpu_custom_call" | custom-call | tf_op jit(solution)/shard_map/between_forward/pallas_call | solution.py:1164
  208.3 0.3 reduce-scatter.3.cloned.1.call-start
  208.5 0.0 all-gather.5.cloned.1.call-done
  208.6 28.7 %mix_forward.3 = (f32[1024,768]{1,0:T(8,128)}, f32[1024,768]{1,0:T(8,128)}, f32[1024,256]{1,0:T(8,128)}, f32[1024,128]{1,0:T(8,128)}, f32[1024,768]{1,0:T(8,128)...) custom-call(bf16[1024,1536]{1,0:T(8,128)(2,1)} %get-tuple-element.98, ...), custom_call_target="tpu_custom_call" | custom-call | tf_op jit(solution)/shard_map/mix_forward/pallas_call | solution.py:248
  237.3 0.3 reduce-scatter.5.cloned.1.call-start
  237.6 11.4 %turn_around.1 = (f32[8,1024]{1,0:T(8,128)}, f32[256,128]{1,0:T(8,128)}, f32[4,96,768]{2,1,0:T(8,128)}) custom-call(f32[8,1024]{1,0:T(8,128)} %get-tuple-element.101.own_ref, bf16[4,96,1536]{2,1,0:T(8,128)(2,1)} %bitcast.32, bf16[4,96,768]{2,1,0:T(8,128)(2,1)} %get-tuple-element.103.mixed_ref, bf16[1536,2688]{1,0:T(8,128)(2,1)} %bitcast.25), custom_call_target="tpu_custom_call" | custom-call | tf_op jit(solution)/shard_map/turn_around/pallas_call | solution.py:1229
  249.1 35.9 %mix_backward.2 = (bf16[1024,2688]{1,0:T(8,128)(2,1)}, bf16[1024,1536]{1,0:T(8,128)(2,1)}, f32[8,768]{1,0:T(8,128)}, f32[8,256]{1,0:T(8,128)}, f32[8,128]{1,0:T(8,128)}, /*index=5*/f32[8,1536]{1,0:T(8,128)}) custom-call(f32[4,160,768]{2,1,0:T(8,128)} %get-tuple-element.100.gb_ref, f32[8,1024]{1,0:T(8,128)} %get-tuple-element.104.e_ref, ...), custom_call_target="tpu_custom_call" | custom-call | tf_op jit(solution)/shard_map/mix_backward/pallas_call | solution.py:461
  285.0 102.0 %between_backward.1 = (f32[256,1536]{1,0:T(8,128)}, f32[192,2688]{1,0:T(8,128)}, bf16[1024,1536]{1,0:T(8,128)(2,1)}, f32[8,1024]{1,0:T(8,128)}) custom-call(bf16[1024,1536]{1,0:T(8,128)(2,1)} %get-tuple-element.113.refs_0_, f32[256,1536]{1,0:T(8,128)} %get-tuple-element.114.refs_1_.refs_5_, f32[16,1536]{1,0:T(8,128)} %get-tuple-element.94.gain_ref.refs_3_.refs_2_, ...), custom_call_target="tpu_custom_call" | custom-call | tf_op jit(solution)/shard_map/between_backward/pallas_call | solution.py:1164
  387.0 37.8 %mix_backward.3 = (bf16[1024,2688]{1,0:T(8,128)(2,1)}, bf16[1024,1536]{1,0:T(8,128)(2,1)}, f32[8,768]{1,0:T(8,128)}, f32[8,256]{1,0:T(8,128)}, f32[8,128]{1,0:T(8,128)}, /*index=5*/f32[8,1536]{1,0:T(8,128)}) custom-call(bf16[1024,1536]{1,0:T(8,128)(2,1)} %get-tuple-element.118.gb_ref.refs_6_, f32[8,1024]{1,0:T(8,128)} %get-tuple-element.119.e_ref, ...), custom_call_target="tpu_custom_call" | custom-call | tf_op jit(solution)/shard_map/mix_backward/pallas_call | solution.py:461
  424.8 70.0 %last_backward.1 = (f32[256,1536]{1,0:T(8,128)}, f32[192,2688]{1,0:T(8,128)}, f32[8,2304]{1,0:T(8,128)}, f32[8,1536]{1,0:T(8,128)}) custom-call(bf16[1024,1536]{1,0:T(8,128)(2,1)} %get-tuple-element.128.refs_0_, bf16[256,1536]{1,0:T(8,128)(2,1)} %refs_1_.3, f32[16,1536]{1,0:T(8,128)} %get-tuple-element.94.gain_ref.refs_3_.refs_2_, ...), custom_call_target="tpu_custom_call" | custom-call | tf_op jit(solution)/shard_map/last_backward/pallas_call | solution.py:1164
  494.8 0.0 reduce-scatter.3.cloned.1.call-done.refs_7_
  494.9 5.9 %assemble.1 = (f32[2,192]{1,0:T(2,128)}, f32[2,192,768]{2,1,0:T(8,128)}, f32[2,192,768]{2,1,0:T(8,128)}, f32[2,192,256]{2,1,0:T(8,128)}, f32[12,2,192]{2,1,0:T(2...) custom-call(f32[192,2688]{1,0:T(8,128)} %get-tuple-element.141.refs_, ...), custom_call_target="tpu_custom_call" | custom-call | tf_op jit(solution)/shard_map/assemble/pallas_call | solution.py:1341
  500.8 1.1 copy.55
  (31 shorter events, 0.2 us)
Async XLA Ops:
  7.2 65.9 %copy-start = (bf16[256,1536]{1,0:T(8,128)(2,1)S(1)}, bf16[256,1536]{1,0:T(8,128)(2,1)}, u32[]{:S(2)}) copy-start(bf16[256,1536]{1,0:T(8,128)(2,1)} %refs_3_.2) | copy-start | bytes 2359300
  7.2 67.5 %copy-start.3 = (bf16[2,768]{1,0:T(2,128)(2,1)S(1)}, bf16[2,768]{1,0:T(2,128)(2,1)}, u32[]{:S(2)}) copy-start(bf16[2,768]{1,0:T(2,128)(2,1)} %param.25) | copy-start | bytes 9220
  7.2 67.5 %copy-start.4 = (bf16[2,768]{1,0:T(2,128)(2,1)S(1)}, bf16[2,768]{1,0:T(2,128)(2,1)}, u32[]{:S(2)}) copy-start(bf16[2,768]{1,0:T(2,128)(2,1)} %param.31) | copy-start | bytes 9220
  7.2 67.5 %copy-start.5 = (bf16[2,12]{1,0:T(2,128)(2,1)S(1)}, bf16[2,12]{1,0:T(2,128)(2,1)}, u32[]{:S(2)}) copy-start(bf16[2,12]{1,0:T(2,128)(2,1)} %param.30) | copy-start | bytes 148
  7.2 69.3 %copy-start.6 = (bf16[2,12]{1,0:T(2,128)(2,1)S(1)}, bf16[2,12]{1,0:T(2,128)(2,1)}, u32[]{:S(2)}) copy-start(bf16[2,12]{1,0:T(2,128)(2,1)} %param.28) | copy-start | bytes 148
  7.2 69.3 %copy-start.7 = (bf16[2,12]{1,0:T(2,128)(2,1)S(1)}, bf16[2,12]{1,0:T(2,128)(2,1)}, u32[]{:S(2)}) copy-start(bf16[2,12]{1,0:T(2,128)(2,1)} %param.29) | copy-start | bytes 148
  7.2 69.9 %copy-start.2 = (bf16[2,4,768]{2,1,0:T(4,128)(2,1)S(1)}, bf16[2,4,768]{2,1,0:T(4,128)(2,1)}, u32[]{:S(2)}) copy-start(bf16[2,4,768]{2,1,0:T(4,128)(2,1)} %param.24) | copy-start | bytes 36868
  7.3 201.3 %all-gather.5.cloned.1.call-start = ((), (), s32[]{:S(2)}) async-start(), calls=%async_computation.4 | async-start | bytes 2457600 | tf_op jit(solution)/shard_map/all_gather | solution.py:1431
  73.9 163.7 %all-gather.7.cloned.1.call-start = ((), (), s32[]{:S(2)}) async-start(), calls=%async_computation.5 | async-start | bytes 1474560 | tf_op jit(solution)/shard_map/all_gather | solution.py:1431
  208.3 286.6 %reduce-scatter.3.cloned.1.call-start = ((), (), s32[]{:S(2)}) async-start(), calls=%async_computation.2 | async-start | bytes 1966080 | tf_op jit(solution)/shard_map/reduce_scatter | solution.py:1469
  237.3 257.6 %reduce-scatter.5.cloned.1.call-start = ((), (), s32[]{:S(2)}) async-start(), calls=%async_computation.3 | async-start | bytes 1966080 | tf_op jit(solution)/shard_map/reduce_scatter | solution.py:1469
  494.9 5.9 %copy-start.1 = (f32[256,1536]{1,0:T(8,128)S(1)}, f32[256,1536]{1,0:T(8,128)}, u32[]{:S(2)}) copy-start(f32[256,1536]{1,0:T(8,128)} %get-tuple-element.181) | copy-start | bytes 4718596
Sparse Core Ops, SparseCore 0:
  74.0 43.3 all-gather.4
  208.4 29.1 all-gather.6
  239.9 34.3 reduce-scatter.2
  387.1 34.6 reduce-scatter.4

commit v9 on v8

--- a/solution.py
+++ b/solution.py
@@ -1514,7 +1514,7 @@
         got = comm_call(
             Step(
                 partial=True, gather=more, late=more, inner=more, grads=column_chunks,
-                chunks=16 if more else 8, lag=2 if more else 1,
+                chunks=16 if more else 8, lag=3 if more else 1,
                 states=bc_width, sums=not more, gain_row=per_layer * l,
                 early=("grad_out",), halves=last, double=0 if more else 2,
                 lazy=("right", "lrows", "res", "grad_in")

time: 515 us -> 513 us (level)
  no operation moved by 1% of the time
where the time goes in v9:
time: 513 us; the launch traced here: 506 us
  Pallas kernels  481 us (94%)
  between operations  14.2 us (3%)
  local copies, waits for them, and re-layouts  7.05 us (1%)
    pallas_call x4, Pallas kernels, comm_call(): pl.pallas_call(functools.partial(comm_kernel, o, names), in_specs=[pl.Blo...  334 us
    pallas_call x2, Pallas kernels, backward_mix(): pl.pallas_call(functools.partial(bwd_kernel, ready, l), grid=(blocks,), i...  73.8 us
    pallas_call x2, Pallas kernels, forward_mix(): pl.pallas_call(functools.partial(fwd_kernel, first, last), grid=(blocks,)...  56.5 us
    pallas_call x1, Pallas kernels, meet(): pl.pallas_call(functools.partial(meet_kernel, n, inner_all), in_specs=[vm...  11.4 us
  transfers between devices with their start and end apart: 4, of which 0 were waited for; matrix products, arithmetic and copies ran while one was open for 1% of the time, Pallas kernels for 82%

profile of v9, /device:TPU:0, one launch (start us, length us, event | category | flops | bytes accessed | tf_op | source)
XLA Modules:
  0.0 506.0 jit_solution(1761340055463787736)
XLA Ops:
  7.3 0.0 all-gather.5.cloned.1.call-start
  7.3 0.7 copy.38
  8.0 0.7 copy.39
  8.7 0.7 fusion.2
  9.4 0.1 copy.40
  9.6 0.9 copy.41
  10.4 0.1 pad.18.clone
  10.5 0.7 maximum_maximum_fusion.refs_2_.refs_5_
  11.3 61.8 %gather_first.1 = (bf16[1024,1536]{1,0:T(8,128)(2,1)}, f32[16,1536]{1,0:T(8,128)}, bf16[2,2,2,192,2688]{4,3,2,1,0:T(8,128)(2,1)}) custom-call(bf16[256,1536]{1,0:T(8,128)(2,1)} %refs_1_.3, bf16[2,192,256]{2,1,0:T(8,128)(2,1)} %refs_4_.4, bf16[2,192,128]{2,1,0:T(8,128)(2,1)} %maximum_maximum_fusion.refs_2_.refs_5_, bf16[2,192,768]{2,1,0:T(8,128)(2,1)} %refs_6_.1, ...), custom_call_target="tpu_custom_call" | custom-call | tf_op jit(solution)/shard_map/gather_first/pallas_call | solution.py:1164
  73.0 0.8 slice.15
  73.9 0.0 all-gather.7.cloned.1.call-start
  73.9 0.7 slice.12
  74.7 0.1 broadcast_in_dim.29
  74.8 0.1 broadcast_in_dim_reshape.4
  74.9 1.0 reshape.56
  75.9 0.7 reshape.64.cst_ref
  76.6 0.6 select_maximum_fusion.tiny_ref
  77.2 0.6 maximum_convert_fusion.vec_ref
  77.8 27.8 %mix_forward.2 = (f32[1024,768]{1,0:T(8,128)}, f32[1024,768]{1,0:T(8,128)}, f32[1024,256]{1,0:T(8,128)}, f32[1024,128]{1,0:T(8,128)}, f32[1024,768]{1,0:T(8,128)...) custom-call(bf16[1024,1536]{1,0:T(8,128)(2,1)} %get-tuple-element.92, ...), custom_call_target="tpu_custom_call" | custom-call | tf_op jit(solution)/shard_map/mix_forward/pallas_call | solution.py:248
  105.6 102.6 %between_forward.1 = (bf16[1024,1536]{1,0:T(8,128)(2,1)}, f32[256,1536]{1,0:T(8,128)}, f32[256,1536]{1,0:T(8,128)}, f32[256,128]{1,0:T(8,128)}, bf16[2,2,2,192,2688]{4,3,2,1,0:T(8,128)(2,1)}) custom-call(bf16[1024,1536]{1,0:T(8,128)(2,1)} %get-tuple-element.95.refs_0_, f32[8,1024]{1,0:T(8,128)} %get-tuple-element.96.refs_1_, bf16[256,1536]{1,0:T(8,128)(2,1)} %refs_1_.3, ...), custom_call_target="tpu_custom_call" | custom-call | tf_op jit(solution)/shard_map/between_forward/pallas_call | solution.py:1164
  208.3 0.3 reduce-scatter.3.cloned.1.call-start
  208.6 28.7 %mix_forward.3 = (f32[1024,768]{1,0:T(8,128)}, f32[1024,768]{1,0:T(8,128)}, f32[1024,256]{1,0:T(8,128)}, f32[1024,128]{1,0:T(8,128)}, f32[1024,768]{1,0:T(8,128)...) custom-call(bf16[1024,1536]{1,0:T(8,128)(2,1)} %get-tuple-element.98, ...), custom_call_target="tpu_custom_call" | custom-call | tf_op jit(solution)/shard_map/mix_forward/pallas_call | solution.py:248
  237.3 0.3 reduce-scatter.5.cloned.1.call-start
  237.6 11.4 %turn_around.1 = (f32[8,1024]{1,0:T(8,128)}, f32[256,128]{1,0:T(8,128)}, f32[4,96,768]{2,1,0:T(8,128)}) custom-call(f32[8,1024]{1,0:T(8,128)} %get-tuple-element.101.own_ref, bf16[4,96,1536]{2,1,0:T(8,128)(2,1)} %bitcast.32, bf16[4,96,768]{2,1,0:T(8,128)(2,1)} %get-tuple-element.103.mixed_ref, bf16[1536,2688]{1,0:T(8,128)(2,1)} %bitcast.25), custom_call_target="tpu_custom_call" | custom-call | tf_op jit(solution)/shard_map/turn_around/pallas_call | solution.py:1229
  249.1 35.9 %mix_backward.2 = (bf16[1024,2688]{1,0:T(8,128)(2,1)}, bf16[1024,1536]{1,0:T(8,128)(2,1)}, f32[8,768]{1,0:T(8,128)}, f32[8,256]{1,0:T(8,128)}, f32[8,128]{1,0:T(8,128)}, /*index=5*/f32[8,1536]{1,0:T(8,128)}) custom-call(f32[4,160,768]{2,1,0:T(8,128)} %get-tuple-element.100.gb_ref, f32[8,1024]{1,0:T(8,128)} %get-tuple-element.104.e_ref, ...), custom_call_target="tpu_custom_call" | custom-call | tf_op jit(solution)/shard_map/mix_backward/pallas_call | solution.py:461
  285.0 100.8 %between_backward.1 = (f32[256,1536]{1,0:T(8,128)}, f32[192,2688]{1,0:T(8,128)}, bf16[1024,1536]{1,0:T(8,128)(2,1)}, f32[8,1024]{1,0:T(8,128)}) custom-call(bf16[1024,1536]{1,0:T(8,128)(2,1)} %get-tuple-element.113.refs_0_, f32[256,1536]{1,0:T(8,128)} %get-tuple-element.114.refs_1_.refs_5_, f32[16,1536]{1,0:T(8,128)} %get-tuple-element.94.gain_ref.refs_3_.refs_2_, ...), custom_call_target="tpu_custom_call" | custom-call | tf_op jit(solution)/shard_map/between_backward/pallas_call | solution.py:1164
  385.8 37.9 %mix_backward.3 = (bf16[1024,2688]{1,0:T(8,128)(2,1)}, bf16[1024,1536]{1,0:T(8,128)(2,1)}, f32[8,768]{1,0:T(8,128)}, f32[8,256]{1,0:T(8,128)}, f32[8,128]{1,0:T(8,128)}, /*index=5*/f32[8,1536]{1,0:T(8,128)}) custom-call(bf16[1024,1536]{1,0:T(8,128)(2,1)} %get-tuple-element.118.gb_ref.refs_6_, f32[8,1024]{1,0:T(8,128)} %get-tuple-element.119.e_ref, ...), custom_call_target="tpu_custom_call" | custom-call | tf_op jit(solution)/shard_map/mix_backward/pallas_call | solution.py:461
  423.7 68.5 %last_backward.1 = (f32[256,1536]{1,0:T(8,128)}, f32[192,2688]{1,0:T(8,128)}, f32[8,2304]{1,0:T(8,128)}, f32[8,1536]{1,0:T(8,128)}) custom-call(bf16[1024,1536]{1,0:T(8,128)(2,1)} %get-tuple-element.128.refs_0_, bf16[256,1536]{1,0:T(8,128)(2,1)} %refs_1_.3, f32[16,1536]{1,0:T(8,128)} %get-tuple-element.94.gain_ref.refs_3_.refs_2_, ...), custom_call_target="tpu_custom_call" | custom-call | tf_op jit(solution)/shard_map/last_backward/pallas_call | solution.py:1164
  492.2 0.0 reduce-scatter.3.cloned.1.call-done.refs_7_
  492.2 0.0 reduce-scatter.5.cloned.1.call-done.refs_8_
  492.2 5.9 %assemble.1 = (f32[2,192]{1,0:T(2,128)}, f32[2,192,768]{2,1,0:T(8,128)}, f32[2,192,768]{2,1,0:T(8,128)}, f32[2,192,256]{2,1,0:T(8,128)}, f32[12,2,192]{2,1,0:T(2...) custom-call(f32[192,2688]{1,0:T(8,128)} %get-tuple-element.141.refs_, ...), custom_call_target="tpu_custom_call" | custom-call | tf_op jit(solution)/shard_map/assemble/pallas_call | solution.py:1341
  498.1 1.1 copy.55
  (31 shorter events, 0.2 us)
Async XLA Ops:
  7.2 65.9 %copy-start = (bf16[256,1536]{1,0:T(8,128)(2,1)S(1)}, bf16[256,1536]{1,0:T(8,128)(2,1)}, u32[]{:S(2)}) copy-start(bf16[256,1536]{1,0:T(8,128)(2,1)} %refs_3_.2) | copy-start | bytes 2359300
  7.2 67.5 %copy-start.3 = (bf16[2,768]{1,0:T(2,128)(2,1)S(1)}, bf16[2,768]{1,0:T(2,128)(2,1)}, u32[]{:S(2)}) copy-start(bf16[2,768]{1,0:T(2,128)(2,1)} %param.25) | copy-start | bytes 9220
  7.2 67.5 %copy-start.4 = (bf16[2,768]{1,0:T(2,128)(2,1)S(1)}, bf16[2,768]{1,0:T(2,128)(2,1)}, u32[]{:S(2)}) copy-start(bf16[2,768]{1,0:T(2,128)(2,1)} %param.31) | copy-start | bytes 9220
  7.2 67.5 %copy-start.5 = (bf16[2,12]{1,0:T(2,128)(2,1)S(1)}, bf16[2,12]{1,0:T(2,128)(2,1)}, u32[]{:S(2)}) copy-start(bf16[2,12]{1,0:T(2,128)(2,1)} %param.30) | copy-start | bytes 148
  7.2 69.3 %copy-start.6 = (bf16[2,12]{1,0:T(2,128)(2,1)S(1)}, bf16[2,12]{1,0:T(2,128)(2,1)}, u32[]{:S(2)}) copy-start(bf16[2,12]{1,0:T(2,128)(2,1)} %param.28) | copy-start | bytes 148
  7.2 69.3 %copy-start.7 = (bf16[2,12]{1,0:T(2,128)(2,1)S(1)}, bf16[2,12]{1,0:T(2,128)(2,1)}, u32[]{:S(2)}) copy-start(bf16[2,12]{1,0:T(2,128)(2,1)} %param.29) | copy-start | bytes 148
  7.2 69.9 %copy-start.2 = (bf16[2,4,768]{2,1,0:T(4,128)(2,1)S(1)}, bf16[2,4,768]{2,1,0:T(4,128)(2,1)}, u32[]{:S(2)}) copy-start(bf16[2,4,768]{2,1,0:T(4,128)(2,1)} %param.24) | copy-start | bytes 36868
  7.3 201.3 %all-gather.5.cloned.1.call-start = ((), (), s32[]{:S(2)}) async-start(), calls=%async_computation.4 | async-start | bytes 2457600 | tf_op jit(solution)/shard_map/all_gather | solution.py:1431
  73.9 163.7 %all-gather.7.cloned.1.call-start = ((), (), s32[]{:S(2)}) async-start(), calls=%async_computation.5 | async-start | bytes 1474560 | tf_op jit(solution)/shard_map/all_gather | solution.py:1431
  208.3 283.9 %reduce-scatter.3.cloned.1.call-start = ((), (), s32[]{:S(2)}) async-start(), calls=%async_computation.2 | async-start | bytes 1966080 | tf_op jit(solution)/shard_map/reduce_scatter | solution.py:1469
  237.3 254.9 %reduce-scatter.5.cloned.1.call-start = ((), (), s32[]{:S(2)}) async-start(), calls=%async_computation.3 | async-start | bytes 1966080 | tf_op jit(solution)/shard_map/reduce_scatter | solution.py:1469
  492.2 5.9 %copy-start.1 = (f32[256,1536]{1,0:T(8,128)S(1)}, f32[256,1536]{1,0:T(8,128)}, u32[]{:S(2)}) copy-start(f32[256,1536]{1,0:T(8,128)} %get-tuple-element.181) | copy-start | bytes 4718596
Sparse Core Ops, SparseCore 0:
  74.0 43.3 all-gather.4
  208.4 29.1 all-gather.6
  239.9 34.3 reduce-scatter.2
  385.9 34.1 reduce-scatter.4
